TPU v7x, 32 devices: a whole 2x2x4 slice. The times are simulated.
32 devices in a mesh: groups: 2 (over y), date: 4 (over z), rng: 2 (over x), az: 2 (over core).
Axes of the slice: x: 2, y: 2, z: 4, core: 2. Of those that a mesh axis runs over, the one named last changes fastest.
Arguments:
- slc: bfloat16 [2, 8, 64, 5120], P(None, ('groups', 'date'), 'az', 'rng'), parts along dimension 1, may hold values from -24 to 24
- offsets: int32 [8, 2], P(('groups', 'date')), parts along dimension 0, may hold values from -24 to 24, as said below
- kernel_index: int32 [8, 2], P(('groups', 'date')), parts along dimension 0, may hold values from 0 to 15
- range_shift: float32 [8], P('groups'), parts along dimension 0, may hold values from -0.15 to 0.15
Outputs:
- ifg: float32 [2, 8, 8, 16, 256], P(None, ('groups', 'date'), None, 'az', 'rng'), parts along dimension 1
There are 2 independent parts, one for each index of `groups`. A program takes and returns all parts, laid end to end along the dimension named above; each array names one. Nothing has to cross between parts.
Inputs may be any that keep to these rules, and one draw needn't show every extreme that they name: `offsets`: column 0 is the azimuth offset, within -8 to 8; column 1 is the range offset. Both ends of both ranges are taken by some date.
All inputs are finite; a program needn't handle non-finite values.
Results may differ from a plain program's by a relative error of at most 0.0039.
Values may be sent and summed in bfloat16 or wider, within the bound.
No kernel may reach another device: no remote copies, remote signals or barrier semaphores. Data moves between devices by JAX's collectives and lax.ppermute only.
A program may use at most 64 MiB of HBM per device.

v0:
```python
import functools

import jax
import jax.numpy as jnp
import numpy as np
from jax import lax
from jax.experimental import pallas as pl
from jax.experimental.pallas import tpu as pltpu
from jax.sharding import PartitionSpec as P

LAGS = 8
KERNELS = 16
TAPS = 8
FILTER_HALF = 8
FILTER_TAPS = 2 * FILTER_HALF + 1
LOOK_AZ = 4
LOOK_RG = 20
LANES = 128
META = 3
UNROLLED_PAIRS = 12


def up(value, unit):
    return -(-value // unit) * unit


def kernel_table():
    position = np.arange(TAPS) - 3.0 - np.arange(KERNELS)[:, None] / KERNELS
    shaped = np.sinc(position) * (0.5 + 0.5 * np.cos(np.pi * position / 5.0))
    table = np.zeros((KERNELS, LANES), np.float32)
    table[:, :TAPS] = shaped / shaped.sum(1, keepdims=True)
    return table


def lowpass_row(width):
    t = np.arange(FILTER_TAPS) - FILTER_HALF
    row = np.zeros((1, width), np.float32)
    row[0, :FILTER_TAPS] = 0.4 * np.sinc(0.4 * t) * (0.54 + 0.46 * np.cos(np.pi * t / (FILTER_HALF + 1)))
    return row


def halves(value):
    high = value.astype(jnp.bfloat16)
    return high, (value - high.astype(jnp.float32)).astype(jnp.bfloat16)


def dot(a, b):
    return jnp.dot(a, b, preferred_element_type=jnp.float32)


def dot_nt(a, b):
    return lax.dot_general(a, b, (((1,), (1,)), ((), ())), preferred_element_type=jnp.float32)


def pack_kernel(chunk, place_ref, offsets_ref, index_ref, slc_ref, before_ref, after_ref, out_ref, wide_ref):
    columns = slc_ref.shape[1]
    wide = out_ref.shape[2]
    first = place_ref[0] == 0
    last = place_ref[0] == place_ref[1] - 1
    zero = jnp.zeros_like(before_ref[...])
    wide_ref[:, :LANES] = jnp.where(first, zero, before_ref[...])
    wide_ref[:, LANES : LANES + columns] = slc_ref[...]
    wide_ref[:, LANES + columns :] = jnp.where(last, zero, after_ref[...])
    lane = lax.broadcasted_iota(jnp.int32, (slc_ref.shape[0], wide), 1)
    numbers = [offsets_ref[0, 0], index_ref[0, 0], index_ref[0, 1]]
    for j in range(out_ref.shape[0]):
        start = LANES + chunk * j - FILTER_HALF - 3 + offsets_ref[0, 1]
        tile = lax.shift_right_logical(start, 7)
        within = lax.bitwise_and(start, LANES - 1)
        window = wide_ref[:, pl.ds(pl.multiple_of(tile * LANES, LANES), wide + LANES)].astype(jnp.float32)
        moved = pltpu.roll(window, wide + LANES - within, 1)[:, :wide]
        for slot, number in enumerate(numbers):
            moved = jnp.where(lane == wide - META + slot, number.astype(jnp.float32), moved)
        out_ref[j] = moved.astype(jnp.bfloat16)


def picked_taps(table, index):
    row = lax.broadcasted_iota(jnp.int32, table.shape, 0).astype(jnp.float32)
    return jnp.sum(jnp.where(row == index, table, 0.0), axis=0, keepdims=True)


def banded(taps, distance):
    out = jnp.zeros(distance.shape, jnp.float32)
    for q in range(TAPS):
        out = jnp.where(distance == q, taps[:, q : q + 1], out)
    return out


def pairs_kernel(chunk, pairs, *refs):
    if isinstance(pairs, int):
        table_of_pairs, refs = refs[0], refs[1:]
    shift_ref, table_ref, lowpass_ref, recv_ref, out_ref, resampled_ref, weight_ref, product_ref = refs
    sources, rows, wide = recv_ref.shape
    dates = shift_ref.shape[0]
    az_count = sources // dates
    own_lines = rows // 2
    lines = own_lines * az_count
    groups = lines // LOOK_AZ
    looks = chunk // LOOK_RG
    table = table_ref[...]
    held = resampled_ref.shape[2]

    out_row = lax.broadcasted_iota(jnp.int32, (lines, lines), 0)
    in_row = lax.broadcasted_iota(jnp.int32, (lines, lines), 1)
    line = LOOK_AZ * (out_row % groups) + out_row // groups
    line_distance = (in_row - line + 3).astype(jnp.float32)
    span = min(2 * LANES, wide)
    column_distance = (
        lax.broadcasted_iota(jnp.int32, (span, LANES), 0) - lax.broadcasted_iota(jnp.int32, (span, LANES), 1)
    ).astype(jnp.float32)
    for date in range(dates):
        numbers = recv_ref[date * az_count, 0:16, wide - LANES :].astype(jnp.float32)[0:1, LANES - META :]
        line_offset, line_index, column_index = (numbers[:, s : s + 1] for s in range(META))
        line_taps = banded(picked_taps(table, line_index), line_distance - line_offset)
        line_taps = jnp.concatenate(halves(line_taps), axis=0)
        column_high, column_low = halves(banded(picked_taps(table, column_index), column_distance))
        moved = []
        for plane in range(2):
            rows_of = slice(plane * own_lines, (plane + 1) * own_lines)
            source = jnp.concatenate([recv_ref[date * az_count + a, rows_of, :] for a in range(az_count)], axis=0)
            both = dot(line_taps, source)
            moved.append(both[:lines] + both[lines:])
        moved_high, moved_low = halves(jnp.concatenate(moved, axis=0))
        for begin in range(0, held, LANES):
            end = min(begin + span, wide)
            taken = end - begin
            total = dot(moved_high[:, begin:end], column_high[:taken])
            total += dot(moved_low[:, begin:end], column_high[:taken])
            total += dot(moved_high[:, begin:end], column_low[:taken])
            resampled_ref[date, :, begin : begin + LANES] = total.astype(jnp.bfloat16)

    window = lowpass_ref[...]
    spacing = lax.broadcasted_iota(jnp.int32, window.shape, 1).astype(jnp.float32) - FILTER_HALF
    span = min(2 * LANES, held)

    def one_pair(place, own, other):
        gap = shift_ref[own] - shift_ref[other]
        angle = jnp.where(jnp.abs(spacing) <= FILTER_HALF, jnp.pi * gap * spacing, 0.0)
        for part, taps in enumerate((window * jnp.cos(angle), window * jnp.sin(angle))):
            spread = jnp.broadcast_to(taps, (LANES, 2 * LANES))
            spread = pltpu.roll(spread, 0, 1, stride=1, stride_axis=0)
            high, low = halves(spread)
            weight_ref[0, part * LANES : (part + 1) * LANES, :] = high
            weight_ref[1, part * LANES : (part + 1) * LANES, :] = low
        both = jnp.concatenate([resampled_ref[own], resampled_ref[other]], axis=0)
        for begin in range(0, up(chunk, LANES), LANES):
            end = min(begin + span, held)
            taken = end - begin
            total = dot_nt(both[:, begin:end], weight_ref[0, :, :taken])
            total += dot_nt(both[:, begin:end], weight_ref[1, :, :taken])
            cos, sin = total[:, :LANES], total[:, LANES:]
            re, im = slice(0, lines), slice(lines, 2 * lines)
            master_re = cos[re] + sin[im]
            master_im = cos[im] - sin[re]
            re, im = slice(2 * lines, 3 * lines), slice(3 * lines, 4 * lines)
            partner_re = cos[re] - sin[im]
            partner_im = cos[im] + sin[re]
            for part, product in enumerate(
                (
                    master_re * partner_re + master_im * partner_im,
                    master_im * partner_re - master_re * partner_im,
                )
            ):
                summed = sum(product[k * groups : (k + 1) * groups] for k in range(LOOK_AZ))
                product_ref[place, part, :, begin : begin + LANES] = summed

    if isinstance(pairs, int):
        count = pairs

        def step(place, carry):
            one_pair(place, table_of_pairs[place, 0], table_of_pairs[place, 1])
            return carry

        lax.fori_loop(0, count, step, 0)
    else:
        count = len(pairs)
        for place, (own, other) in enumerate(pairs):
            one_pair(place, own, other)

    out_width = out_ref.shape[2]
    column = lax.broadcasted_iota(jnp.int32, (product_ref.shape[3], out_width), 0)
    lane = lax.broadcasted_iota(jnp.int32, (product_ref.shape[3], out_width), 1)
    collect = jnp.where(column // LOOK_RG == lane % looks, 1.0, 0.0).astype(jnp.bfloat16)
    high, low = halves(product_ref[...].reshape(count * 2 * groups, product_ref.shape[3]))
    total = (dot(high, collect) + dot(low, collect)) * (1.0 / (LOOK_AZ * LOOK_RG))
    total = total.reshape(count, 2, groups, out_width)
    own_lane = lax.broadcasted_iota(jnp.int32, (groups, out_width), 1) // looks
    place = 0
    for own in range(dates):
        value = jnp.zeros((groups, out_width), jnp.float32)
        for lag in range(min(LAGS, dates - 1 - own)):
            for part in range(2):
                value = jnp.where(own_lane == lag * 2 + part, total[place, part], value)
            place += 1
        out_ref[own * az_count : (own + 1) * az_count] = value.reshape(az_count, groups // az_count, out_width)


def unpack_kernel(used_lags, looks, recv_ref, out_ref):
    sources, groups, width = recv_ref.shape
    columns = out_ref.shape[-1]
    lane = lax.broadcasted_iota(jnp.int32, (groups, columns), 1) // looks
    out_ref[...] = jnp.zeros_like(out_ref)
    for lag in range(used_lags):
        for part in range(2):
            value = jnp.zeros((groups, columns), jnp.float32)
            for source in range(sources):
                block = recv_ref[source]
                if width != columns:
                    block = block[:, :columns]
                shift = looks * (source - lag * 2 - part) % columns
                if shift:
                    block = pltpu.roll(block, shift, 1)
                value = jnp.where(lane == source, block, value)
            out_ref[part, lag] = value


def chunked_body(slc, offsets, kernel_index, range_shift):
    axes = ("date", "az")
    date_count, az_count, rng_count = (lax.axis_size(a) for a in ("date", "az", "rng"))
    peers = date_count * az_count
    lines, columns = slc.shape[2], slc.shape[3]
    dates = range_shift.shape[0]
    chunk = columns // peers
    looks = chunk // LOOK_RG
    groups = lines * az_count // LOOK_AZ
    wide = up(chunk + 2 * FILTER_HALF + TAPS - 1 + META, LANES)
    held = up(chunk + 2 * FILTER_HALF, LANES)
    used_lags = min(LAGS, dates - 1)
    out_width = up(used_lags * 2 * looks, LANES)
    vmem = pl.BlockSpec(memory_space=pltpu.VMEM)
    smem = pl.BlockSpec(memory_space=pltpu.SMEM)
    limit = pltpu.CompilerParams(vmem_limit_bytes=32 * 1024 * 1024)

    cells = slc.reshape(2 * lines, columns)
    place = lax.axis_index("rng")
    if rng_count == 2:
        edge = jnp.where(place == 0, cells[:, columns - LANES :], cells[:, :LANES])
        before = after = lax.ppermute(edge, "rng", [(0, 1), (1, 0)])
    else:
        forth = [(i, i + 1) for i in range(rng_count - 1)]
        before = lax.ppermute(cells[:, columns - LANES :], "rng", forth)
        after = lax.ppermute(cells[:, :LANES], "rng", [(b, a) for a, b in forth])

    packed = pl.pallas_call(
        functools.partial(pack_kernel, chunk),
        out_shape=jax.ShapeDtypeStruct((peers, 2 * lines, wide), jnp.bfloat16),
        in_specs=[smem] * 3 + [vmem] * 3,
        out_specs=vmem,
        scratch_shapes=[pltpu.VMEM((2 * lines, columns + 2 * LANES), jnp.bfloat16)],
        compiler_params=limit,
    )(jnp.stack([place, rng_count]).astype(jnp.int32), offsets, kernel_index, cells, before, after)
    arrived = lax.all_to_all(packed, axes, 0, 0, tiled=True)

    pairs = [(own, own + lag) for own in range(dates) for lag in range(1, LAGS + 1) if own + lag < dates]
    count = len(pairs)
    first = [jnp.asarray(np.array(pairs, np.int32))] if count > UNROLLED_PAIRS else []
    looked = pl.pallas_call(
        functools.partial(pairs_kernel, chunk, count if first else pairs),
        out_shape=jax.ShapeDtypeStruct((peers, groups // az_count, out_width), jnp.float32),
        in_specs=[smem] * len(first) + [smem] + [vmem] * 3,
        out_specs=vmem,
        scratch_shapes=[
            pltpu.VMEM((dates, 4 * (groups * LOOK_AZ) // 2, held), jnp.bfloat16),
            pltpu.VMEM((2, 2 * LANES, 2 * LANES), jnp.bfloat16),
            pltpu.VMEM((count, 2, groups, up(chunk, LANES)), jnp.float32),
        ],
        compiler_params=limit,
    )(*first, range_shift, jnp.asarray(kernel_table()), jnp.asarray(lowpass_row(2 * LANES)), arrived)
    returned = lax.all_to_all(looked, axes, 0, 0, tiled=True)

    out = pl.pallas_call(
        functools.partial(unpack_kernel, used_lags, looks),
        out_shape=jax.ShapeDtypeStruct((2, LAGS, groups // az_count, looks * peers), jnp.float32),
        in_specs=[vmem],
        out_specs=vmem,
        compiler_params=limit,
    )(returned)
    return out[:, None]


HALO_LINES = 16
FOLD = 16
TAIL = 2 * FILTER_HALF


def reach(step, dates):
    return {dates - 1: dates // 2, dates // 2: dates - 1}.get(step, step)


def sinc(value):
    angle = jnp.pi * value
    return jnp.where(angle == 0.0, 1.0, jnp.sin(angle) / jnp.where(angle == 0.0, 1.0, angle))


def tap_row(index):
    lane = lax.broadcasted_iota(jnp.int32, (1, LANES), 1)
    position = lane.astype(jnp.float32) - 3.0 - index.astype(jnp.float32) / KERNELS
    shaped = sinc(position) * (0.5 + 0.5 * jnp.cos(jnp.pi * position / 5.0))
    shaped = jnp.where(lane < TAPS, shaped, 0.0)
    return shaped / jnp.sum(shaped, axis=1, keepdims=True)


def row_line(row, az):
    quarter = HALO_LINES // LOOK_AZ
    within = row % HALO_LINES
    return HALO_LINES * ((row // HALO_LINES) ^ az) + LOOK_AZ * (within % quarter) + within // quarter


def prepare_kernel(offsets_hbm, index_hbm, slc_ref, side_ref, corner_ref, lines_ref, line_ref, column_ref, held_ref, offsets_ref, index_ref, semaphores):
    lines, columns = slc_ref.shape[1:]
    az = lax.axis_index("az")
    row = pl.multiple_of((1 - az) * (lines - HALO_LINES), HALO_LINES)
    edge = pl.multiple_of((1 - lax.axis_index("rng")) * (columns - LANES), LANES)
    nearest, outermost = pl.ds(row, HALO_LINES), pl.ds(edge, LANES)
    moves = [
        (offsets_hbm, offsets_ref),
        (index_hbm, index_ref),
        (slc_ref.at[:, :, outermost], side_ref),
        (slc_ref.at[:, nearest, outermost], corner_ref),
        (slc_ref.at[:, nearest, :], lines_ref),
        (slc_ref, held_ref.at[:, :, pl.ds(LANES, columns)]),
    ]
    copies = [pltpu.make_async_copy(a, b, semaphores.at[i]) for i, (a, b) in enumerate(moves)]
    for copy in copies:
        copy.start()
    held_ref[:, :, :LANES] = jnp.zeros((2, lines, LANES), held_ref.dtype)
    held_ref[:, :, LANES + columns :] = jnp.zeros((2, lines, 2 * LANES), held_ref.dtype)
    copies[0].wait()
    copies[1].wait()
    for half in range(2):
        shape = (HALO_LINES, lines + HALO_LINES)
        line = row_line(lax.broadcasted_iota(jnp.int32, shape, 0) + half * HALO_LINES, az)
        place = lax.broadcasted_iota(jnp.int32, shape, 1)
        source = jnp.where(place < lines, place, place + jnp.where(az == 0, 0, -lines - HALO_LINES))
        taps = banded(tap_row(index_ref[0, 0]), source - line - offsets_ref[0, 0] + 3)
        line_ref[half] = jnp.concatenate(halves(taps), axis=0)
    shape = (3 * LANES, LANES)
    distance = lax.broadcasted_iota(jnp.int32, shape, 0) - lax.broadcasted_iota(jnp.int32, shape, 1)
    distance = distance - (LANES - FILTER_HALF - 3) - offsets_ref[0, 1]
    taps = banded(tap_row(index_ref[0, 1]), distance)
    column_ref[...] = jnp.concatenate(halves(taps), axis=1)
    for copy in copies[2:]:
        copy.wait()


def along_range(moved, column_ref, tiles):
    high, low = halves(moved)
    starts = range(0, tiles * LANES, LANES)
    high = jnp.concatenate([high[:, s : s + 3 * LANES] for s in starts], axis=0)
    low = jnp.concatenate([low[:, s : s + 3 * LANES] for s in starts], axis=0)
    total = dot(high, column_ref[...])
    return total[:, :LANES] + total[:, LANES:] + dot(low, column_ref[:, :LANES])


def early_kernel(tiles, held_ref, line_ref, column_ref, out_ref):
    lines = held_ref.shape[1]
    early = out_ref.shape[0] // (2 * HALO_LINES)
    dates = lax.axis_size("date")
    chunk = lax.axis_index("date") ^ reach(dates - 1, dates)
    begin = pl.multiple_of((chunk * tiles + lax.axis_index("rng")) * LANES, LANES)
    moved = []
    for plane in range(2):
        both = dot(line_ref[0, :, :lines], held_ref[plane, :, pl.ds(begin, (early + 2) * LANES)])
        moved.append(both[:HALO_LINES] + both[HALO_LINES:])
    moved = jnp.concatenate(moved, axis=0)
    out_ref[...] = along_range(moved, column_ref, early).astype(jnp.bfloat16)


def resample_kernel(side_ref, corner_ref, lines_ref, held_ref, line_ref, column_ref, *outs):
    outs, tiles_ref, tails_ref = outs[:-2], outs[-2], outs[-1]
    lines, width = held_ref.shape[1:]
    width -= LANES
    block = lax.axis_index("rng")
    taps = jnp.concatenate([line_ref[0], line_ref[1]], axis=0)
    moved = [[], []]
    for plane in range(2):
        own = jnp.concatenate([side_ref[plane], held_ref[plane, :, LANES : width - LANES], side_ref[plane]], axis=1)
        halo = jnp.concatenate([corner_ref[plane], lines_ref[plane], corner_ref[plane]], axis=1)
        both = dot(taps, jnp.concatenate([own, halo], axis=0))
        for half in range(2):
            at = 2 * half * HALO_LINES
            moved[half].append(both[at : at + HALO_LINES] + both[at + HALO_LINES : at + 2 * HALO_LINES])
    moved = jnp.concatenate(moved[0] + moved[1], axis=0)
    left = jnp.where(block > 0, moved[:, :LANES], 0.0)
    right = jnp.where(block == 0, moved[:, width - LANES :], 0.0)
    moved = jnp.concatenate([left, moved[:, LANES : width - LANES], right, jnp.zeros_like(right)], axis=1)
    total = along_range(moved, column_ref, width // LANES - 1)
    rows = 2 * lines
    tiles_ref[...] = total.astype(jnp.bfloat16)
    chunk_rows = outs[0].shape[0] - FOLD
    lane = lax.broadcasted_iota(jnp.int32, (FOLD, LANES), 1) // TAIL
    for chunk in range(len(outs)):
        begin = (chunk + 1) * chunk_rows
        folded = total[begin : begin + FOLD]
        for part in range(1, rows // FOLD):
            value = pltpu.roll(total[begin + part * FOLD : begin + (part + 1) * FOLD], part * TAIL, 1)
            folded = jnp.where(lane == part, value, folded)
        tails_ref[chunk] = folded.astype(jnp.bfloat16)
    date = lax.axis_index("date")
    for step, out_ref in enumerate(outs[:-1]):
        chunk = date ^ reach(step, len(outs))
        out_ref[:chunk_rows] = tiles_ref[pl.ds(pl.multiple_of(chunk * chunk_rows, FOLD), chunk_rows), :]
        out_ref[chunk_rows:] = tails_ref[chunk]
    out_ref = outs[-1]
    chunk = date ^ reach(len(outs) - 1, len(outs))
    early = chunk_rows // rows - 1
    for tile in range(early):
        begin = pl.multiple_of(chunk * chunk_rows + (tile + block) * rows + lines, FOLD)
        out_ref[tile * lines : (tile + 1) * lines] = tiles_ref[pl.ds(begin, lines), :]
    begin = pl.multiple_of(chunk * chunk_rows + (1 - block) * early * rows, FOLD)
    out_ref[early * lines : early * lines + rows] = tiles_ref[pl.ds(begin, rows), :]
    out_ref[early * lines + rows :] = tails_ref[chunk]


def filter_kernel(pairs, shift_hbm, early_ref, out_ref, spread_ref, shift_ref, semaphore):
    copy = pltpu.make_async_copy(shift_hbm, shift_ref, semaphore)
    copy.start()
    lines = 2 * HALO_LINES
    spread_ref[...] = jnp.zeros_like(spread_ref)
    for tile in range(early_ref.shape[0] // lines):
        begin = pl.multiple_of((tile + lax.axis_index("rng")) * 2 * lines, FOLD)
        spread_ref[pl.ds(begin, lines), :] = early_ref[tile * lines : (tile + 1) * lines]
    date = lax.axis_index("date")
    spacing = lax.broadcasted_iota(jnp.int32, (1, 2 * LANES), 1).astype(jnp.float32) - FILTER_HALF
    window = 0.4 * sinc(0.4 * spacing) * (0.54 + 0.46 * jnp.cos(jnp.pi * spacing / (FILTER_HALF + 1)))
    window = jnp.where(jnp.abs(spacing) <= FILTER_HALF, window, 0.0)
    copy.wait()
    for place, (first, second) in enumerate(pairs):
        dates = shift_ref.shape[0]
        gap = shift_ref[date ^ reach(first, dates)] - shift_ref[date ^ reach(second, dates)]
        angle = jnp.where(jnp.abs(spacing) <= FILTER_HALF, jnp.pi * gap * spacing, 0.0)
        for part, taps in enumerate((window * jnp.cos(angle), window * jnp.sin(angle))):
            spread = jnp.broadcast_to(taps, (LANES, 2 * LANES))
            spread = pltpu.roll(spread, 0, 1, stride=1, stride_axis=0)
            high, low = halves(spread)
            out_ref[place, 0, part * LANES : (part + 1) * LANES, :] = high
            out_ref[place, 1, part * LANES : (part + 1) * LANES, :] = low


def looks_kernel(pairs, dates, weight_ref, *refs):
    early_ref, chunks, outs = refs[0], list(refs[1 : dates + 1][::-1]), refs[dates + 1 : 2 * dates + 1]
    whole_ref, window_ref, product_ref = refs[-3:]
    groups, lines = outs[0].shape[0], outs[0].shape[0] * LOOK_AZ
    rows = 2 * lines
    blocks = (chunks[0].shape[0] - FOLD) // rows
    looks = blocks * LANES // LOOK_RG
    date = lax.axis_index("date")
    block = lax.axis_index("rng")
    early = blocks - 1
    whole_ref[: blocks * rows] = early_ref[...]
    for tile in range(early):
        begin = pl.multiple_of((tile + block) * rows, FOLD)
        whole_ref[pl.ds(begin + lines, lines), :] = chunks[-1][tile * lines : (tile + 1) * lines]
    begin = pl.multiple_of((1 - block) * early * rows, FOLD)
    whole_ref[pl.ds(begin, rows), :] = chunks[-1][early * lines : early * lines + rows]
    whole_ref[blocks * rows :] = chunks[-1][early * lines + rows :]
    chunks[-1] = whole_ref
    az = lax.axis_index("az")
    upper = lax.broadcasted_iota(jnp.int32, (groups, LANES), 0) // (groups // 2) == az
    for step, chunk_ref in enumerate(chunks):
        window_ref[step, :, :LANES] = chunk_ref[: blocks * rows]
        window_ref[step, : (blocks - 1) * rows, LANES:] = chunk_ref[rows : blocks * rows]
        folded = chunk_ref[blocks * rows :].astype(jnp.float32)
        for part in range(rows // FOLD):
            value = pltpu.roll(folded, LANES - part * TAIL, 1) if part else folded
            at = pl.ds((blocks - 1) * rows + part * FOLD, FOLD)
            window_ref[step, at, LANES:] = value.astype(jnp.bfloat16)
    for place, (first, second) in enumerate(pairs):
        def filtered(step):
            total = dot_nt(window_ref[step], weight_ref[place, 0]) + dot_nt(window_ref[step], weight_ref[place, 1])
            total = total.reshape(blocks, 2, 2, HALO_LINES, 2 * LANES)
            re, im = total[:, :, 0], total[:, :, 1]
            return re[..., :LANES], im[..., :LANES], re[..., LANES:], im[..., LANES:]

        cos_re, cos_im, sin_re, sin_im = filtered(first)
        master_re, master_im = cos_re + sin_im, cos_im - sin_re
        cos_re, cos_im, sin_re, sin_im = filtered(second)
        partner_re, partner_im = cos_re - sin_im, cos_im + sin_re
        for part, product in enumerate(
            (
                master_re * partner_re + master_im * partner_im,
                master_im * partner_re - master_re * partner_im,
            )
        ):
            summed = product[:, :, :groups] + product[:, :, groups:]
            at = pl.ds((place * 2 + part) * groups, groups)
            for k in range(blocks):
                both = [summed[k, half] + pltpu.roll(summed[k, half], groups // 2, 0) for half in range(2)]
                product_ref[at, k * LANES : (k + 1) * LANES] = jnp.where(upper, both[0], both[1])

    out_width = outs[0].shape[1]
    column = lax.broadcasted_iota(jnp.int32, (product_ref.shape[1], out_width), 0)
    lane = lax.broadcasted_iota(jnp.int32, (product_ref.shape[1], out_width), 1)
    collect = jnp.where(column // LOOK_RG == lane % looks, 1.0, 0.0).astype(jnp.bfloat16)
    high, low = halves(product_ref[...])
    total = (dot(high, collect) + dot(low, collect)) * (1.0 / (LOOK_AZ * LOOK_RG))
    total = total.reshape(len(pairs), 2, groups, out_width)
    own_lane = lax.broadcasted_iota(jnp.int32, (groups, out_width), 1) // looks
    for step, out_ref in enumerate(outs):
        value = jnp.zeros((groups, out_width), jnp.float32)
        for place, pair in enumerate(pairs):
            if step in pair:
                other = pair[1] if pair[0] == step else pair[0]
                lag = (date ^ reach(other, dates)) - (date ^ reach(step, dates))
                for part in range(2):
                    signed = -total[place, part] if part == 1 and pair[1] == step else total[place, part]
                    value = jnp.where(own_lane == (lag - 1) * 2 + part, signed, value)
        out_ref[...] = value


def place_kernel(used_lags, looks, *refs):
    out_ref = refs[-1]
    groups, columns = out_ref.shape[2:]
    date = lax.axis_index("date")
    lane = lax.broadcasted_iota(jnp.int32, (groups, LANES), 1) // looks
    out_ref[...] = jnp.zeros_like(out_ref)
    each = LANES // looks
    for step, recv_ref in enumerate(refs[:-1][::-1]):
        chunk = date ^ reach(step, len(refs) - 1)
        for lag in range(used_lags):
            for part in range(2):
                tile, group = divmod(lag * 2 + part, each)
                block = recv_ref[:, tile * LANES : (tile + 1) * LANES]
                block = pltpu.roll(block, lax.bitwise_and(looks * (chunk - group), LANES - 1), 1)
                out_ref[part, lag] = jnp.where(lane == chunk, block, out_ref[part, lag])


def tiled_body(slc, offsets, kernel_index, range_shift):
    dates = lax.axis_size("date")
    lines, columns = slc.shape[2], slc.shape[3]
    chunk = columns // dates
    looks = chunk // LOOK_RG
    groups = lines // LOOK_AZ
    out_width = up(min(LAGS, dates - 1) * 2 * looks, LANES)
    vmem = pl.BlockSpec(memory_space=pltpu.VMEM)
    hbm = pl.BlockSpec(memory_space=pltpu.HBM)
    limit = pltpu.CompilerParams(vmem_limit_bytes=32 * 1024 * 1024)
    bf16 = jnp.bfloat16
    cells, offsets, kernel_index, range_shift = (
        pltpu.with_memory_space_constraint(value, pltpu.HBM)
        for value in (slc.reshape(2, lines, columns), offsets, kernel_index, range_shift)
    )
    tiles = chunk // LANES
    chunk_rows = tiles * 2 * lines

    side, corner, halo_lines, line_taps, column_taps, held = pl.pallas_call(
        prepare_kernel,
        out_shape=[
            jax.ShapeDtypeStruct((2, lines, LANES), bf16),
            jax.ShapeDtypeStruct((2, HALO_LINES, LANES), bf16),
            jax.ShapeDtypeStruct((2, HALO_LINES, columns), bf16),
            jax.ShapeDtypeStruct((2, 2 * HALO_LINES, lines + HALO_LINES), bf16),
            jax.ShapeDtypeStruct((3 * LANES, 2 * LANES), bf16),
            jax.ShapeDtypeStruct((2, lines, columns + 3 * LANES), bf16),
        ],
        in_specs=[hbm] * 3,
        out_specs=[vmem] * 6,
        scratch_shapes=[
            pltpu.SMEM(offsets.shape, jnp.int32),
            pltpu.SMEM(kernel_index.shape, jnp.int32),
            pltpu.SemaphoreType.DMA((6,)),
        ],
        compiler_params=limit,
    )(offsets, kernel_index, cells)
    swap = [(0, 1), (1, 0)]
    side = lax.ppermute(side, "rng", swap)
    corner = lax.ppermute(corner, ("rng", "az"), [(0, 3), (1, 2), (2, 1), (3, 0)])
    halo_lines = lax.ppermute(halo_lines, "az", swap)

    early_rows = (tiles - 1) * lines
    early = pl.pallas_call(
        functools.partial(early_kernel, tiles),
        out_shape=jax.ShapeDtypeStruct((early_rows, LANES), bf16),
        in_specs=[vmem] * 3,
        out_specs=vmem,
        compiler_params=limit,
    )(held, line_taps, column_taps)
    early = lax.ppermute(early, "date", [(i, i ^ reach(dates - 1, dates)) for i in range(dates)])
    out_rows = [chunk_rows + FOLD] * (dates - 1) + [chunk_rows + FOLD - early_rows]
    sent = pl.pallas_call(
        resample_kernel,
        out_shape=[jax.ShapeDtypeStruct((rows, LANES), bf16) for rows in out_rows],
        in_specs=[vmem] * 6,
        out_specs=[vmem] * dates,
        scratch_shapes=[
            pltpu.VMEM(((columns // LANES + 1) * 2 * lines, LANES), bf16),
            pltpu.VMEM((dates, FOLD, LANES), bf16),
        ],
        compiler_params=limit,
    )(side, corner, halo_lines, held, line_taps, column_taps)

    def exchanged(values, order):
        arrived = {0: values[0]}
        for step in order:
            arrived[step] = lax.ppermute(values[step], "date", [(i, i ^ reach(step, dates)) for i in range(dates)])
        return [arrived[step] for step in reversed(range(dates))]

    steps = range(dates - 1, 0, -1)

    chunks = exchanged(sent, steps)
    pairs = [(first, second) for first in range(dates) for second in range(first + 1, dates)]
    weights, early = pl.pallas_call(
        functools.partial(filter_kernel, pairs),
        out_shape=[
            jax.ShapeDtypeStruct((len(pairs), 2, 2 * LANES, 2 * LANES), bf16),
            jax.ShapeDtypeStruct((chunk_rows, LANES), bf16),
        ],
        in_specs=[hbm, vmem],
        out_specs=[vmem] * 2,
        scratch_shapes=[pltpu.SMEM(range_shift.shape, jnp.float32), pltpu.SemaphoreType.DMA],
        compiler_params=limit,
        cost_estimate=pl.CostEstimate(flops=600_000_000, bytes_accessed=0, transcendentals=0),
    )(range_shift, early)
    looked = pl.pallas_call(
        functools.partial(looks_kernel, pairs, dates),
        out_shape=[jax.ShapeDtypeStruct((groups, out_width), jnp.float32)] * dates,
        in_specs=[vmem] * (2 + dates),
        out_specs=[vmem] * dates,
        scratch_shapes=[
            pltpu.VMEM((chunk_rows + FOLD, LANES), bf16),
            pltpu.VMEM((dates, chunk_rows, 2 * LANES), bf16),
            pltpu.VMEM((len(pairs) * 2 * groups, chunk), jnp.float32),
        ],
        compiler_params=limit,
    )(weights, early, *chunks)
    out = pl.pallas_call(
        functools.partial(place_kernel, min(LAGS, dates - 1), looks),
        out_shape=jax.ShapeDtypeStruct((2, LAGS, groups, looks * dates), jnp.float32),
        in_specs=[vmem] * dates,
        out_specs=vmem,
        compiler_params=limit,
    )(*exchanged(looked, steps))
    return out[:, None]


def body(slc, offsets, kernel_index, range_shift):
    dates, az_count = (lax.axis_size(a) for a in ("date", "az"))
    lines, columns = slc.shape[2], slc.shape[3]
    whole_tiles = columns % (dates * LANES) == 0 and columns % (dates * LOOK_RG) == 0
    one_row = columns // LOOK_RG == LANES and range_shift.shape[0] == dates
    few = dates & (dates - 1) == 0 and dates - 1 <= LAGS
    folds = lines == 2 * HALO_LINES and lax.axis_size("rng") == 2 and dates >= 4 and 2 * lines // FOLD * TAIL <= LANES
    if az_count == 2 and whole_tiles and one_row and few and folds:
        return tiled_body(slc, offsets, kernel_index, range_shift)
    return chunked_body(slc, offsets, kernel_index, range_shift)


def solution(mesh):
    return jax.shard_map(
        body,
        mesh=mesh,
        in_specs=(
            P(None, ("groups", "date"), "az", "rng"),
            P(("groups", "date"), None),
            P(("groups", "date"), None),
            P("groups"),
        ),
        out_specs=P(None, ("groups", "date"), None, "az", "rng"),
        check_vma=False,
    )
```

profile of v0, /device:TPU:0, one launch (start us, length us, event | category | flops | bytes accessed | tf_op | source)
XLA Modules:
  0.0 28.6 jit_solution(2748835139631911430)
XLA Ops:
  0.0 1.2 %shard_map.46 = (bf16[2,32,128]{2,1,0:T(8,128)(2,1)S(1)}, bf16[2,16,128]{2,1,0:T(8,128)(2,1)S(1)}, bf16[2,16,2560]{2,1,0:T(8,128)(2,1)S(1)}, bf16[2,32,48]{2,1,0...) custom-call(s32[1,2]{1,0:T(1,128)} %offsets_hbm.1, s32[1,2]{1,0:T(1,128)} %index_hbm.1, ...), custom_call_target="tpu_custom_call" | custom-call | tf_op jit(solution)/shard_map/pallas_call | solution.py:546
  1.2 0.5 %collective-permute-start.3 = (bf16[2,16,2560]{2,1,0:T(8,128)(2,1)S(1)}, bf16[2,16,2560]{2,1,0:T(8,128)(2,1)S(1)}, u32[]{:S(2)}, u32[]{:S(2)}) collective-permute-start(bf16[2,16,2560]{2,1,0:T(8,128)(2,1)S(1)} %get-tuple-element.28), channel_id=1, source_target_pairs={{0,1},{1,0},{2,3},{3,2},{4,5},{5,4},{6,7},{7,6},{8,9},{9,8},{10,11... | collective-permute-start | bytes 491528 | tf_op jit(solution)/shard_map/ppermute | solution.py:568
  1.7 2.6 %collective-permute-start.1 = (bf16[2,32,128]{2,1,0:T(8,128)(2,1)S(1)}, bf16[2,32,128]{2,1,0:T(8,128)(2,1)S(1)}, u32[]{:S(2)}, u32[]{:S(2)}) collective-permute-start(bf16[2,32,128]{2,1,0:T(8,128)(2,1)S(1)} %get-tuple-element.26), channel_id=1, source_target_pairs={{0,2},{2,0},{1,3},{3,1},{4,6},{6,4},{5,7},{7,5},{8,10},{10,8},{9,1... | collective-permute-start | bytes 49160 | tf_op jit(solution)/shard_map/ppermute | solution.py:566
  4.3 0.1 collective-permute-start.2
  4.4 0.3 %shard_map.47 = bf16[128,128]{1,0:T(8,128)(2,1)S(1)} custom-call(bf16[2,32,2944]{2,1,0:T(8,128)(2,1)S(1)} %get-tuple-element.21.held_ref, bf16[2,32,48]{2,1,0:T(8,128)(2,1)S(1)} %get-tuple-element.22.line_ref, bf16[384,256]{1,0:T(8,128)(2,1)S(1)} %get-tuple-element.23.column_ref), custom_call_target="tpu_custom_call" | custom-call | tf_op jit(solution)/shard_map/pallas_call | solution.py:571
  4.7 2.9 %collective-permute-start = (bf16[128,128]{1,0:T(8,128)(2,1)S(1)}, bf16[128,128]{1,0:T(8,128)(2,1)S(1)}, u32[]{:S(2)}, u32[]{:S(2)}) collective-permute-start(bf16[128,128]{1,0:T(8,128)(2,1)S(1)} %shard_map.47), channel_id=1, source_target_pairs={{0,8},{4,12},{8,0},{12,4},{1,9},{5,13},{9,1},{13,5},{2,10},{6,14},... | collective-permute-start | bytes 98312 | tf_op jit(solution)/shard_map/ppermute | solution.py:578
  7.6 0.0 collective-permute-done.2.corner_ref
  7.6 0.0 collective-permute-done.1.side_ref
  7.6 0.0 collective-permute-done.3.lines_ref
  7.6 1.2 %shard_map.49 = (bf16[336,128]{1,0:T(8,128)(2,1)S(1)}, bf16[336,128]{1,0:T(8,128)(2,1)S(1)}, bf16[336,128]{1,0:T(8,128)(2,1)S(1)}, bf16[208,128]{1,0:T(8,128)(2,1)S(1)}) custom-call(bf16[2,32,128]{2,1,0:T(8,128)(2,1)S(1)} %collective-permute-done.1.side_ref, bf16[2,16,128]{2,1,0:T(8,128)(2,1)S(1)} %collective-permute-done.2.corner_ref, ...), custom_call_target="tpu_custom_call" | custom-call | tf_op jit(solution)/shard_map/pallas_call | solution.py:580
  8.8 3.4 %collective-permute-start.5 = (bf16[336,128]{1,0:T(8,128)(2,1)S(1)}, bf16[336,128]{1,0:T(8,128)(2,1)S(1)}, u32[]{:S(2)}, u32[]{:S(2)}) collective-permute-start(bf16[336,128]{1,0:T(8,128)(2,1)S(1)} %get-tuple-element.30), channel_id=1, source_target_pairs={{0,12},{4,8},{8,4},{12,0},{1,13},{5,9},{9,5},{13,1},{2,14},{6,10},... | collective-permute-start | bytes 258056 | tf_op jit(solution)/shard_map/ppermute | solution.py:595
  12.2 0.0 collective-permute-start.6
  12.2 1.0 %collective-permute-start.4 = (bf16[208,128]{1,0:T(8,128)(2,1)S(1)}, bf16[208,128]{1,0:T(8,128)(2,1)S(1)}, u32[]{:S(2)}, u32[]{:S(2)}) collective-permute-start(bf16[208,128]{1,0:T(8,128)(2,1)S(1)} %get-tuple-element.29), channel_id=1, source_target_pairs={{0,8},{4,12},{8,0},{12,4},{1,9},{5,13},{9,1},{13,5},{2,10},{6,14},... | collective-permute-start | bytes 159752 | tf_op jit(solution)/shard_map/ppermute | solution.py:595
  13.3 0.0 collective-permute-done.early_ref
  13.3 1.2 %shard_map.48 = (bf16[6,2,256,256]{3,2,1,0:T(8,128)(2,1)S(1)}, bf16[320,128]{1,0:T(8,128)(2,1)S(1)}) custom-call(f32[4]{0:T(128)} %shift_hbm.1, bf16[128,128]{1,0:T(8,128)(2,1)S(1)} %collective-permute-done.early_ref), custom_call_target="tpu_custom_call" | custom-call | flops 600000000 | tf_op jit(solution)/shard_map/pallas_call | solution.py:602
  14.5 3.5 %collective-permute-done.4.refs_1_ = bf16[208,128]{1,0:T(8,128)(2,1)S(1)} collective-permute-done((bf16[208,128]{1,0:T(8,128)(2,1)S(1)}, bf16[208,128]{1,0:T(8,128)(2,1)S(1)}, u32[]{:S(2)}, u32[]{:S(2)}) %collective-permute-start.4) | collective-permute-done | bytes 53280 | tf_op jit(solution)/shard_map/ppermute | solution.py:595
  18.0 0.0 collective-permute-done.5.refs_2_
  18.0 0.4 %collective-permute-done.6.refs_3_ = bf16[336,128]{1,0:T(8,128)(2,1)S(1)} collective-permute-done((bf16[336,128]{1,0:T(8,128)(2,1)S(1)}, bf16[336,128]{1,0:T(8,128)(2,1)S(1)}, u32[]{:S(2)}, u32[]{:S(2)}) %collective-permute-start.6) | collective-permute-done | bytes 86048 | tf_op jit(solution)/shard_map/ppermute | solution.py:595
  18.4 1.6 %shard_map.50 = (f32[8,256]{1,0:T(8,128)S(1)}, f32[8,256]{1,0:T(8,128)S(1)}, f32[8,256]{1,0:T(8,128)S(1)}, f32[8,256]{1,0:T(8,128)S(1)}) custom-call(bf16[6,2,256,256]{3,2,1,0:T(8,128)(2,1)S(1)} %get-tuple-element.24.weight_ref, bf16[320,128]{1,0:T(8,128)(2,1)S(1)} %get-tuple-element.25.refs_0_, bf16[208,128]{1,0:T(8,128)(2,1)S(1)} %collective-permute-done.4.refs_1_, ...), custom_call_target="tpu_custom_call" | custom-call | tf_op jit(solution)/shard_map/pallas_call | solution.py:614
  20.0 2.4 %collective-permute-start.7 = (f32[8,256]{1,0:T(8,128)S(1)}, f32[8,256]{1,0:T(8,128)S(1)}, u32[]{:S(2)}, u32[]{:S(2)}) collective-permute-start(f32[8,256]{1,0:T(8,128)S(1)} %get-tuple-element.33), channel_id=1, source_target_pairs={{0,8},{4,12},{8,0},{12,4},{1,9},{5,13},{9,1},{13,5},{2,10},{6,14},... | collective-permute-start | bytes 24584 | tf_op jit(solution)/shard_map/ppermute | solution.py:595
  22.4 0.9 %collective-permute-start.8 = (f32[8,256]{1,0:T(8,128)S(1)}, f32[8,256]{1,0:T(8,128)S(1)}, u32[]{:S(2)}, u32[]{:S(2)}) collective-permute-start(f32[8,256]{1,0:T(8,128)S(1)} %get-tuple-element.34), channel_id=1, source_target_pairs={{0,12},{4,8},{8,4},{12,0},{1,13},{5,9},{9,5},{13,1},{2,14},{6,10},... | collective-permute-start | bytes 24584 | tf_op jit(solution)/shard_map/ppermute | solution.py:595
  23.3 0.2 collective-permute-start.9
  23.5 1.1 %collective-permute-done.7.refs_0_ = f32[8,256]{1,0:T(8,128)S(1)} collective-permute-done((f32[8,256]{1,0:T(8,128)S(1)}, f32[8,256]{1,0:T(8,128)S(1)}, u32[]{:S(2)}, u32[]{:S(2)}) %collective-permute-start.7) | collective-permute-done | bytes 8224 | tf_op jit(solution)/shard_map/ppermute | solution.py:595
  24.6 3.2 %collective-permute-done.8.refs_1_ = f32[8,256]{1,0:T(8,128)S(1)} collective-permute-done((f32[8,256]{1,0:T(8,128)S(1)}, f32[8,256]{1,0:T(8,128)S(1)}, u32[]{:S(2)}, u32[]{:S(2)}) %collective-permute-start.8) | collective-permute-done | bytes 8224 | tf_op jit(solution)/shard_map/ppermute | solution.py:595
  27.8 0.0 collective-permute-done.9.refs_2_
  27.8 0.7 %shard_map.51 = f32[2,8,8,128]{3,2,1,0:T(8,128)} custom-call(f32[8,256]{1,0:T(8,128)S(1)} %collective-permute-done.7.refs_0_, f32[8,256]{1,0:T(8,128)S(1)} %collective-permute-done.8.refs_1_, f32[8,256]{1,0:T(8,128)S(1)} %collective-permute-done.9.refs_2_, f32[8,256]{1,0:T(8,128)S(1)} %get-tuple-element.36.refs_3_), custom_call_target="tpu_custom_call" | custom-call | tf_op jit(solution)/shard_map/pallas_call | solution.py:626
Async XLA Ops:
  1.2 6.4 %collective-permute-start.3 = (bf16[2,16,2560]{2,1,0:T(8,128)(2,1)S(1)}, bf16[2,16,2560]{2,1,0:T(8,128)(2,1)S(1)}, u32[]{:S(2)}, u32[]{:S(2)}) collective-permute-start(bf16[2,16,2560]{2,1,0:T(8,128)(2,1)S(1)} %get-tuple-element.28), channel_id=1, source_target_pairs={{0,1},{1,0},{2,3},{3,2},{4,5},{5,4},{6,7},{7,6},{8,9},{9,8},{10,11... | collective-permute-start | bytes 491528 | tf_op jit(solution)/shard_map/ppermute | solution.py:568
  1.7 5.9 %collective-permute-start.1 = (bf16[2,32,128]{2,1,0:T(8,128)(2,1)S(1)}, bf16[2,32,128]{2,1,0:T(8,128)(2,1)S(1)}, u32[]{:S(2)}, u32[]{:S(2)}) collective-permute-start(bf16[2,32,128]{2,1,0:T(8,128)(2,1)S(1)} %get-tuple-element.26), channel_id=1, source_target_pairs={{0,2},{2,0},{1,3},{3,1},{4,6},{6,4},{5,7},{7,5},{8,10},{10,8},{9,1... | collective-permute-start | bytes 49160 | tf_op jit(solution)/shard_map/ppermute | solution.py:566
  4.3 3.3 %collective-permute-start.2 = (bf16[2,16,128]{2,1,0:T(8,128)(2,1)S(1)}, bf16[2,16,128]{2,1,0:T(8,128)(2,1)S(1)}, u32[]{:S(2)}, u32[]{:S(2)}) collective-permute-start(bf16[2,16,128]{2,1,0:T(8,128)(2,1)S(1)} %get-tuple-element.27), channel_id=1, source_target_pairs={{0,3},{1,2},{2,1},{3,0},{4,7},{5,6},{6,5},{7,4},{8,11},{9,10},{10,... | collective-permute-start | bytes 24584 | tf_op jit(solution)/shard_map/ppermute | solution.py:567
  4.7 8.5 %collective-permute-start = (bf16[128,128]{1,0:T(8,128)(2,1)S(1)}, bf16[128,128]{1,0:T(8,128)(2,1)S(1)}, u32[]{:S(2)}, u32[]{:S(2)}) collective-permute-start(bf16[128,128]{1,0:T(8,128)(2,1)S(1)} %shard_map.47), channel_id=1, source_target_pairs={{0,8},{4,12},{8,0},{12,4},{1,9},{5,13},{9,1},{13,5},{2,10},{6,14},... | collective-permute-start | bytes 98312 | tf_op jit(solution)/shard_map/ppermute | solution.py:578
  8.8 9.1 %collective-permute-start.5 = (bf16[336,128]{1,0:T(8,128)(2,1)S(1)}, bf16[336,128]{1,0:T(8,128)(2,1)S(1)}, u32[]{:S(2)}, u32[]{:S(2)}) collective-permute-start(bf16[336,128]{1,0:T(8,128)(2,1)S(1)} %get-tuple-element.30), channel_id=1, source_target_pairs={{0,12},{4,8},{8,4},{12,0},{1,13},{5,9},{9,5},{13,1},{2,14},{6,10},... | collective-permute-start | bytes 258056 | tf_op jit(solution)/shard_map/ppermute | solution.py:595
  12.2 6.1 %collective-permute-start.6 = (bf16[336,128]{1,0:T(8,128)(2,1)S(1)}, bf16[336,128]{1,0:T(8,128)(2,1)S(1)}, u32[]{:S(2)}, u32[]{:S(2)}) collective-permute-start(bf16[336,128]{1,0:T(8,128)(2,1)S(1)} %get-tuple-element.31), channel_id=1, source_target_pairs={{0,4},{4,0},{8,12},{12,8},{1,5},{5,1},{9,13},{13,9},{2,6},{6,2},{1... | collective-permute-start | bytes 258056 | tf_op jit(solution)/shard_map/ppermute | solution.py:595
  12.2 5.7 %collective-permute-start.4 = (bf16[208,128]{1,0:T(8,128)(2,1)S(1)}, bf16[208,128]{1,0:T(8,128)(2,1)S(1)}, u32[]{:S(2)}, u32[]{:S(2)}) collective-permute-start(bf16[208,128]{1,0:T(8,128)(2,1)S(1)} %get-tuple-element.29), channel_id=1, source_target_pairs={{0,8},{4,12},{8,0},{12,4},{1,9},{5,13},{9,1},{13,5},{2,10},{6,14},... | collective-permute-start | bytes 159752 | tf_op jit(solution)/shard_map/ppermute | solution.py:595
  20.0 4.6 %collective-permute-start.7 = (f32[8,256]{1,0:T(8,128)S(1)}, f32[8,256]{1,0:T(8,128)S(1)}, u32[]{:S(2)}, u32[]{:S(2)}) collective-permute-start(f32[8,256]{1,0:T(8,128)S(1)} %get-tuple-element.33), channel_id=1, source_target_pairs={{0,8},{4,12},{8,0},{12,4},{1,9},{5,13},{9,1},{13,5},{2,10},{6,14},... | collective-permute-start | bytes 24584 | tf_op jit(solution)/shard_map/ppermute | solution.py:595
  22.4 5.4 %collective-permute-start.8 = (f32[8,256]{1,0:T(8,128)S(1)}, f32[8,256]{1,0:T(8,128)S(1)}, u32[]{:S(2)}, u32[]{:S(2)}) collective-permute-start(f32[8,256]{1,0:T(8,128)S(1)} %get-tuple-element.34), channel_id=1, source_target_pairs={{0,12},{4,8},{8,4},{12,0},{1,13},{5,9},{9,5},{13,1},{2,14},{6,10},... | collective-permute-start | bytes 24584 | tf_op jit(solution)/shard_map/ppermute | solution.py:595
  23.3 4.5 %collective-permute-start.9 = (f32[8,256]{1,0:T(8,128)S(1)}, f32[8,256]{1,0:T(8,128)S(1)}, u32[]{:S(2)}, u32[]{:S(2)}) collective-permute-start(f32[8,256]{1,0:T(8,128)S(1)} %get-tuple-element.35), channel_id=1, source_target_pairs={{0,4},{4,0},{8,12},{12,8},{1,5},{5,1},{9,13},{13,9},{2,6},{6,2},{1... | collective-permute-start | bytes 24584 | tf_op jit(solution)/shard_map/ppermute | solution.py:595
where the time goes:
time: 28.7 us; the launch traced here: 28.6 us
  starting transfers between devices  14 us (49%)
  waiting for transfers between devices  8.22 us (29%)
  Pallas kernels  6.29 us (22%)
    ppermute x6, waiting for transfers between devices, exchanged(): lax.ppermute(values[step], 'date', [(i, i ^ reach(step, dates)) for i in...  8.21 us
    ppermute x6, starting transfers between devices, exchanged(): lax.ppermute(values[step], 'date', [(i, i ^ reach(step, dates)) for i in...  7.98 us
    ppermute x1, starting transfers between devices, tiled_body(): lax.ppermute(early, 'date', [(i, i ^ reach(dates - 1, dates)) for i in ra...  2.89 us
    ppermute x1, starting transfers between devices, tiled_body(): side = lax.ppermute(side, 'rng', swap)  2.56 us
    pallas_call x1, Pallas kernels, tiled_body(): pl.pallas_call(functools.partial(looks_kernel, pairs, dates), out_shape=[...  1.58 us
    pallas_call x1, Pallas kernels, tiled_body(): pl.pallas_call(functools.partial(filter_kernel, pairs), out_shape=[jax.Sh...  1.23 us
    pallas_call x1, Pallas kernels, tiled_body(): pl.pallas_call(prepare_kernel, out_shape=[jax.ShapeDtypeStruct((2, lines,...  1.21 us
    pallas_call x1, Pallas kernels, tiled_body(): pl.pallas_call(resample_kernel, out_shape=[jax.ShapeDtypeStruct((rows, LA...  1.2 us
  transfers between devices with their start and end apart: 10, of which 4 were waited for; matrix products, arithmetic and copies ran while one was open for 0% of the time, Pallas kernels for 10%

commit v1 on v0

--- a/solution.py
+++ b/solution.py
@@ -516,7 +516,7 @@
     out_ref[...] = jnp.zeros_like(out_ref)
     each = LANES // looks
     for step, recv_ref in enumerate(refs[:-1][::-1]):
-        chunk = date ^ reach(step, len(refs) - 1)
+        chunk = date ^ step
         for lag in range(used_lags):
             for part in range(2):
                 tile, group = divmod(lag * 2 + part, each)
@@ -623,13 +623,15 @@
         ],
         compiler_params=limit,
     )(weights, early, *chunks)
+    returned = exchanged(looked, steps)[::-1]
+    returned = [returned[reach(distance, dates)] for distance in reversed(range(dates))]
     out = pl.pallas_call(
         functools.partial(place_kernel, min(LAGS, dates - 1), looks),
         out_shape=jax.ShapeDtypeStruct((2, LAGS, groups, looks * dates), jnp.float32),
         in_specs=[vmem] * dates,
         out_specs=vmem,
         compiler_params=limit,
-    )(*exchanged(looked, steps))
+    )(*returned)
     return out[:, None]
 
 

time: 28.7 us -> 27.2 us (0.948)
  waiting for transfers between devices: 8.22 us -> 5.84 us
  starting transfers between devices: 14 us -> 14.9 us
    ppermute x6, waiting for transfers between devices: 8.21 us -> 5.83 us  [exchanged(): lax.ppermute(values[step], 'date', [(i, i ^ reach(step, dates)) for i in...]
    ppermute x6, starting transfers between devices: 7.98 us -> 8.88 us  [exchanged(): lax.ppermute(values[step], 'date', [(i, i ^ reach(step, dates)) for i in...]
where the time goes in v1:
time: 27.2 us; the launch traced here: 27.1 us
  starting transfers between devices  14.9 us (55%)
  Pallas kernels  6.29 us (23%)
  waiting for transfers between devices  5.84 us (21%)
    ppermute x6, starting transfers between devices, exchanged(): lax.ppermute(values[step], 'date', [(i, i ^ reach(step, dates)) for i in...  8.88 us
    ppermute x6, waiting for transfers between devices, exchanged(): lax.ppermute(values[step], 'date', [(i, i ^ reach(step, dates)) for i in...  5.83 us
    ppermute x1, starting transfers between devices, tiled_body(): lax.ppermute(early, 'date', [(i, i ^ reach(dates - 1, dates)) for i in ra...  2.89 us
    ppermute x1, starting transfers between devices, tiled_body(): side = lax.ppermute(side, 'rng', swap)  2.56 us
    pallas_call x1, Pallas kernels, tiled_body(): pl.pallas_call(functools.partial(looks_kernel, pairs, dates), out_shape=[...  1.58 us
    pallas_call x1, Pallas kernels, tiled_body(): pl.pallas_call(functools.partial(filter_kernel, pairs), out_shape=[jax.Sh...  1.23 us
    pallas_call x1, Pallas kernels, tiled_body(): pl.pallas_call(prepare_kernel, out_shape=[jax.ShapeDtypeStruct((2, lines,...  1.21 us
    pallas_call x1, Pallas kernels, tiled_body(): pl.pallas_call(resample_kernel, out_shape=[jax.ShapeDtypeStruct((rows, LA...  1.2 us
  transfers between devices with their start and end apart: 10, of which 4 were waited for; matrix products, arithmetic and copies ran while one was open for 0% of the time, Pallas kernels for 10%

profile of v1, /device:TPU:0, one launch (start us, length us, event | category | flops | bytes accessed | tf_op | source)
XLA Modules:
  0.0 27.1 jit_solution(15035756323527265454)
XLA Ops:
  0.0 1.2 %shard_map.46 = (bf16[2,32,128]{2,1,0:T(8,128)(2,1)S(1)}, bf16[2,16,128]{2,1,0:T(8,128)(2,1)S(1)}, bf16[2,16,2560]{2,1,0:T(8,128)(2,1)S(1)}, bf16[2,32,48]{2,1,0...) custom-call(s32[1,2]{1,0:T(1,128)} %offsets_hbm.1, s32[1,2]{1,0:T(1,128)} %index_hbm.1, ...), custom_call_target="tpu_custom_call" | custom-call | tf_op jit(solution)/shard_map/pallas_call | solution.py:546
  1.2 0.5 %collective-permute-start.3 = (bf16[2,16,2560]{2,1,0:T(8,128)(2,1)S(1)}, bf16[2,16,2560]{2,1,0:T(8,128)(2,1)S(1)}, u32[]{:S(2)}, u32[]{:S(2)}) collective-permute-start(bf16[2,16,2560]{2,1,0:T(8,128)(2,1)S(1)} %get-tuple-element.28), channel_id=1, source_target_pairs={{0,1},{1,0},{2,3},{3,2},{4,5},{5,4},{6,7},{7,6},{8,9},{9,8},{10,11... | collective-permute-start | bytes 491528 | tf_op jit(solution)/shard_map/ppermute | solution.py:568
  1.7 2.6 %collective-permute-start.1 = (bf16[2,32,128]{2,1,0:T(8,128)(2,1)S(1)}, bf16[2,32,128]{2,1,0:T(8,128)(2,1)S(1)}, u32[]{:S(2)}, u32[]{:S(2)}) collective-permute-start(bf16[2,32,128]{2,1,0:T(8,128)(2,1)S(1)} %get-tuple-element.26), channel_id=1, source_target_pairs={{0,2},{2,0},{1,3},{3,1},{4,6},{6,4},{5,7},{7,5},{8,10},{10,8},{9,1... | collective-permute-start | bytes 49160 | tf_op jit(solution)/shard_map/ppermute | solution.py:566
  4.3 0.1 collective-permute-start.2
  4.4 0.3 %shard_map.47 = bf16[128,128]{1,0:T(8,128)(2,1)S(1)} custom-call(bf16[2,32,2944]{2,1,0:T(8,128)(2,1)S(1)} %get-tuple-element.21.held_ref, bf16[2,32,48]{2,1,0:T(8,128)(2,1)S(1)} %get-tuple-element.22.line_ref, bf16[384,256]{1,0:T(8,128)(2,1)S(1)} %get-tuple-element.23.column_ref), custom_call_target="tpu_custom_call" | custom-call | tf_op jit(solution)/shard_map/pallas_call | solution.py:571
  4.7 2.9 %collective-permute-start = (bf16[128,128]{1,0:T(8,128)(2,1)S(1)}, bf16[128,128]{1,0:T(8,128)(2,1)S(1)}, u32[]{:S(2)}, u32[]{:S(2)}) collective-permute-start(bf16[128,128]{1,0:T(8,128)(2,1)S(1)} %shard_map.47), channel_id=1, source_target_pairs={{0,8},{4,12},{8,0},{12,4},{1,9},{5,13},{9,1},{13,5},{2,10},{6,14},... | collective-permute-start | bytes 98312 | tf_op jit(solution)/shard_map/ppermute | solution.py:578
  7.6 0.0 collective-permute-done.2.corner_ref
  7.6 0.0 collective-permute-done.1.side_ref
  7.6 0.0 collective-permute-done.3.lines_ref
  7.6 1.2 %shard_map.49 = (bf16[336,128]{1,0:T(8,128)(2,1)S(1)}, bf16[336,128]{1,0:T(8,128)(2,1)S(1)}, bf16[336,128]{1,0:T(8,128)(2,1)S(1)}, bf16[208,128]{1,0:T(8,128)(2,1)S(1)}) custom-call(bf16[2,32,128]{2,1,0:T(8,128)(2,1)S(1)} %collective-permute-done.1.side_ref, bf16[2,16,128]{2,1,0:T(8,128)(2,1)S(1)} %collective-permute-done.2.corner_ref, ...), custom_call_target="tpu_custom_call" | custom-call | tf_op jit(solution)/shard_map/pallas_call | solution.py:580
  8.8 3.4 %collective-permute-start.5 = (bf16[336,128]{1,0:T(8,128)(2,1)S(1)}, bf16[336,128]{1,0:T(8,128)(2,1)S(1)}, u32[]{:S(2)}, u32[]{:S(2)}) collective-permute-start(bf16[336,128]{1,0:T(8,128)(2,1)S(1)} %get-tuple-element.30), channel_id=1, source_target_pairs={{0,12},{4,8},{8,4},{12,0},{1,13},{5,9},{9,5},{13,1},{2,14},{6,10},... | collective-permute-start | bytes 258056 | tf_op jit(solution)/shard_map/ppermute | solution.py:595
  12.2 0.0 collective-permute-start.6
  12.2 1.0 %collective-permute-start.4 = (bf16[208,128]{1,0:T(8,128)(2,1)S(1)}, bf16[208,128]{1,0:T(8,128)(2,1)S(1)}, u32[]{:S(2)}, u32[]{:S(2)}) collective-permute-start(bf16[208,128]{1,0:T(8,128)(2,1)S(1)} %get-tuple-element.29), channel_id=1, source_target_pairs={{0,8},{4,12},{8,0},{12,4},{1,9},{5,13},{9,1},{13,5},{2,10},{6,14},... | collective-permute-start | bytes 159752 | tf_op jit(solution)/shard_map/ppermute | solution.py:595
  13.3 0.0 collective-permute-done.early_ref
  13.3 1.2 %shard_map.48 = (bf16[6,2,256,256]{3,2,1,0:T(8,128)(2,1)S(1)}, bf16[320,128]{1,0:T(8,128)(2,1)S(1)}) custom-call(f32[4]{0:T(128)} %shift_hbm.1, bf16[128,128]{1,0:T(8,128)(2,1)S(1)} %collective-permute-done.early_ref), custom_call_target="tpu_custom_call" | custom-call | flops 600000000 | tf_op jit(solution)/shard_map/pallas_call | solution.py:602
  14.5 3.5 %collective-permute-done.4.refs_1_ = bf16[208,128]{1,0:T(8,128)(2,1)S(1)} collective-permute-done((bf16[208,128]{1,0:T(8,128)(2,1)S(1)}, bf16[208,128]{1,0:T(8,128)(2,1)S(1)}, u32[]{:S(2)}, u32[]{:S(2)}) %collective-permute-start.4) | collective-permute-done | bytes 53280 | tf_op jit(solution)/shard_map/ppermute | solution.py:595
  18.0 0.0 collective-permute-done.5.refs_2_
  18.0 0.4 %collective-permute-done.6.refs_3_ = bf16[336,128]{1,0:T(8,128)(2,1)S(1)} collective-permute-done((bf16[336,128]{1,0:T(8,128)(2,1)S(1)}, bf16[336,128]{1,0:T(8,128)(2,1)S(1)}, u32[]{:S(2)}, u32[]{:S(2)}) %collective-permute-start.6) | collective-permute-done | bytes 86048 | tf_op jit(solution)/shard_map/ppermute | solution.py:595
  18.4 1.6 %shard_map.50 = (f32[8,256]{1,0:T(8,128)S(1)}, f32[8,256]{1,0:T(8,128)S(1)}, f32[8,256]{1,0:T(8,128)S(1)}, f32[8,256]{1,0:T(8,128)S(1)}) custom-call(bf16[6,2,256,256]{3,2,1,0:T(8,128)(2,1)S(1)} %get-tuple-element.24.weight_ref, bf16[320,128]{1,0:T(8,128)(2,1)S(1)} %get-tuple-element.25.refs_0_, bf16[208,128]{1,0:T(8,128)(2,1)S(1)} %collective-permute-done.4.refs_1_, ...), custom_call_target="tpu_custom_call" | custom-call | tf_op jit(solution)/shard_map/pallas_call | solution.py:614
  20.0 1.8 %collective-permute-start.7 = (f32[8,256]{1,0:T(8,128)S(1)}, f32[8,256]{1,0:T(8,128)S(1)}, u32[]{:S(2)}, u32[]{:S(2)}) collective-permute-start(f32[8,256]{1,0:T(8,128)S(1)} %get-tuple-element.33), channel_id=1, source_target_pairs={{0,12},{4,8},{8,4},{12,0},{1,13},{5,9},{9,5},{13,1},{2,14},{6,10},... | collective-permute-start | bytes 24584 | tf_op jit(solution)/shard_map/ppermute | solution.py:595
  21.8 0.7 %collective-permute-start.8 = (f32[8,256]{1,0:T(8,128)S(1)}, f32[8,256]{1,0:T(8,128)S(1)}, u32[]{:S(2)}, u32[]{:S(2)}) collective-permute-start(f32[8,256]{1,0:T(8,128)S(1)} %get-tuple-element.34), channel_id=1, source_target_pairs={{0,8},{4,12},{8,0},{12,4},{1,9},{5,13},{9,1},{13,5},{2,10},{6,14},... | collective-permute-start | bytes 24584 | tf_op jit(solution)/shard_map/ppermute | solution.py:595
  22.5 2.0 %collective-permute-start.9 = (f32[8,256]{1,0:T(8,128)S(1)}, f32[8,256]{1,0:T(8,128)S(1)}, u32[]{:S(2)}, u32[]{:S(2)}) collective-permute-start(f32[8,256]{1,0:T(8,128)S(1)} %get-tuple-element.35), channel_id=1, source_target_pairs={{0,4},{4,0},{8,12},{12,8},{1,5},{5,1},{9,13},{13,9},{2,6},{6,2},{1... | collective-permute-start | bytes 24584 | tf_op jit(solution)/shard_map/ppermute | solution.py:595
  24.4 1.1 %collective-permute-done.7.refs_0_ = f32[8,256]{1,0:T(8,128)S(1)} collective-permute-done((f32[8,256]{1,0:T(8,128)S(1)}, f32[8,256]{1,0:T(8,128)S(1)}, u32[]{:S(2)}, u32[]{:S(2)}) %collective-permute-start.7) | collective-permute-done | bytes 8224 | tf_op jit(solution)/shard_map/ppermute | solution.py:595
  25.5 0.9 %collective-permute-done.8.refs_1_ = f32[8,256]{1,0:T(8,128)S(1)} collective-permute-done((f32[8,256]{1,0:T(8,128)S(1)}, f32[8,256]{1,0:T(8,128)S(1)}, u32[]{:S(2)}, u32[]{:S(2)}) %collective-permute-start.8) | collective-permute-done | bytes 8224 | tf_op jit(solution)/shard_map/ppermute | solution.py:595
  26.4 0.0 collective-permute-done.9.refs_2_
  26.4 0.7 %shard_map.51 = f32[2,8,8,128]{3,2,1,0:T(8,128)} custom-call(f32[8,256]{1,0:T(8,128)S(1)} %collective-permute-done.7.refs_0_, f32[8,256]{1,0:T(8,128)S(1)} %collective-permute-done.8.refs_1_, f32[8,256]{1,0:T(8,128)S(1)} %collective-permute-done.9.refs_2_, f32[8,256]{1,0:T(8,128)S(1)} %get-tuple-element.36.refs_3_), custom_call_target="tpu_custom_call" | custom-call | tf_op jit(solution)/shard_map/pallas_call | solution.py:628
Async XLA Ops:
  1.2 6.4 %collective-permute-start.3 = (bf16[2,16,2560]{2,1,0:T(8,128)(2,1)S(1)}, bf16[2,16,2560]{2,1,0:T(8,128)(2,1)S(1)}, u32[]{:S(2)}, u32[]{:S(2)}) collective-permute-start(bf16[2,16,2560]{2,1,0:T(8,128)(2,1)S(1)} %get-tuple-element.28), channel_id=1, source_target_pairs={{0,1},{1,0},{2,3},{3,2},{4,5},{5,4},{6,7},{7,6},{8,9},{9,8},{10,11... | collective-permute-start | bytes 491528 | tf_op jit(solution)/shard_map/ppermute | solution.py:568
  1.7 5.9 %collective-permute-start.1 = (bf16[2,32,128]{2,1,0:T(8,128)(2,1)S(1)}, bf16[2,32,128]{2,1,0:T(8,128)(2,1)S(1)}, u32[]{:S(2)}, u32[]{:S(2)}) collective-permute-start(bf16[2,32,128]{2,1,0:T(8,128)(2,1)S(1)} %get-tuple-element.26), channel_id=1, source_target_pairs={{0,2},{2,0},{1,3},{3,1},{4,6},{6,4},{5,7},{7,5},{8,10},{10,8},{9,1... | collective-permute-start | bytes 49160 | tf_op jit(solution)/shard_map/ppermute | solution.py:566
  4.3 3.3 %collective-permute-start.2 = (bf16[2,16,128]{2,1,0:T(8,128)(2,1)S(1)}, bf16[2,16,128]{2,1,0:T(8,128)(2,1)S(1)}, u32[]{:S(2)}, u32[]{:S(2)}) collective-permute-start(bf16[2,16,128]{2,1,0:T(8,128)(2,1)S(1)} %get-tuple-element.27), channel_id=1, source_target_pairs={{0,3},{1,2},{2,1},{3,0},{4,7},{5,6},{6,5},{7,4},{8,11},{9,10},{10,... | collective-permute-start | bytes 24584 | tf_op jit(solution)/shard_map/ppermute | solution.py:567
  4.7 8.5 %collective-permute-start = (bf16[128,128]{1,0:T(8,128)(2,1)S(1)}, bf16[128,128]{1,0:T(8,128)(2,1)S(1)}, u32[]{:S(2)}, u32[]{:S(2)}) collective-permute-start(bf16[128,128]{1,0:T(8,128)(2,1)S(1)} %shard_map.47), channel_id=1, source_target_pairs={{0,8},{4,12},{8,0},{12,4},{1,9},{5,13},{9,1},{13,5},{2,10},{6,14},... | collective-permute-start | bytes 98312 | tf_op jit(solution)/shard_map/ppermute | solution.py:578
  8.8 9.1 %collective-permute-start.5 = (bf16[336,128]{1,0:T(8,128)(2,1)S(1)}, bf16[336,128]{1,0:T(8,128)(2,1)S(1)}, u32[]{:S(2)}, u32[]{:S(2)}) collective-permute-start(bf16[336,128]{1,0:T(8,128)(2,1)S(1)} %get-tuple-element.30), channel_id=1, source_target_pairs={{0,12},{4,8},{8,4},{12,0},{1,13},{5,9},{9,5},{13,1},{2,14},{6,10},... | collective-permute-start | bytes 258056 | tf_op jit(solution)/shard_map/ppermute | solution.py:595
  12.2 6.1 %collective-permute-start.6 = (bf16[336,128]{1,0:T(8,128)(2,1)S(1)}, bf16[336,128]{1,0:T(8,128)(2,1)S(1)}, u32[]{:S(2)}, u32[]{:S(2)}) collective-permute-start(bf16[336,128]{1,0:T(8,128)(2,1)S(1)} %get-tuple-element.31), channel_id=1, source_target_pairs={{0,4},{4,0},{8,12},{12,8},{1,5},{5,1},{9,13},{13,9},{2,6},{6,2},{1... | collective-permute-start | bytes 258056 | tf_op jit(solution)/shard_map/ppermute | solution.py:595
  12.2 5.7 %collective-permute-start.4 = (bf16[208,128]{1,0:T(8,128)(2,1)S(1)}, bf16[208,128]{1,0:T(8,128)(2,1)S(1)}, u32[]{:S(2)}, u32[]{:S(2)}) collective-permute-start(bf16[208,128]{1,0:T(8,128)(2,1)S(1)} %get-tuple-element.29), channel_id=1, source_target_pairs={{0,8},{4,12},{8,0},{12,4},{1,9},{5,13},{9,1},{13,5},{2,10},{6,14},... | collective-permute-start | bytes 159752 | tf_op jit(solution)/shard_map/ppermute | solution.py:595
  20.0 5.5 %collective-permute-start.7 = (f32[8,256]{1,0:T(8,128)S(1)}, f32[8,256]{1,0:T(8,128)S(1)}, u32[]{:S(2)}, u32[]{:S(2)}) collective-permute-start(f32[8,256]{1,0:T(8,128)S(1)} %get-tuple-element.33), channel_id=1, source_target_pairs={{0,12},{4,8},{8,4},{12,0},{1,13},{5,9},{9,5},{13,1},{2,14},{6,10},... | collective-permute-start | bytes 24584 | tf_op jit(solution)/shard_map/ppermute | solution.py:595
  21.8 4.5 %collective-permute-start.8 = (f32[8,256]{1,0:T(8,128)S(1)}, f32[8,256]{1,0:T(8,128)S(1)}, u32[]{:S(2)}, u32[]{:S(2)}) collective-permute-start(f32[8,256]{1,0:T(8,128)S(1)} %get-tuple-element.34), channel_id=1, source_target_pairs={{0,8},{4,12},{8,0},{12,4},{1,9},{5,13},{9,1},{13,5},{2,10},{6,14},... | collective-permute-start | bytes 24584 | tf_op jit(solution)/shard_map/ppermute | solution.py:595
  22.5 3.9 %collective-permute-start.9 = (f32[8,256]{1,0:T(8,128)S(1)}, f32[8,256]{1,0:T(8,128)S(1)}, u32[]{:S(2)}, u32[]{:S(2)}) collective-permute-start(f32[8,256]{1,0:T(8,128)S(1)} %get-tuple-element.35), channel_id=1, source_target_pairs={{0,4},{4,0},{8,12},{12,8},{1,5},{5,1},{9,13},{13,9},{2,6},{6,2},{1... | collective-permute-start | bytes 24584 | tf_op jit(solution)/shard_map/ppermute | solution.py:595

commit v2 on v1

--- a/solution.py
+++ b/solution.py
@@ -318,8 +318,13 @@
         (slc_ref.at[:, :, outermost], side_ref),
         (slc_ref.at[:, nearest, outermost], corner_ref),
         (slc_ref.at[:, nearest, :], lines_ref),
-        (slc_ref, held_ref.at[:, :, pl.ds(LANES, columns)]),
     ]
+    for plane in range(2):
+        for part in range(lines // HALO_LINES):
+            for side in range(2):
+                at = pl.ds(part * HALO_LINES, HALO_LINES)
+                source = slc_ref.at[plane, at, pl.ds(side * columns // 2, columns // 2)]
+                moves.append((source, held_ref.at[plane, at, pl.ds(LANES + side * columns // 2, columns // 2)]))
     copies = [pltpu.make_async_copy(a, b, semaphores.at[i]) for i, (a, b) in enumerate(moves)]
     for copy in copies:
         copy.start()
@@ -433,8 +438,8 @@
             spread = jnp.broadcast_to(taps, (LANES, 2 * LANES))
             spread = pltpu.roll(spread, 0, 1, stride=1, stride_axis=0)
             high, low = halves(spread)
-            out_ref[place, 0, part * LANES : (part + 1) * LANES, :] = high
-            out_ref[place, 1, part * LANES : (part + 1) * LANES, :] = low
+            out_ref[place, part * LANES : (part + 1) * LANES, : 2 * LANES] = high
+            out_ref[place, part * LANES : (part + 1) * LANES, 2 * LANES :] = low
 
 
 def looks_kernel(pairs, dates, weight_ref, *refs):
@@ -467,7 +472,8 @@
             window_ref[step, at, LANES:] = value.astype(jnp.bfloat16)
     for place, (first, second) in enumerate(pairs):
         def filtered(step):
-            total = dot_nt(window_ref[step], weight_ref[place, 0]) + dot_nt(window_ref[step], weight_ref[place, 1])
+            window = window_ref[step]
+            total = dot_nt(jnp.concatenate([window, window], axis=1), weight_ref[place])
             total = total.reshape(blocks, 2, 2, HALO_LINES, 2 * LANES)
             re, im = total[:, :, 0], total[:, :, 1]
             return re[..., :LANES], im[..., :LANES], re[..., LANES:], im[..., LANES:]
@@ -558,7 +564,7 @@
         scratch_shapes=[
             pltpu.SMEM(offsets.shape, jnp.int32),
             pltpu.SMEM(kernel_index.shape, jnp.int32),
-            pltpu.SemaphoreType.DMA((6,)),
+            pltpu.SemaphoreType.DMA((5 + 4 * (lines // HALO_LINES),)),
         ],
         compiler_params=limit,
     )(offsets, kernel_index, cells)
@@ -602,7 +608,7 @@
     weights, early = pl.pallas_call(
         functools.partial(filter_kernel, pairs),
         out_shape=[
-            jax.ShapeDtypeStruct((len(pairs), 2, 2 * LANES, 2 * LANES), bf16),
+            jax.ShapeDtypeStruct((len(pairs), 2 * LANES, 4 * LANES), bf16),
             jax.ShapeDtypeStruct((chunk_rows, LANES), bf16),
         ],
         in_specs=[hbm, vmem],

time: 27.2 us -> 27.2 us (level)
  no operation moved by 1% of the time
where the time goes in v2:
time: 27.2 us; the launch traced here: 27.1 us
  starting transfers between devices  14.9 us (55%)
  Pallas kernels  6.27 us (23%)
  waiting for transfers between devices  5.84 us (21%)
    ppermute x6, starting transfers between devices, exchanged(): lax.ppermute(values[step], 'date', [(i, i ^ reach(step, dates)) for i in...  8.88 us
    ppermute x6, waiting for transfers between devices, exchanged(): lax.ppermute(values[step], 'date', [(i, i ^ reach(step, dates)) for i in...  5.83 us
    ppermute x1, starting transfers between devices, tiled_body(): lax.ppermute(early, 'date', [(i, i ^ reach(dates - 1, dates)) for i in ra...  2.89 us
    ppermute x1, starting transfers between devices, tiled_body(): side = lax.ppermute(side, 'rng', swap)  2.56 us
    pallas_call x1, Pallas kernels, tiled_body(): pl.pallas_call(functools.partial(looks_kernel, pairs, dates), out_shape=[...  1.57 us
    pallas_call x1, Pallas kernels, tiled_body(): pl.pallas_call(functools.partial(filter_kernel, pairs), out_shape=[jax.Sh...  1.23 us
    pallas_call x1, Pallas kernels, tiled_body(): pl.pallas_call(prepare_kernel, out_shape=[jax.ShapeDtypeStruct((2, lines,...  1.2 us
    pallas_call x1, Pallas kernels, tiled_body(): pl.pallas_call(resample_kernel, out_shape=[jax.ShapeDtypeStruct((rows, LA...  1.2 us
  transfers between devices with their start and end apart: 10, of which 4 were waited for; matrix products, arithmetic and copies ran while one was open for 0% of the time, Pallas kernels for 10%

profile of v2, /device:TPU:0, one launch (start us, length us, event | category | flops | bytes accessed | tf_op | source)
XLA Modules:
  0.0 27.1 jit_solution(3765847726540657302)
XLA Ops:
  0.0 1.2 %shard_map.46 = (bf16[2,32,128]{2,1,0:T(8,128)(2,1)S(1)}, bf16[2,16,128]{2,1,0:T(8,128)(2,1)S(1)}, bf16[2,16,2560]{2,1,0:T(8,128)(2,1)S(1)}, bf16[2,32,48]{2,1,0...) custom-call(s32[1,2]{1,0:T(1,128)} %offsets_hbm.1, s32[1,2]{1,0:T(1,128)} %index_hbm.1, ...), custom_call_target="tpu_custom_call" | custom-call | tf_op jit(solution)/shard_map/pallas_call | solution.py:552
  1.2 0.5 %collective-permute-start.3 = (bf16[2,16,2560]{2,1,0:T(8,128)(2,1)S(1)}, bf16[2,16,2560]{2,1,0:T(8,128)(2,1)S(1)}, u32[]{:S(2)}, u32[]{:S(2)}) collective-permute-start(bf16[2,16,2560]{2,1,0:T(8,128)(2,1)S(1)} %get-tuple-element.28), channel_id=1, source_target_pairs={{0,1},{1,0},{2,3},{3,2},{4,5},{5,4},{6,7},{7,6},{8,9},{9,8},{10,11... | collective-permute-start | bytes 491528 | tf_op jit(solution)/shard_map/ppermute | solution.py:574
  1.7 2.6 %collective-permute-start.1 = (bf16[2,32,128]{2,1,0:T(8,128)(2,1)S(1)}, bf16[2,32,128]{2,1,0:T(8,128)(2,1)S(1)}, u32[]{:S(2)}, u32[]{:S(2)}) collective-permute-start(bf16[2,32,128]{2,1,0:T(8,128)(2,1)S(1)} %get-tuple-element.26), channel_id=1, source_target_pairs={{0,2},{2,0},{1,3},{3,1},{4,6},{6,4},{5,7},{7,5},{8,10},{10,8},{9,1... | collective-permute-start | bytes 49160 | tf_op jit(solution)/shard_map/ppermute | solution.py:572
  4.3 0.1 collective-permute-start.2
  4.4 0.3 %shard_map.47 = bf16[128,128]{1,0:T(8,128)(2,1)S(1)} custom-call(bf16[2,32,2944]{2,1,0:T(8,128)(2,1)S(1)} %get-tuple-element.21.held_ref, bf16[2,32,48]{2,1,0:T(8,128)(2,1)S(1)} %get-tuple-element.22.line_ref, bf16[384,256]{1,0:T(8,128)(2,1)S(1)} %get-tuple-element.23.column_ref), custom_call_target="tpu_custom_call" | custom-call | tf_op jit(solution)/shard_map/pallas_call | solution.py:577
  4.7 2.9 %collective-permute-start = (bf16[128,128]{1,0:T(8,128)(2,1)S(1)}, bf16[128,128]{1,0:T(8,128)(2,1)S(1)}, u32[]{:S(2)}, u32[]{:S(2)}) collective-permute-start(bf16[128,128]{1,0:T(8,128)(2,1)S(1)} %shard_map.47), channel_id=1, source_target_pairs={{0,8},{4,12},{8,0},{12,4},{1,9},{5,13},{9,1},{13,5},{2,10},{6,14},... | collective-permute-start | bytes 98312 | tf_op jit(solution)/shard_map/ppermute | solution.py:584
  7.6 0.0 collective-permute-done.2.corner_ref
  7.6 0.0 collective-permute-done.1.side_ref
  7.6 0.0 collective-permute-done.3.lines_ref
  7.6 1.2 %shard_map.49 = (bf16[336,128]{1,0:T(8,128)(2,1)S(1)}, bf16[336,128]{1,0:T(8,128)(2,1)S(1)}, bf16[336,128]{1,0:T(8,128)(2,1)S(1)}, bf16[208,128]{1,0:T(8,128)(2,1)S(1)}) custom-call(bf16[2,32,128]{2,1,0:T(8,128)(2,1)S(1)} %collective-permute-done.1.side_ref, bf16[2,16,128]{2,1,0:T(8,128)(2,1)S(1)} %collective-permute-done.2.corner_ref, ...), custom_call_target="tpu_custom_call" | custom-call | tf_op jit(solution)/shard_map/pallas_call | solution.py:586
  8.8 3.4 %collective-permute-start.5 = (bf16[336,128]{1,0:T(8,128)(2,1)S(1)}, bf16[336,128]{1,0:T(8,128)(2,1)S(1)}, u32[]{:S(2)}, u32[]{:S(2)}) collective-permute-start(bf16[336,128]{1,0:T(8,128)(2,1)S(1)} %get-tuple-element.30), channel_id=1, source_target_pairs={{0,12},{4,8},{8,4},{12,0},{1,13},{5,9},{9,5},{13,1},{2,14},{6,10},... | collective-permute-start | bytes 258056 | tf_op jit(solution)/shard_map/ppermute | solution.py:601
  12.2 0.0 collective-permute-start.6
  12.2 1.0 %collective-permute-start.4 = (bf16[208,128]{1,0:T(8,128)(2,1)S(1)}, bf16[208,128]{1,0:T(8,128)(2,1)S(1)}, u32[]{:S(2)}, u32[]{:S(2)}) collective-permute-start(bf16[208,128]{1,0:T(8,128)(2,1)S(1)} %get-tuple-element.29), channel_id=1, source_target_pairs={{0,8},{4,12},{8,0},{12,4},{1,9},{5,13},{9,1},{13,5},{2,10},{6,14},... | collective-permute-start | bytes 159752 | tf_op jit(solution)/shard_map/ppermute | solution.py:601
  13.3 0.0 collective-permute-done.early_ref
  13.3 1.2 %shard_map.48 = (bf16[6,256,512]{2,1,0:T(8,128)(2,1)S(1)}, bf16[320,128]{1,0:T(8,128)(2,1)S(1)}) custom-call(f32[4]{0:T(128)} %shift_hbm.1, bf16[128,128]{1,0:T(8,128)(2,1)S(1)} %collective-permute-done.early_ref), custom_call_target="tpu_custom_call" | custom-call | flops 600000000 | tf_op jit(solution)/shard_map/pallas_call | solution.py:608
  14.5 3.5 %collective-permute-done.4.refs_1_ = bf16[208,128]{1,0:T(8,128)(2,1)S(1)} collective-permute-done((bf16[208,128]{1,0:T(8,128)(2,1)S(1)}, bf16[208,128]{1,0:T(8,128)(2,1)S(1)}, u32[]{:S(2)}, u32[]{:S(2)}) %collective-permute-start.4) | collective-permute-done | bytes 53280 | tf_op jit(solution)/shard_map/ppermute | solution.py:601
  18.0 0.0 collective-permute-done.5.refs_2_
  18.0 0.4 %collective-permute-done.6.refs_3_ = bf16[336,128]{1,0:T(8,128)(2,1)S(1)} collective-permute-done((bf16[336,128]{1,0:T(8,128)(2,1)S(1)}, bf16[336,128]{1,0:T(8,128)(2,1)S(1)}, u32[]{:S(2)}, u32[]{:S(2)}) %collective-permute-start.6) | collective-permute-done | bytes 86048 | tf_op jit(solution)/shard_map/ppermute | solution.py:601
  18.4 1.6 %shard_map.50 = (f32[8,256]{1,0:T(8,128)S(1)}, f32[8,256]{1,0:T(8,128)S(1)}, f32[8,256]{1,0:T(8,128)S(1)}, f32[8,256]{1,0:T(8,128)S(1)}) custom-call(bf16[6,256,512]{2,1,0:T(8,128)(2,1)S(1)} %get-tuple-element.24.weight_ref, bf16[320,128]{1,0:T(8,128)(2,1)S(1)} %get-tuple-element.25.refs_0_, bf16[208,128]{1,0:T(8,128)(2,1)S(1)} %collective-permute-done.4.refs_1_, ...), custom_call_target="tpu_custom_call" | custom-call | tf_op jit(solution)/shard_map/pallas_call | solution.py:620
  20.0 1.8 %collective-permute-start.7 = (f32[8,256]{1,0:T(8,128)S(1)}, f32[8,256]{1,0:T(8,128)S(1)}, u32[]{:S(2)}, u32[]{:S(2)}) collective-permute-start(f32[8,256]{1,0:T(8,128)S(1)} %get-tuple-element.33), channel_id=1, source_target_pairs={{0,12},{4,8},{8,4},{12,0},{1,13},{5,9},{9,5},{13,1},{2,14},{6,10},... | collective-permute-start | bytes 24584 | tf_op jit(solution)/shard_map/ppermute | solution.py:601
  21.8 0.6 %collective-permute-start.8 = (f32[8,256]{1,0:T(8,128)S(1)}, f32[8,256]{1,0:T(8,128)S(1)}, u32[]{:S(2)}, u32[]{:S(2)}) collective-permute-start(f32[8,256]{1,0:T(8,128)S(1)} %get-tuple-element.34), channel_id=1, source_target_pairs={{0,8},{4,12},{8,0},{12,4},{1,9},{5,13},{9,1},{13,5},{2,10},{6,14},... | collective-permute-start | bytes 24584 | tf_op jit(solution)/shard_map/ppermute | solution.py:601
  22.4 2.0 %collective-permute-start.9 = (f32[8,256]{1,0:T(8,128)S(1)}, f32[8,256]{1,0:T(8,128)S(1)}, u32[]{:S(2)}, u32[]{:S(2)}) collective-permute-start(f32[8,256]{1,0:T(8,128)S(1)} %get-tuple-element.35), channel_id=1, source_target_pairs={{0,4},{4,0},{8,12},{12,8},{1,5},{5,1},{9,13},{13,9},{2,6},{6,2},{1... | collective-permute-start | bytes 24584 | tf_op jit(solution)/shard_map/ppermute | solution.py:601
  24.4 1.1 %collective-permute-done.7.refs_0_ = f32[8,256]{1,0:T(8,128)S(1)} collective-permute-done((f32[8,256]{1,0:T(8,128)S(1)}, f32[8,256]{1,0:T(8,128)S(1)}, u32[]{:S(2)}, u32[]{:S(2)}) %collective-permute-start.7) | collective-permute-done | bytes 8224 | tf_op jit(solution)/shard_map/ppermute | solution.py:601
  25.5 0.9 %collective-permute-done.8.refs_1_ = f32[8,256]{1,0:T(8,128)S(1)} collective-permute-done((f32[8,256]{1,0:T(8,128)S(1)}, f32[8,256]{1,0:T(8,128)S(1)}, u32[]{:S(2)}, u32[]{:S(2)}) %collective-permute-start.8) | collective-permute-done | bytes 8224 | tf_op jit(solution)/shard_map/ppermute | solution.py:601
  26.4 0.0 collective-permute-done.9.refs_2_
  26.4 0.7 %shard_map.51 = f32[2,8,8,128]{3,2,1,0:T(8,128)} custom-call(f32[8,256]{1,0:T(8,128)S(1)} %collective-permute-done.7.refs_0_, f32[8,256]{1,0:T(8,128)S(1)} %collective-permute-done.8.refs_1_, f32[8,256]{1,0:T(8,128)S(1)} %collective-permute-done.9.refs_2_, f32[8,256]{1,0:T(8,128)S(1)} %get-tuple-element.36.refs_3_), custom_call_target="tpu_custom_call" | custom-call | tf_op jit(solution)/shard_map/pallas_call | solution.py:634
Async XLA Ops:
  1.2 6.4 %collective-permute-start.3 = (bf16[2,16,2560]{2,1,0:T(8,128)(2,1)S(1)}, bf16[2,16,2560]{2,1,0:T(8,128)(2,1)S(1)}, u32[]{:S(2)}, u32[]{:S(2)}) collective-permute-start(bf16[2,16,2560]{2,1,0:T(8,128)(2,1)S(1)} %get-tuple-element.28), channel_id=1, source_target_pairs={{0,1},{1,0},{2,3},{3,2},{4,5},{5,4},{6,7},{7,6},{8,9},{9,8},{10,11... | collective-permute-start | bytes 491528 | tf_op jit(solution)/shard_map/ppermute | solution.py:574
  1.7 5.9 %collective-permute-start.1 = (bf16[2,32,128]{2,1,0:T(8,128)(2,1)S(1)}, bf16[2,32,128]{2,1,0:T(8,128)(2,1)S(1)}, u32[]{:S(2)}, u32[]{:S(2)}) collective-permute-start(bf16[2,32,128]{2,1,0:T(8,128)(2,1)S(1)} %get-tuple-element.26), channel_id=1, source_target_pairs={{0,2},{2,0},{1,3},{3,1},{4,6},{6,4},{5,7},{7,5},{8,10},{10,8},{9,1... | collective-permute-start | bytes 49160 | tf_op jit(solution)/shard_map/ppermute | solution.py:572
  4.3 3.3 %collective-permute-start.2 = (bf16[2,16,128]{2,1,0:T(8,128)(2,1)S(1)}, bf16[2,16,128]{2,1,0:T(8,128)(2,1)S(1)}, u32[]{:S(2)}, u32[]{:S(2)}) collective-permute-start(bf16[2,16,128]{2,1,0:T(8,128)(2,1)S(1)} %get-tuple-element.27), channel_id=1, source_target_pairs={{0,3},{1,2},{2,1},{3,0},{4,7},{5,6},{6,5},{7,4},{8,11},{9,10},{10,... | collective-permute-start | bytes 24584 | tf_op jit(solution)/shard_map/ppermute | solution.py:573
  4.7 8.5 %collective-permute-start = (bf16[128,128]{1,0:T(8,128)(2,1)S(1)}, bf16[128,128]{1,0:T(8,128)(2,1)S(1)}, u32[]{:S(2)}, u32[]{:S(2)}) collective-permute-start(bf16[128,128]{1,0:T(8,128)(2,1)S(1)} %shard_map.47), channel_id=1, source_target_pairs={{0,8},{4,12},{8,0},{12,4},{1,9},{5,13},{9,1},{13,5},{2,10},{6,14},... | collective-permute-start | bytes 98312 | tf_op jit(solution)/shard_map/ppermute | solution.py:584
  8.8 9.1 %collective-permute-start.5 = (bf16[336,128]{1,0:T(8,128)(2,1)S(1)}, bf16[336,128]{1,0:T(8,128)(2,1)S(1)}, u32[]{:S(2)}, u32[]{:S(2)}) collective-permute-start(bf16[336,128]{1,0:T(8,128)(2,1)S(1)} %get-tuple-element.30), channel_id=1, source_target_pairs={{0,12},{4,8},{8,4},{12,0},{1,13},{5,9},{9,5},{13,1},{2,14},{6,10},... | collective-permute-start | bytes 258056 | tf_op jit(solution)/shard_map/ppermute | solution.py:601
  12.2 6.1 %collective-permute-start.6 = (bf16[336,128]{1,0:T(8,128)(2,1)S(1)}, bf16[336,128]{1,0:T(8,128)(2,1)S(1)}, u32[]{:S(2)}, u32[]{:S(2)}) collective-permute-start(bf16[336,128]{1,0:T(8,128)(2,1)S(1)} %get-tuple-element.31), channel_id=1, source_target_pairs={{0,4},{4,0},{8,12},{12,8},{1,5},{5,1},{9,13},{13,9},{2,6},{6,2},{1... | collective-permute-start | bytes 258056 | tf_op jit(solution)/shard_map/ppermute | solution.py:601
  12.2 5.7 %collective-permute-start.4 = (bf16[208,128]{1,0:T(8,128)(2,1)S(1)}, bf16[208,128]{1,0:T(8,128)(2,1)S(1)}, u32[]{:S(2)}, u32[]{:S(2)}) collective-permute-start(bf16[208,128]{1,0:T(8,128)(2,1)S(1)} %get-tuple-element.29), channel_id=1, source_target_pairs={{0,8},{4,12},{8,0},{12,4},{1,9},{5,13},{9,1},{13,5},{2,10},{6,14},... | collective-permute-start | bytes 159752 | tf_op jit(solution)/shard_map/ppermute | solution.py:601
  20.0 5.5 %collective-permute-start.7 = (f32[8,256]{1,0:T(8,128)S(1)}, f32[8,256]{1,0:T(8,128)S(1)}, u32[]{:S(2)}, u32[]{:S(2)}) collective-permute-start(f32[8,256]{1,0:T(8,128)S(1)} %get-tuple-element.33), channel_id=1, source_target_pairs={{0,12},{4,8},{8,4},{12,0},{1,13},{5,9},{9,5},{13,1},{2,14},{6,10},... | collective-permute-start | bytes 24584 | tf_op jit(solution)/shard_map/ppermute | solution.py:601
  21.8 4.5 %collective-permute-start.8 = (f32[8,256]{1,0:T(8,128)S(1)}, f32[8,256]{1,0:T(8,128)S(1)}, u32[]{:S(2)}, u32[]{:S(2)}) collective-permute-start(f32[8,256]{1,0:T(8,128)S(1)} %get-tuple-element.34), channel_id=1, source_target_pairs={{0,8},{4,12},{8,0},{12,4},{1,9},{5,13},{9,1},{13,5},{2,10},{6,14},... | collective-permute-start | bytes 24584 | tf_op jit(solution)/shard_map/ppermute | solution.py:601
  22.4 3.9 %collective-permute-start.9 = (f32[8,256]{1,0:T(8,128)S(1)}, f32[8,256]{1,0:T(8,128)S(1)}, u32[]{:S(2)}, u32[]{:S(2)}) collective-permute-start(f32[8,256]{1,0:T(8,128)S(1)} %get-tuple-element.35), channel_id=1, source_target_pairs={{0,4},{4,0},{8,12},{12,8},{1,5},{5,1},{9,13},{13,9},{2,6},{6,2},{1... | collective-permute-start | bytes 24584 | tf_op jit(solution)/shard_map/ppermute | solution.py:601

commit v3 on v2

--- a/solution.py
+++ b/solution.py
@@ -348,27 +348,34 @@
         copy.wait()
 
 
-def along_range(moved, column_ref, tiles):
-    high, low = halves(moved)
+def along_range(blocks, column_ref, tiles):
+    blocks = [halves(moved) for moved in blocks]
     starts = range(0, tiles * LANES, LANES)
-    high = jnp.concatenate([high[:, s : s + 3 * LANES] for s in starts], axis=0)
-    low = jnp.concatenate([low[:, s : s + 3 * LANES] for s in starts], axis=0)
+    high = jnp.concatenate([high[:, s : s + 3 * LANES] for high, _ in blocks for s in starts], axis=0)
+    low = jnp.concatenate([low[:, s : s + 3 * LANES] for _, low in blocks for s in starts], axis=0)
     total = dot(high, column_ref[...])
     return total[:, :LANES] + total[:, LANES:] + dot(low, column_ref[:, :LANES])
 
 
-def early_kernel(tiles, held_ref, line_ref, column_ref, out_ref):
+def early_kernel(tiles, steps, held_ref, line_ref, column_ref, *outs):
     lines = held_ref.shape[1]
-    early = out_ref.shape[0] // (2 * HALO_LINES)
-    dates = lax.axis_size("date")
-    chunk = lax.axis_index("date") ^ reach(dates - 1, dates)
-    begin = pl.multiple_of((chunk * tiles + lax.axis_index("rng")) * LANES, LANES)
+    early = tiles - 1
     moved = []
-    for plane in range(2):
-        both = dot(line_ref[0, :, :lines], held_ref[plane, :, pl.ds(begin, (early + 2) * LANES)])
-        moved.append(both[:HALO_LINES] + both[HALO_LINES:])
-    moved = jnp.concatenate(moved, axis=0)
-    out_ref[...] = along_range(moved, column_ref, early).astype(jnp.bfloat16)
+    for step in steps:
+        chunk = lax.axis_index("date") ^ reach(step, lax.axis_size("date"))
+        begin = pl.multiple_of((chunk * tiles + lax.axis_index("rng")) * LANES, LANES)
+        moved += [held_ref[plane, :, pl.ds(begin, (early + 2) * LANES)] for plane in range(2)]
+    both = dot(line_ref[0, :, :lines], jnp.concatenate(moved, axis=1))
+    both = both[:HALO_LINES] + both[HALO_LINES:]
+    width = (early + 2) * LANES
+    moved = [
+        jnp.concatenate([both[:, (2 * i + plane) * width : (2 * i + plane + 1) * width] for plane in range(2)], axis=0)
+        for i in range(len(outs))
+    ]
+    total = along_range(moved, column_ref, early).astype(jnp.bfloat16)
+    rows = early * lines
+    for i, out_ref in enumerate(outs):
+        out_ref[...] = total[i * rows : (i + 1) * rows]
 
 
 def resample_kernel(side_ref, corner_ref, lines_ref, held_ref, line_ref, column_ref, *outs):
@@ -389,7 +396,7 @@
     left = jnp.where(block > 0, moved[:, :LANES], 0.0)
     right = jnp.where(block == 0, moved[:, width - LANES :], 0.0)
     moved = jnp.concatenate([left, moved[:, LANES : width - LANES], right, jnp.zeros_like(right)], axis=1)
-    total = along_range(moved, column_ref, width // LANES - 1)
+    total = along_range([moved], column_ref, width // LANES - 1)
     rows = 2 * lines
     tiles_ref[...] = total.astype(jnp.bfloat16)
     chunk_rows = outs[0].shape[0] - FOLD
@@ -402,29 +409,32 @@
             folded = jnp.where(lane == part, value, folded)
         tails_ref[chunk] = folded.astype(jnp.bfloat16)
     date = lax.axis_index("date")
-    for step, out_ref in enumerate(outs[:-1]):
+    early = chunk_rows // rows - 1
+    for step, out_ref in enumerate(outs):
         chunk = date ^ reach(step, len(outs))
-        out_ref[:chunk_rows] = tiles_ref[pl.ds(pl.multiple_of(chunk * chunk_rows, FOLD), chunk_rows), :]
-        out_ref[chunk_rows:] = tails_ref[chunk]
-    out_ref = outs[-1]
-    chunk = date ^ reach(len(outs) - 1, len(outs))
-    early = chunk_rows // rows - 1
-    for tile in range(early):
-        begin = pl.multiple_of(chunk * chunk_rows + (tile + block) * rows + lines, FOLD)
-        out_ref[tile * lines : (tile + 1) * lines] = tiles_ref[pl.ds(begin, lines), :]
-    begin = pl.multiple_of(chunk * chunk_rows + (1 - block) * early * rows, FOLD)
-    out_ref[early * lines : early * lines + rows] = tiles_ref[pl.ds(begin, rows), :]
-    out_ref[early * lines + rows :] = tails_ref[chunk]
-
-
-def filter_kernel(pairs, shift_hbm, early_ref, out_ref, spread_ref, shift_ref, semaphore):
+        if out_ref.shape[0] == outs[0].shape[0]:
+            out_ref[:chunk_rows] = tiles_ref[pl.ds(pl.multiple_of(chunk * chunk_rows, FOLD), chunk_rows), :]
+            out_ref[chunk_rows:] = tails_ref[chunk]
+            continue
+        for tile in range(early):
+            begin = pl.multiple_of(chunk * chunk_rows + (tile + block) * rows + lines, FOLD)
+            out_ref[tile * lines : (tile + 1) * lines] = tiles_ref[pl.ds(begin, lines), :]
+        begin = pl.multiple_of(chunk * chunk_rows + (1 - block) * early * rows, FOLD)
+        out_ref[early * lines : early * lines + rows] = tiles_ref[pl.ds(begin, rows), :]
+        out_ref[early * lines + rows :] = tails_ref[chunk]
+
+
+def filter_kernel(pairs, shift_hbm, *refs):
+    count = (len(refs) - 3) // 2
+    earlies, out_ref, spreads, (shift_ref, semaphore) = refs[:count], refs[count], refs[count + 1 : -2], refs[-2:]
     copy = pltpu.make_async_copy(shift_hbm, shift_ref, semaphore)
     copy.start()
     lines = 2 * HALO_LINES
-    spread_ref[...] = jnp.zeros_like(spread_ref)
-    for tile in range(early_ref.shape[0] // lines):
-        begin = pl.multiple_of((tile + lax.axis_index("rng")) * 2 * lines, FOLD)
-        spread_ref[pl.ds(begin, lines), :] = early_ref[tile * lines : (tile + 1) * lines]
+    for early_ref, spread_ref in zip(earlies, spreads):
+        spread_ref[...] = jnp.zeros_like(spread_ref)
+        for tile in range(early_ref.shape[0] // lines):
+            begin = pl.multiple_of((tile + lax.axis_index("rng")) * 2 * lines, FOLD)
+            spread_ref[pl.ds(begin, lines), :] = early_ref[tile * lines : (tile + 1) * lines]
     date = lax.axis_index("date")
     spacing = lax.broadcasted_iota(jnp.int32, (1, 2 * LANES), 1).astype(jnp.float32) - FILTER_HALF
     window = 0.4 * sinc(0.4 * spacing) * (0.54 + 0.46 * jnp.cos(jnp.pi * spacing / (FILTER_HALF + 1)))
@@ -443,8 +453,9 @@
 
 
 def looks_kernel(pairs, dates, weight_ref, *refs):
-    early_ref, chunks, outs = refs[0], list(refs[1 : dates + 1][::-1]), refs[dates + 1 : 2 * dates + 1]
-    whole_ref, window_ref, product_ref = refs[-3:]
+    far = dates - 2
+    earlies, chunks = refs[:far], list(refs[far : far + dates][::-1])
+    outs, (whole_ref, window_ref, product_ref) = refs[far + dates : -3], refs[-3:]
     groups, lines = outs[0].shape[0], outs[0].shape[0] * LOOK_AZ
     rows = 2 * lines
     blocks = (chunks[0].shape[0] - FOLD) // rows
@@ -452,14 +463,16 @@
     date = lax.axis_index("date")
     block = lax.axis_index("rng")
     early = blocks - 1
-    whole_ref[: blocks * rows] = early_ref[...]
-    for tile in range(early):
-        begin = pl.multiple_of((tile + block) * rows, FOLD)
-        whole_ref[pl.ds(begin + lines, lines), :] = chunks[-1][tile * lines : (tile + 1) * lines]
-    begin = pl.multiple_of((1 - block) * early * rows, FOLD)
-    whole_ref[pl.ds(begin, rows), :] = chunks[-1][early * lines : early * lines + rows]
-    whole_ref[blocks * rows :] = chunks[-1][early * lines + rows :]
-    chunks[-1] = whole_ref
+    for i, early_ref in enumerate(earlies):
+        whole, rest_ref = whole_ref.at[i], chunks[dates - 1 - i]
+        whole[: blocks * rows] = early_ref[...]
+        for tile in range(early):
+            begin = pl.multiple_of((tile + block) * rows, FOLD)
+            whole[pl.ds(begin + lines, lines), :] = rest_ref[tile * lines : (tile + 1) * lines]
+        begin = pl.multiple_of((1 - block) * early * rows, FOLD)
+        whole[pl.ds(begin, rows), :] = rest_ref[early * lines : early * lines + rows]
+        whole[blocks * rows :] = rest_ref[early * lines + rows :]
+        chunks[dates - 1 - i] = whole
     az = lax.axis_index("az")
     upper = lax.broadcasted_iota(jnp.int32, (groups, LANES), 0) // (groups // 2) == az
     for step, chunk_ref in enumerate(chunks):
@@ -573,16 +586,20 @@
     corner = lax.ppermute(corner, ("rng", "az"), [(0, 3), (1, 2), (2, 1), (3, 0)])
     halo_lines = lax.ppermute(halo_lines, "az", swap)
 
+    steps = range(dates - 1, 0, -1)
+    far = dates - 2
     early_rows = (tiles - 1) * lines
     early = pl.pallas_call(
-        functools.partial(early_kernel, tiles),
-        out_shape=jax.ShapeDtypeStruct((early_rows, LANES), bf16),
+        functools.partial(early_kernel, tiles, steps[:far]),
+        out_shape=[jax.ShapeDtypeStruct((early_rows, LANES), bf16)] * far,
         in_specs=[vmem] * 3,
-        out_specs=vmem,
+        out_specs=[vmem] * far,
         compiler_params=limit,
     )(held, line_taps, column_taps)
-    early = lax.ppermute(early, "date", [(i, i ^ reach(dates - 1, dates)) for i in range(dates)])
-    out_rows = [chunk_rows + FOLD] * (dates - 1) + [chunk_rows + FOLD - early_rows]
+    early = [
+        lax.ppermute(rows, "date", [(i, i ^ reach(step, dates)) for i in range(dates)]) for rows, step in zip(early, steps)
+    ]
+    out_rows = [chunk_rows + FOLD] * 2 + [chunk_rows + FOLD - early_rows] * far
     sent = pl.pallas_call(
         resample_kernel,
         out_shape=[jax.ShapeDtypeStruct((rows, LANES), bf16) for rows in out_rows],
@@ -593,6 +610,7 @@
             pltpu.VMEM((dates, FOLD, LANES), bf16),
         ],
         compiler_params=limit,
+        cost_estimate=pl.CostEstimate(flops=700_000_000, bytes_accessed=0, transcendentals=0),
     )(side, corner, halo_lines, held, line_taps, column_taps)
 
     def exchanged(values, order):
@@ -601,34 +619,32 @@
             arrived[step] = lax.ppermute(values[step], "date", [(i, i ^ reach(step, dates)) for i in range(dates)])
         return [arrived[step] for step in reversed(range(dates))]
 
-    steps = range(dates - 1, 0, -1)
-
     chunks = exchanged(sent, steps)
     pairs = [(first, second) for first in range(dates) for second in range(first + 1, dates)]
-    weights, early = pl.pallas_call(
+    weights, *early = pl.pallas_call(
         functools.partial(filter_kernel, pairs),
         out_shape=[
             jax.ShapeDtypeStruct((len(pairs), 2 * LANES, 4 * LANES), bf16),
-            jax.ShapeDtypeStruct((chunk_rows, LANES), bf16),
-        ],
-        in_specs=[hbm, vmem],
-        out_specs=[vmem] * 2,
+        ]
+        + [jax.ShapeDtypeStruct((chunk_rows, LANES), bf16)] * far,
+        in_specs=[hbm] + [vmem] * far,
+        out_specs=[vmem] * (1 + far),
         scratch_shapes=[pltpu.SMEM(range_shift.shape, jnp.float32), pltpu.SemaphoreType.DMA],
         compiler_params=limit,
-        cost_estimate=pl.CostEstimate(flops=600_000_000, bytes_accessed=0, transcendentals=0),
-    )(range_shift, early)
+        cost_estimate=pl.CostEstimate(flops=1_000_000_000, bytes_accessed=0, transcendentals=0),
+    )(range_shift, *early)
     looked = pl.pallas_call(
         functools.partial(looks_kernel, pairs, dates),
         out_shape=[jax.ShapeDtypeStruct((groups, out_width), jnp.float32)] * dates,
-        in_specs=[vmem] * (2 + dates),
+        in_specs=[vmem] * (1 + far + dates),
         out_specs=[vmem] * dates,
         scratch_shapes=[
-            pltpu.VMEM((chunk_rows + FOLD, LANES), bf16),
+            pltpu.VMEM((far, chunk_rows + FOLD, LANES), bf16),
             pltpu.VMEM((dates, chunk_rows, 2 * LANES), bf16),
             pltpu.VMEM((len(pairs) * 2 * groups, chunk), jnp.float32),
         ],
         compiler_params=limit,
-    )(weights, early, *chunks)
+    )(weights, *early, *chunks)
     returned = exchanged(looked, steps)[::-1]
     returned = [returned[reach(distance, dates)] for distance in reversed(range(dates))]
     out = pl.pallas_call(

time: 27.2 us -> 28 us (1.029)
  starting transfers between devices: 14.9 us -> 15.4 us
    ppermute x1 -> x2, starting transfers between devices: 2.89 us -> 4.24 us  [tiled_body(): lax.ppermute(rows, 'date', [(i, i ^ reach(step, dates)) for i in range(da...]
    ppermute x6, starting transfers between devices: 8.88 us -> 7.98 us  [exchanged(): lax.ppermute(values[step], 'date', [(i, i ^ reach(step, dates)) for i in...]
  transfers between devices with their start and end apart: 10 -> 11, of which waited for: 4 -> 5; matrix products, arithmetic and copies ran while one was open for 0% -> 0% of each run, Pallas kernels for 10% -> 10%
where the time goes in v3:
time: 28 us; the launch traced here: 27.8 us
  starting transfers between devices  15.4 us (55%)
  Pallas kernels  6.37 us (23%)
  waiting for transfers between devices  6.04 us (22%)
    ppermute x6, starting transfers between devices, exchanged(): lax.ppermute(values[step], 'date', [(i, i ^ reach(step, dates)) for i in...  7.98 us
    ppermute x6, waiting for transfers between devices, exchanged(): lax.ppermute(values[step], 'date', [(i, i ^ reach(step, dates)) for i in...  6.03 us
    ppermute x2, starting transfers between devices, tiled_body(): lax.ppermute(rows, 'date', [(i, i ^ reach(step, dates)) for i in range(da...  4.24 us
    ppermute x1, starting transfers between devices, tiled_body(): side = lax.ppermute(side, 'rng', swap)  2.56 us
    pallas_call x1, Pallas kernels, tiled_body(): pl.pallas_call(functools.partial(looks_kernel, pairs, dates), out_shape=[...  1.58 us
    pallas_call x1, Pallas kernels, tiled_body(): pl.pallas_call(functools.partial(filter_kernel, pairs), out_shape=[jax.Sh...  1.23 us
    pallas_call x1, Pallas kernels, tiled_body(): pl.pallas_call(prepare_kernel, out_shape=[jax.ShapeDtypeStruct((2, lines,...  1.2 us
    pallas_call x1, Pallas kernels, tiled_body(): pl.pallas_call(resample_kernel, out_shape=[jax.ShapeDtypeStruct((rows, LA...  1.2 us
  transfers between devices with their start and end apart: 11, of which 5 were waited for; matrix products, arithmetic and copies ran while one was open for 0% of the time, Pallas kernels for 10%

profile of v3, /device:TPU:0, one launch (start us, length us, event | category | flops | bytes accessed | tf_op | source)
XLA Modules:
  0.0 27.8 jit_solution(3754003910886213901)
XLA Ops:
  0.0 1.2 %shard_map.46 = (bf16[2,32,128]{2,1,0:T(8,128)(2,1)S(1)}, bf16[2,16,128]{2,1,0:T(8,128)(2,1)S(1)}, bf16[2,16,2560]{2,1,0:T(8,128)(2,1)S(1)}, bf16[2,32,48]{2,1,0...) custom-call(s32[1,2]{1,0:T(1,128)} %offsets_hbm.1, s32[1,2]{1,0:T(1,128)} %index_hbm.1, ...), custom_call_target="tpu_custom_call" | custom-call | tf_op jit(solution)/shard_map/pallas_call | solution.py:565
  1.2 0.5 %collective-permute-start.4 = (bf16[2,16,2560]{2,1,0:T(8,128)(2,1)S(1)}, bf16[2,16,2560]{2,1,0:T(8,128)(2,1)S(1)}, u32[]{:S(2)}, u32[]{:S(2)}) collective-permute-start(bf16[2,16,2560]{2,1,0:T(8,128)(2,1)S(1)} %get-tuple-element.34), channel_id=1, source_target_pairs={{0,1},{1,0},{2,3},{3,2},{4,5},{5,4},{6,7},{7,6},{8,9},{9,8},{10,11... | collective-permute-start | bytes 491528 | tf_op jit(solution)/shard_map/ppermute | solution.py:587
  1.7 2.6 %collective-permute-start.2 = (bf16[2,32,128]{2,1,0:T(8,128)(2,1)S(1)}, bf16[2,32,128]{2,1,0:T(8,128)(2,1)S(1)}, u32[]{:S(2)}, u32[]{:S(2)}) collective-permute-start(bf16[2,32,128]{2,1,0:T(8,128)(2,1)S(1)} %get-tuple-element.32), channel_id=1, source_target_pairs={{0,2},{2,0},{1,3},{3,1},{4,6},{6,4},{5,7},{7,5},{8,10},{10,8},{9,1... | collective-permute-start | bytes 49160 | tf_op jit(solution)/shard_map/ppermute | solution.py:585
  4.3 0.1 collective-permute-start.3
  4.4 0.4 %shard_map.47 = (bf16[128,128]{1,0:T(8,128)(2,1)S(1)}, bf16[128,128]{1,0:T(8,128)(2,1)S(1)}) custom-call(bf16[2,32,2944]{2,1,0:T(8,128)(2,1)S(1)} %get-tuple-element.24.held_ref, bf16[2,32,48]{2,1,0:T(8,128)(2,1)S(1)} %get-tuple-element.25.line_ref, bf16[384,256]{1,0:T(8,128)(2,1)S(1)} %get-tuple-element.26.column_ref), custom_call_target="tpu_custom_call" | custom-call | tf_op jit(solution)/shard_map/pallas_call | solution.py:592
  4.8 2.9 %collective-permute-start = (bf16[128,128]{1,0:T(8,128)(2,1)S(1)}, bf16[128,128]{1,0:T(8,128)(2,1)S(1)}, u32[]{:S(2)}, u32[]{:S(2)}) collective-permute-start(bf16[128,128]{1,0:T(8,128)(2,1)S(1)} %get-tuple-element.27), channel_id=1, source_target_pairs={{0,8},{4,12},{8,0},{12,4},{1,9},{5,13},{9,1},{13,5},{2,10},{6,14},... | collective-permute-start | bytes 98312 | tf_op jit(solution)/shard_map/ppermute | solution.py:600
  7.7 1.3 %collective-permute-start.1 = (bf16[128,128]{1,0:T(8,128)(2,1)S(1)}, bf16[128,128]{1,0:T(8,128)(2,1)S(1)}, u32[]{:S(2)}, u32[]{:S(2)}) collective-permute-start(bf16[128,128]{1,0:T(8,128)(2,1)S(1)} %get-tuple-element.28), channel_id=1, source_target_pairs={{0,12},{4,8},{8,4},{12,0},{1,13},{5,9},{9,5},{13,1},{2,14},{6,10},... | collective-permute-start | bytes 98312 | tf_op jit(solution)/shard_map/ppermute | solution.py:600
  9.0 0.0 collective-permute-done.3.corner_ref
  9.0 0.0 collective-permute-done.2.side_ref
  9.0 0.0 collective-permute-done.4.lines_ref
  9.1 1.2 %shard_map.49 = (bf16[336,128]{1,0:T(8,128)(2,1)S(1)}, bf16[336,128]{1,0:T(8,128)(2,1)S(1)}, bf16[208,128]{1,0:T(8,128)(2,1)S(1)}, bf16[208,128]{1,0:T(8,128)(2,1)S(1)}) custom-call(bf16[2,32,128]{2,1,0:T(8,128)(2,1)S(1)} %collective-permute-done.2.side_ref, bf16[2,16,128]{2,1,0:T(8,128)(2,1)S(1)} %collective-permute-done.3.corner_ref, ...), custom_call_target="tpu_custom_call" | custom-call | flops 700000000 | tf_op jit(solution)/shard_map/pallas_call | solution.py:603
  10.3 1.7 %collective-permute-start.5 = (bf16[208,128]{1,0:T(8,128)(2,1)S(1)}, bf16[208,128]{1,0:T(8,128)(2,1)S(1)}, u32[]{:S(2)}, u32[]{:S(2)}) collective-permute-start(bf16[208,128]{1,0:T(8,128)(2,1)S(1)} %get-tuple-element.35), channel_id=1, source_target_pairs={{0,8},{4,12},{8,0},{12,4},{1,9},{5,13},{9,1},{13,5},{2,10},{6,14},... | collective-permute-start | bytes 159752 | tf_op jit(solution)/shard_map/ppermute | solution.py:619
  12.0 0.9 %collective-permute-start.6 = (bf16[208,128]{1,0:T(8,128)(2,1)S(1)}, bf16[208,128]{1,0:T(8,128)(2,1)S(1)}, u32[]{:S(2)}, u32[]{:S(2)}) collective-permute-start(bf16[208,128]{1,0:T(8,128)(2,1)S(1)} %get-tuple-element.36), channel_id=1, source_target_pairs={{0,12},{4,8},{8,4},{12,0},{1,13},{5,9},{9,5},{13,1},{2,14},{6,10},... | collective-permute-start | bytes 159752 | tf_op jit(solution)/shard_map/ppermute | solution.py:619
  12.9 0.9 %collective-permute-start.7 = (bf16[336,128]{1,0:T(8,128)(2,1)S(1)}, bf16[336,128]{1,0:T(8,128)(2,1)S(1)}, u32[]{:S(2)}, u32[]{:S(2)}) collective-permute-start(bf16[336,128]{1,0:T(8,128)(2,1)S(1)} %get-tuple-element.37), channel_id=1, source_target_pairs={{0,4},{4,0},{8,12},{12,8},{1,5},{5,1},{9,13},{13,9},{2,6},{6,2},{1... | collective-permute-start | bytes 258056 | tf_op jit(solution)/shard_map/ppermute | solution.py:619
  13.8 0.0 collective-permute-done.refs_0_
  13.8 0.0 collective-permute-done.1.refs_1_
  13.8 1.2 %shard_map.48 = (bf16[6,256,512]{2,1,0:T(8,128)(2,1)S(1)}, bf16[320,128]{1,0:T(8,128)(2,1)S(1)}, bf16[320,128]{1,0:T(8,128)(2,1)S(1)}) custom-call(f32[4]{0:T(128)} %shift_hbm.1, bf16[128,128]{1,0:T(8,128)(2,1)S(1)} %collective-permute-done.refs_0_, bf16[128,128]{1,0:T(8,128)(2,1)S(1)} %collective-permute-done.1.refs_1_), custom_call_target="tpu_custom_call" | custom-call | flops 1000000000 | tf_op jit(solution)/shard_map/pallas_call | solution.py:624
  15.0 1.7 %collective-permute-done.5.refs_2_ = bf16[208,128]{1,0:T(8,128)(2,1)S(1)} collective-permute-done((bf16[208,128]{1,0:T(8,128)(2,1)S(1)}, bf16[208,128]{1,0:T(8,128)(2,1)S(1)}, u32[]{:S(2)}, u32[]{:S(2)}) %collective-permute-start.5) | collective-permute-done | bytes 53280 | tf_op jit(solution)/shard_map/ppermute | solution.py:619
  16.7 1.4 %collective-permute-done.6.refs_3_ = bf16[208,128]{1,0:T(8,128)(2,1)S(1)} collective-permute-done((bf16[208,128]{1,0:T(8,128)(2,1)S(1)}, bf16[208,128]{1,0:T(8,128)(2,1)S(1)}, u32[]{:S(2)}, u32[]{:S(2)}) %collective-permute-start.6) | collective-permute-done | bytes 53280 | tf_op jit(solution)/shard_map/ppermute | solution.py:619
  18.1 0.7 %collective-permute-done.7.refs_4_ = bf16[336,128]{1,0:T(8,128)(2,1)S(1)} collective-permute-done((bf16[336,128]{1,0:T(8,128)(2,1)S(1)}, bf16[336,128]{1,0:T(8,128)(2,1)S(1)}, u32[]{:S(2)}, u32[]{:S(2)}) %collective-permute-start.7) | collective-permute-done | bytes 86048 | tf_op jit(solution)/shard_map/ppermute | solution.py:619
  18.8 1.6 %shard_map.50 = (f32[8,256]{1,0:T(8,128)S(1)}, f32[8,256]{1,0:T(8,128)S(1)}, f32[8,256]{1,0:T(8,128)S(1)}, f32[8,256]{1,0:T(8,128)S(1)}) custom-call(bf16[6,256,512]{2,1,0:T(8,128)(2,1)S(1)} %get-tuple-element.29.weight_ref, bf16[320,128]{1,0:T(8,128)(2,1)S(1)} %get-tuple-element.30.refs_0_, bf16[320,128]{1,0:T(8,128)(2,1)S(1)} %get-tuple-element.31.refs_1_, ...), custom_call_target="tpu_custom_call" | custom-call | tf_op jit(solution)/shard_map/pallas_call | solution.py:636
  20.4 2.2 %collective-permute-start.8 = (f32[8,256]{1,0:T(8,128)S(1)}, f32[8,256]{1,0:T(8,128)S(1)}, u32[]{:S(2)}, u32[]{:S(2)}) collective-permute-start(f32[8,256]{1,0:T(8,128)S(1)} %get-tuple-element.39), channel_id=1, source_target_pairs={{0,12},{4,8},{8,4},{12,0},{1,13},{5,9},{9,5},{13,1},{2,14},{6,10},... | collective-permute-start | bytes 24584 | tf_op jit(solution)/shard_map/ppermute | solution.py:619
  22.5 0.0 collective-permute-start.9
  22.5 2.3 %collective-permute-start.10 = (f32[8,256]{1,0:T(8,128)S(1)}, f32[8,256]{1,0:T(8,128)S(1)}, u32[]{:S(2)}, u32[]{:S(2)}) collective-permute-start(f32[8,256]{1,0:T(8,128)S(1)} %get-tuple-element.41), channel_id=1, source_target_pairs={{0,4},{4,0},{8,12},{12,8},{1,5},{5,1},{9,13},{13,9},{2,6},{6,2},{1... | collective-permute-start | bytes 24584 | tf_op jit(solution)/shard_map/ppermute | solution.py:619
  24.8 1.1 %collective-permute-done.8.refs_0_ = f32[8,256]{1,0:T(8,128)S(1)} collective-permute-done((f32[8,256]{1,0:T(8,128)S(1)}, f32[8,256]{1,0:T(8,128)S(1)}, u32[]{:S(2)}, u32[]{:S(2)}) %collective-permute-start.8) | collective-permute-done | bytes 8224 | tf_op jit(solution)/shard_map/ppermute | solution.py:619
  25.9 1.2 %collective-permute-done.9.refs_1_ = f32[8,256]{1,0:T(8,128)S(1)} collective-permute-done((f32[8,256]{1,0:T(8,128)S(1)}, f32[8,256]{1,0:T(8,128)S(1)}, u32[]{:S(2)}, u32[]{:S(2)}) %collective-permute-start.9) | collective-permute-done | bytes 8224 | tf_op jit(solution)/shard_map/ppermute | solution.py:619
  27.1 0.0 collective-permute-done.10.refs_2_
  27.1 0.7 %shard_map.51 = f32[2,8,8,128]{3,2,1,0:T(8,128)} custom-call(f32[8,256]{1,0:T(8,128)S(1)} %collective-permute-done.8.refs_0_, f32[8,256]{1,0:T(8,128)S(1)} %collective-permute-done.9.refs_1_, f32[8,256]{1,0:T(8,128)S(1)} %collective-permute-done.10.refs_2_, f32[8,256]{1,0:T(8,128)S(1)} %get-tuple-element.42.refs_3_), custom_call_target="tpu_custom_call" | custom-call | tf_op jit(solution)/shard_map/pallas_call | solution.py:650
Async XLA Ops:
  1.2 7.8 %collective-permute-start.4 = (bf16[2,16,2560]{2,1,0:T(8,128)(2,1)S(1)}, bf16[2,16,2560]{2,1,0:T(8,128)(2,1)S(1)}, u32[]{:S(2)}, u32[]{:S(2)}) collective-permute-start(bf16[2,16,2560]{2,1,0:T(8,128)(2,1)S(1)} %get-tuple-element.34), channel_id=1, source_target_pairs={{0,1},{1,0},{2,3},{3,2},{4,5},{5,4},{6,7},{7,6},{8,9},{9,8},{10,11... | collective-permute-start | bytes 491528 | tf_op jit(solution)/shard_map/ppermute | solution.py:587
  1.7 7.3 %collective-permute-start.2 = (bf16[2,32,128]{2,1,0:T(8,128)(2,1)S(1)}, bf16[2,32,128]{2,1,0:T(8,128)(2,1)S(1)}, u32[]{:S(2)}, u32[]{:S(2)}) collective-permute-start(bf16[2,32,128]{2,1,0:T(8,128)(2,1)S(1)} %get-tuple-element.32), channel_id=1, source_target_pairs={{0,2},{2,0},{1,3},{3,1},{4,6},{6,4},{5,7},{7,5},{8,10},{10,8},{9,1... | collective-permute-start | bytes 49160 | tf_op jit(solution)/shard_map/ppermute | solution.py:585
  4.3 4.7 %collective-permute-start.3 = (bf16[2,16,128]{2,1,0:T(8,128)(2,1)S(1)}, bf16[2,16,128]{2,1,0:T(8,128)(2,1)S(1)}, u32[]{:S(2)}, u32[]{:S(2)}) collective-permute-start(bf16[2,16,128]{2,1,0:T(8,128)(2,1)S(1)} %get-tuple-element.33), channel_id=1, source_target_pairs={{0,3},{1,2},{2,1},{3,0},{4,7},{5,6},{6,5},{7,4},{8,11},{9,10},{10,... | collective-permute-start | bytes 24584 | tf_op jit(solution)/shard_map/ppermute | solution.py:586
  4.8 9.0 %collective-permute-start = (bf16[128,128]{1,0:T(8,128)(2,1)S(1)}, bf16[128,128]{1,0:T(8,128)(2,1)S(1)}, u32[]{:S(2)}, u32[]{:S(2)}) collective-permute-start(bf16[128,128]{1,0:T(8,128)(2,1)S(1)} %get-tuple-element.27), channel_id=1, source_target_pairs={{0,8},{4,12},{8,0},{12,4},{1,9},{5,13},{9,1},{13,5},{2,10},{6,14},... | collective-permute-start | bytes 98312 | tf_op jit(solution)/shard_map/ppermute | solution.py:600
  7.7 6.1 %collective-permute-start.1 = (bf16[128,128]{1,0:T(8,128)(2,1)S(1)}, bf16[128,128]{1,0:T(8,128)(2,1)S(1)}, u32[]{:S(2)}, u32[]{:S(2)}) collective-permute-start(bf16[128,128]{1,0:T(8,128)(2,1)S(1)} %get-tuple-element.28), channel_id=1, source_target_pairs={{0,12},{4,8},{8,4},{12,0},{1,13},{5,9},{9,5},{13,1},{2,14},{6,10},... | collective-permute-start | bytes 98312 | tf_op jit(solution)/shard_map/ppermute | solution.py:600
  10.3 6.5 %collective-permute-start.5 = (bf16[208,128]{1,0:T(8,128)(2,1)S(1)}, bf16[208,128]{1,0:T(8,128)(2,1)S(1)}, u32[]{:S(2)}, u32[]{:S(2)}) collective-permute-start(bf16[208,128]{1,0:T(8,128)(2,1)S(1)} %get-tuple-element.35), channel_id=1, source_target_pairs={{0,8},{4,12},{8,0},{12,4},{1,9},{5,13},{9,1},{13,5},{2,10},{6,14},... | collective-permute-start | bytes 159752 | tf_op jit(solution)/shard_map/ppermute | solution.py:619
  12.0 6.1 %collective-permute-start.6 = (bf16[208,128]{1,0:T(8,128)(2,1)S(1)}, bf16[208,128]{1,0:T(8,128)(2,1)S(1)}, u32[]{:S(2)}, u32[]{:S(2)}) collective-permute-start(bf16[208,128]{1,0:T(8,128)(2,1)S(1)} %get-tuple-element.36), channel_id=1, source_target_pairs={{0,12},{4,8},{8,4},{12,0},{1,13},{5,9},{9,5},{13,1},{2,14},{6,10},... | collective-permute-start | bytes 159752 | tf_op jit(solution)/shard_map/ppermute | solution.py:619
  12.9 5.9 %collective-permute-start.7 = (bf16[336,128]{1,0:T(8,128)(2,1)S(1)}, bf16[336,128]{1,0:T(8,128)(2,1)S(1)}, u32[]{:S(2)}, u32[]{:S(2)}) collective-permute-start(bf16[336,128]{1,0:T(8,128)(2,1)S(1)} %get-tuple-element.37), channel_id=1, source_target_pairs={{0,4},{4,0},{8,12},{12,8},{1,5},{5,1},{9,13},{13,9},{2,6},{6,2},{1... | collective-permute-start | bytes 258056 | tf_op jit(solution)/shard_map/ppermute | solution.py:619
  20.4 5.5 %collective-permute-start.8 = (f32[8,256]{1,0:T(8,128)S(1)}, f32[8,256]{1,0:T(8,128)S(1)}, u32[]{:S(2)}, u32[]{:S(2)}) collective-permute-start(f32[8,256]{1,0:T(8,128)S(1)} %get-tuple-element.39), channel_id=1, source_target_pairs={{0,12},{4,8},{8,4},{12,0},{1,13},{5,9},{9,5},{13,1},{2,14},{6,10},... | collective-permute-start | bytes 24584 | tf_op jit(solution)/shard_map/ppermute | solution.py:619
  22.5 4.5 %collective-permute-start.9 = (f32[8,256]{1,0:T(8,128)S(1)}, f32[8,256]{1,0:T(8,128)S(1)}, u32[]{:S(2)}, u32[]{:S(2)}) collective-permute-start(f32[8,256]{1,0:T(8,128)S(1)} %get-tuple-element.40), channel_id=1, source_target_pairs={{0,8},{4,12},{8,0},{12,4},{1,9},{5,13},{9,1},{13,5},{2,10},{6,14},... | collective-permute-start | bytes 24584 | tf_op jit(solution)/shard_map/ppermute | solution.py:619
  22.5 4.5 %collective-permute-start.10 = (f32[8,256]{1,0:T(8,128)S(1)}, f32[8,256]{1,0:T(8,128)S(1)}, u32[]{:S(2)}, u32[]{:S(2)}) collective-permute-start(f32[8,256]{1,0:T(8,128)S(1)} %get-tuple-element.41), channel_id=1, source_target_pairs={{0,4},{4,0},{8,12},{12,8},{1,5},{5,1},{9,13},{13,9},{2,6},{6,2},{1... | collective-permute-start | bytes 24584 | tf_op jit(solution)/shard_map/ppermute | solution.py:619

commit v4 on v2

--- a/solution.py
+++ b/solution.py
@@ -339,9 +339,9 @@
         source = jnp.where(place < lines, place, place + jnp.where(az == 0, 0, -lines - HALO_LINES))
         taps = banded(tap_row(index_ref[0, 0]), source - line - offsets_ref[0, 0] + 3)
         line_ref[half] = jnp.concatenate(halves(taps), axis=0)
-    shape = (3 * LANES, LANES)
+    shape = (2 * LANES, LANES)
     distance = lax.broadcasted_iota(jnp.int32, shape, 0) - lax.broadcasted_iota(jnp.int32, shape, 1)
-    distance = distance - (LANES - FILTER_HALF - 3) - offsets_ref[0, 1]
+    distance = distance - (LANES // 2 - FILTER_HALF - 3) - offsets_ref[0, 1]
     taps = banded(tap_row(index_ref[0, 1]), distance)
     column_ref[...] = jnp.concatenate(halves(taps), axis=1)
     for copy in copies[2:]:
@@ -349,10 +349,10 @@
 
 
 def along_range(moved, column_ref, tiles):
-    high, low = halves(moved)
+    high, low = halves(pltpu.roll(moved, moved.shape[1] - LANES // 2, 1))
     starts = range(0, tiles * LANES, LANES)
-    high = jnp.concatenate([high[:, s : s + 3 * LANES] for s in starts], axis=0)
-    low = jnp.concatenate([low[:, s : s + 3 * LANES] for s in starts], axis=0)
+    high = jnp.concatenate([high[:, s : s + 2 * LANES] for s in starts], axis=0)
+    low = jnp.concatenate([low[:, s : s + 2 * LANES] for s in starts], axis=0)
     total = dot(high, column_ref[...])
     return total[:, :LANES] + total[:, LANES:] + dot(low, column_ref[:, :LANES])
 
@@ -556,7 +556,7 @@
             jax.ShapeDtypeStruct((2, HALO_LINES, LANES), bf16),
             jax.ShapeDtypeStruct((2, HALO_LINES, columns), bf16),
             jax.ShapeDtypeStruct((2, 2 * HALO_LINES, lines + HALO_LINES), bf16),
-            jax.ShapeDtypeStruct((3 * LANES, 2 * LANES), bf16),
+            jax.ShapeDtypeStruct((2 * LANES, 2 * LANES), bf16),
             jax.ShapeDtypeStruct((2, lines, columns + 3 * LANES), bf16),
         ],
         in_specs=[hbm] * 3,

time: 27.2 us -> 27 us (level)
  transfers between devices with their start and end apart: 10 -> 10, of which waited for: 4 -> 4; matrix products, arithmetic and copies ran while one was open for 0% -> 0% of each run, Pallas kernels for 10% -> 9%
where the time goes in v4:
time: 27 us; the launch traced here: 26.8 us
  starting transfers between devices  14.9 us (55%)
  Pallas kernels  6 us (22%)
  waiting for transfers between devices  5.84 us (22%)
    ppermute x6, starting transfers between devices, exchanged(): lax.ppermute(values[step], 'date', [(i, i ^ reach(step, dates)) for i in...  8.87 us
    ppermute x6, waiting for transfers between devices, exchanged(): lax.ppermute(values[step], 'date', [(i, i ^ reach(step, dates)) for i in...  5.83 us
    ppermute x1, starting transfers between devices, tiled_body(): lax.ppermute(early, 'date', [(i, i ^ reach(dates - 1, dates)) for i in ra...  2.89 us
    ppermute x1, starting transfers between devices, tiled_body(): side = lax.ppermute(side, 'rng', swap)  2.56 us
    pallas_call x1, Pallas kernels, tiled_body(): pl.pallas_call(functools.partial(looks_kernel, pairs, dates), out_shape=[...  1.57 us
    pallas_call x1, Pallas kernels, tiled_body(): pl.pallas_call(functools.partial(filter_kernel, pairs), out_shape=[jax.Sh...  1.23 us
    pallas_call x1, Pallas kernels, tiled_body(): pl.pallas_call(prepare_kernel, out_shape=[jax.ShapeDtypeStruct((2, lines,...  1.16 us
    pallas_call x1, Pallas kernels, tiled_body(): pl.pallas_call(resample_kernel, out_shape=[jax.ShapeDtypeStruct((rows, LA...  0.93 us
  transfers between devices with their start and end apart: 10, of which 4 were waited for; matrix products, arithmetic and copies ran while one was open for 0% of the time, Pallas kernels for 9%

profile of v4, /device:TPU:0, one launch (start us, length us, event | category | flops | bytes accessed | tf_op | source)
XLA Modules:
  0.0 26.8 jit_solution(10556471401452931398)
XLA Ops:
  0.0 1.2 %shard_map.46 = (bf16[2,32,128]{2,1,0:T(8,128)(2,1)S(1)}, bf16[2,16,128]{2,1,0:T(8,128)(2,1)S(1)}, bf16[2,16,2560]{2,1,0:T(8,128)(2,1)S(1)}, bf16[2,32,48]{2,1,0...) custom-call(s32[1,2]{1,0:T(1,128)} %offsets_hbm.1, s32[1,2]{1,0:T(1,128)} %index_hbm.1, ...), custom_call_target="tpu_custom_call" | custom-call | tf_op jit(solution)/shard_map/pallas_call | solution.py:552
  1.2 0.5 %collective-permute-start.3 = (bf16[2,16,2560]{2,1,0:T(8,128)(2,1)S(1)}, bf16[2,16,2560]{2,1,0:T(8,128)(2,1)S(1)}, u32[]{:S(2)}, u32[]{:S(2)}) collective-permute-start(bf16[2,16,2560]{2,1,0:T(8,128)(2,1)S(1)} %get-tuple-element.28), channel_id=1, source_target_pairs={{0,1},{1,0},{2,3},{3,2},{4,5},{5,4},{6,7},{7,6},{8,9},{9,8},{10,11... | collective-permute-start | bytes 491528 | tf_op jit(solution)/shard_map/ppermute | solution.py:574
  1.7 2.6 %collective-permute-start.1 = (bf16[2,32,128]{2,1,0:T(8,128)(2,1)S(1)}, bf16[2,32,128]{2,1,0:T(8,128)(2,1)S(1)}, u32[]{:S(2)}, u32[]{:S(2)}) collective-permute-start(bf16[2,32,128]{2,1,0:T(8,128)(2,1)S(1)} %get-tuple-element.26), channel_id=1, source_target_pairs={{0,2},{2,0},{1,3},{3,1},{4,6},{6,4},{5,7},{7,5},{8,10},{10,8},{9,1... | collective-permute-start | bytes 49160 | tf_op jit(solution)/shard_map/ppermute | solution.py:572
  4.2 0.1 collective-permute-start.2
  4.3 0.4 %shard_map.47 = bf16[128,128]{1,0:T(8,128)(2,1)S(1)} custom-call(bf16[2,32,2944]{2,1,0:T(8,128)(2,1)S(1)} %get-tuple-element.21.held_ref, bf16[2,32,48]{2,1,0:T(8,128)(2,1)S(1)} %get-tuple-element.22.line_ref, bf16[256,256]{1,0:T(8,128)(2,1)S(1)} %get-tuple-element.23.column_ref), custom_call_target="tpu_custom_call" | custom-call | tf_op jit(solution)/shard_map/pallas_call | solution.py:577
  4.7 2.9 %collective-permute-start = (bf16[128,128]{1,0:T(8,128)(2,1)S(1)}, bf16[128,128]{1,0:T(8,128)(2,1)S(1)}, u32[]{:S(2)}, u32[]{:S(2)}) collective-permute-start(bf16[128,128]{1,0:T(8,128)(2,1)S(1)} %shard_map.47), channel_id=1, source_target_pairs={{0,8},{4,12},{8,0},{12,4},{1,9},{5,13},{9,1},{13,5},{2,10},{6,14},... | collective-permute-start | bytes 98312 | tf_op jit(solution)/shard_map/ppermute | solution.py:584
  7.6 0.0 collective-permute-done.2.corner_ref
  7.6 0.0 collective-permute-done.1.side_ref
  7.6 0.0 collective-permute-done.3.lines_ref
  7.6 0.9 %shard_map.49 = (bf16[336,128]{1,0:T(8,128)(2,1)S(1)}, bf16[336,128]{1,0:T(8,128)(2,1)S(1)}, bf16[336,128]{1,0:T(8,128)(2,1)S(1)}, bf16[208,128]{1,0:T(8,128)(2,1)S(1)}) custom-call(bf16[2,32,128]{2,1,0:T(8,128)(2,1)S(1)} %collective-permute-done.1.side_ref, bf16[2,16,128]{2,1,0:T(8,128)(2,1)S(1)} %collective-permute-done.2.corner_ref, ...), custom_call_target="tpu_custom_call" | custom-call | tf_op jit(solution)/shard_map/pallas_call | solution.py:586
  8.5 3.4 %collective-permute-start.5 = (bf16[336,128]{1,0:T(8,128)(2,1)S(1)}, bf16[336,128]{1,0:T(8,128)(2,1)S(1)}, u32[]{:S(2)}, u32[]{:S(2)}) collective-permute-start(bf16[336,128]{1,0:T(8,128)(2,1)S(1)} %get-tuple-element.30), channel_id=1, source_target_pairs={{0,12},{4,8},{8,4},{12,0},{1,13},{5,9},{9,5},{13,1},{2,14},{6,10},... | collective-permute-start | bytes 258056 | tf_op jit(solution)/shard_map/ppermute | solution.py:601
  11.9 0.0 collective-permute-start.6
  11.9 1.0 %collective-permute-start.4 = (bf16[208,128]{1,0:T(8,128)(2,1)S(1)}, bf16[208,128]{1,0:T(8,128)(2,1)S(1)}, u32[]{:S(2)}, u32[]{:S(2)}) collective-permute-start(bf16[208,128]{1,0:T(8,128)(2,1)S(1)} %get-tuple-element.29), channel_id=1, source_target_pairs={{0,8},{4,12},{8,0},{12,4},{1,9},{5,13},{9,1},{13,5},{2,10},{6,14},... | collective-permute-start | bytes 159752 | tf_op jit(solution)/shard_map/ppermute | solution.py:601
  13.0 0.0 collective-permute-done.early_ref
  13.0 1.2 %shard_map.48 = (bf16[6,256,512]{2,1,0:T(8,128)(2,1)S(1)}, bf16[320,128]{1,0:T(8,128)(2,1)S(1)}) custom-call(f32[4]{0:T(128)} %shift_hbm.1, bf16[128,128]{1,0:T(8,128)(2,1)S(1)} %collective-permute-done.early_ref), custom_call_target="tpu_custom_call" | custom-call | flops 600000000 | tf_op jit(solution)/shard_map/pallas_call | solution.py:608
  14.2 3.5 %collective-permute-done.4.refs_1_ = bf16[208,128]{1,0:T(8,128)(2,1)S(1)} collective-permute-done((bf16[208,128]{1,0:T(8,128)(2,1)S(1)}, bf16[208,128]{1,0:T(8,128)(2,1)S(1)}, u32[]{:S(2)}, u32[]{:S(2)}) %collective-permute-start.4) | collective-permute-done | bytes 53280 | tf_op jit(solution)/shard_map/ppermute | solution.py:601
  17.7 0.0 collective-permute-done.5.refs_2_
  17.7 0.4 %collective-permute-done.6.refs_3_ = bf16[336,128]{1,0:T(8,128)(2,1)S(1)} collective-permute-done((bf16[336,128]{1,0:T(8,128)(2,1)S(1)}, bf16[336,128]{1,0:T(8,128)(2,1)S(1)}, u32[]{:S(2)}, u32[]{:S(2)}) %collective-permute-start.6) | collective-permute-done | bytes 86048 | tf_op jit(solution)/shard_map/ppermute | solution.py:601
  18.1 1.6 %shard_map.50 = (f32[8,256]{1,0:T(8,128)S(1)}, f32[8,256]{1,0:T(8,128)S(1)}, f32[8,256]{1,0:T(8,128)S(1)}, f32[8,256]{1,0:T(8,128)S(1)}) custom-call(bf16[6,256,512]{2,1,0:T(8,128)(2,1)S(1)} %get-tuple-element.24.weight_ref, bf16[320,128]{1,0:T(8,128)(2,1)S(1)} %get-tuple-element.25.refs_0_, bf16[208,128]{1,0:T(8,128)(2,1)S(1)} %collective-permute-done.4.refs_1_, ...), custom_call_target="tpu_custom_call" | custom-call | tf_op jit(solution)/shard_map/pallas_call | solution.py:620
  19.7 1.9 %collective-permute-start.7 = (f32[8,256]{1,0:T(8,128)S(1)}, f32[8,256]{1,0:T(8,128)S(1)}, u32[]{:S(2)}, u32[]{:S(2)}) collective-permute-start(f32[8,256]{1,0:T(8,128)S(1)} %get-tuple-element.33), channel_id=1, source_target_pairs={{0,12},{4,8},{8,4},{12,0},{1,13},{5,9},{9,5},{13,1},{2,14},{6,10},... | collective-permute-start | bytes 24584 | tf_op jit(solution)/shard_map/ppermute | solution.py:601
  21.5 0.6 %collective-permute-start.8 = (f32[8,256]{1,0:T(8,128)S(1)}, f32[8,256]{1,0:T(8,128)S(1)}, u32[]{:S(2)}, u32[]{:S(2)}) collective-permute-start(f32[8,256]{1,0:T(8,128)S(1)} %get-tuple-element.34), channel_id=1, source_target_pairs={{0,8},{4,12},{8,0},{12,4},{1,9},{5,13},{9,1},{13,5},{2,10},{6,14},... | collective-permute-start | bytes 24584 | tf_op jit(solution)/shard_map/ppermute | solution.py:601
  22.1 2.0 %collective-permute-start.9 = (f32[8,256]{1,0:T(8,128)S(1)}, f32[8,256]{1,0:T(8,128)S(1)}, u32[]{:S(2)}, u32[]{:S(2)}) collective-permute-start(f32[8,256]{1,0:T(8,128)S(1)} %get-tuple-element.35), channel_id=1, source_target_pairs={{0,4},{4,0},{8,12},{12,8},{1,5},{5,1},{9,13},{13,9},{2,6},{6,2},{1... | collective-permute-start | bytes 24584 | tf_op jit(solution)/shard_map/ppermute | solution.py:601
  24.1 1.1 %collective-permute-done.7.refs_0_ = f32[8,256]{1,0:T(8,128)S(1)} collective-permute-done((f32[8,256]{1,0:T(8,128)S(1)}, f32[8,256]{1,0:T(8,128)S(1)}, u32[]{:S(2)}, u32[]{:S(2)}) %collective-permute-start.7) | collective-permute-done | bytes 8224 | tf_op jit(solution)/shard_map/ppermute | solution.py:601
  25.2 0.9 %collective-permute-done.8.refs_1_ = f32[8,256]{1,0:T(8,128)S(1)} collective-permute-done((f32[8,256]{1,0:T(8,128)S(1)}, f32[8,256]{1,0:T(8,128)S(1)}, u32[]{:S(2)}, u32[]{:S(2)}) %collective-permute-start.8) | collective-permute-done | bytes 8224 | tf_op jit(solution)/shard_map/ppermute | solution.py:601
  26.1 0.0 collective-permute-done.9.refs_2_
  26.1 0.7 %shard_map.51 = f32[2,8,8,128]{3,2,1,0:T(8,128)} custom-call(f32[8,256]{1,0:T(8,128)S(1)} %collective-permute-done.7.refs_0_, f32[8,256]{1,0:T(8,128)S(1)} %collective-permute-done.8.refs_1_, f32[8,256]{1,0:T(8,128)S(1)} %collective-permute-done.9.refs_2_, f32[8,256]{1,0:T(8,128)S(1)} %get-tuple-element.36.refs_3_), custom_call_target="tpu_custom_call" | custom-call | tf_op jit(solution)/shard_map/pallas_call | solution.py:634
Async XLA Ops:
  1.2 6.4 %collective-permute-start.3 = (bf16[2,16,2560]{2,1,0:T(8,128)(2,1)S(1)}, bf16[2,16,2560]{2,1,0:T(8,128)(2,1)S(1)}, u32[]{:S(2)}, u32[]{:S(2)}) collective-permute-start(bf16[2,16,2560]{2,1,0:T(8,128)(2,1)S(1)} %get-tuple-element.28), channel_id=1, source_target_pairs={{0,1},{1,0},{2,3},{3,2},{4,5},{5,4},{6,7},{7,6},{8,9},{9,8},{10,11... | collective-permute-start | bytes 491528 | tf_op jit(solution)/shard_map/ppermute | solution.py:574
  1.7 5.9 %collective-permute-start.1 = (bf16[2,32,128]{2,1,0:T(8,128)(2,1)S(1)}, bf16[2,32,128]{2,1,0:T(8,128)(2,1)S(1)}, u32[]{:S(2)}, u32[]{:S(2)}) collective-permute-start(bf16[2,32,128]{2,1,0:T(8,128)(2,1)S(1)} %get-tuple-element.26), channel_id=1, source_target_pairs={{0,2},{2,0},{1,3},{3,1},{4,6},{6,4},{5,7},{7,5},{8,10},{10,8},{9,1... | collective-permute-start | bytes 49160 | tf_op jit(solution)/shard_map/ppermute | solution.py:572
  4.2 3.4 %collective-permute-start.2 = (bf16[2,16,128]{2,1,0:T(8,128)(2,1)S(1)}, bf16[2,16,128]{2,1,0:T(8,128)(2,1)S(1)}, u32[]{:S(2)}, u32[]{:S(2)}) collective-permute-start(bf16[2,16,128]{2,1,0:T(8,128)(2,1)S(1)} %get-tuple-element.27), channel_id=1, source_target_pairs={{0,3},{1,2},{2,1},{3,0},{4,7},{5,6},{6,5},{7,4},{8,11},{9,10},{10,... | collective-permute-start | bytes 24584 | tf_op jit(solution)/shard_map/ppermute | solution.py:573
  4.7 8.3 %collective-permute-start = (bf16[128,128]{1,0:T(8,128)(2,1)S(1)}, bf16[128,128]{1,0:T(8,128)(2,1)S(1)}, u32[]{:S(2)}, u32[]{:S(2)}) collective-permute-start(bf16[128,128]{1,0:T(8,128)(2,1)S(1)} %shard_map.47), channel_id=1, source_target_pairs={{0,8},{4,12},{8,0},{12,4},{1,9},{5,13},{9,1},{13,5},{2,10},{6,14},... | collective-permute-start | bytes 98312 | tf_op jit(solution)/shard_map/ppermute | solution.py:584
  8.5 9.1 %collective-permute-start.5 = (bf16[336,128]{1,0:T(8,128)(2,1)S(1)}, bf16[336,128]{1,0:T(8,128)(2,1)S(1)}, u32[]{:S(2)}, u32[]{:S(2)}) collective-permute-start(bf16[336,128]{1,0:T(8,128)(2,1)S(1)} %get-tuple-element.30), channel_id=1, source_target_pairs={{0,12},{4,8},{8,4},{12,0},{1,13},{5,9},{9,5},{13,1},{2,14},{6,10},... | collective-permute-start | bytes 258056 | tf_op jit(solution)/shard_map/ppermute | solution.py:601
  11.9 6.2 %collective-permute-start.6 = (bf16[336,128]{1,0:T(8,128)(2,1)S(1)}, bf16[336,128]{1,0:T(8,128)(2,1)S(1)}, u32[]{:S(2)}, u32[]{:S(2)}) collective-permute-start(bf16[336,128]{1,0:T(8,128)(2,1)S(1)} %get-tuple-element.31), channel_id=1, source_target_pairs={{0,4},{4,0},{8,12},{12,8},{1,5},{5,1},{9,13},{13,9},{2,6},{6,2},{1... | collective-permute-start | bytes 258056 | tf_op jit(solution)/shard_map/ppermute | solution.py:601
  11.9 5.7 %collective-permute-start.4 = (bf16[208,128]{1,0:T(8,128)(2,1)S(1)}, bf16[208,128]{1,0:T(8,128)(2,1)S(1)}, u32[]{:S(2)}, u32[]{:S(2)}) collective-permute-start(bf16[208,128]{1,0:T(8,128)(2,1)S(1)} %get-tuple-element.29), channel_id=1, source_target_pairs={{0,8},{4,12},{8,0},{12,4},{1,9},{5,13},{9,1},{13,5},{2,10},{6,14},... | collective-permute-start | bytes 159752 | tf_op jit(solution)/shard_map/ppermute | solution.py:601
  19.7 5.5 %collective-permute-start.7 = (f32[8,256]{1,0:T(8,128)S(1)}, f32[8,256]{1,0:T(8,128)S(1)}, u32[]{:S(2)}, u32[]{:S(2)}) collective-permute-start(f32[8,256]{1,0:T(8,128)S(1)} %get-tuple-element.33), channel_id=1, source_target_pairs={{0,12},{4,8},{8,4},{12,0},{1,13},{5,9},{9,5},{13,1},{2,14},{6,10},... | collective-permute-start | bytes 24584 | tf_op jit(solution)/shard_map/ppermute | solution.py:601
  21.5 4.5 %collective-permute-start.8 = (f32[8,256]{1,0:T(8,128)S(1)}, f32[8,256]{1,0:T(8,128)S(1)}, u32[]{:S(2)}, u32[]{:S(2)}) collective-permute-start(f32[8,256]{1,0:T(8,128)S(1)} %get-tuple-element.34), channel_id=1, source_target_pairs={{0,8},{4,12},{8,0},{12,4},{1,9},{5,13},{9,1},{13,5},{2,10},{6,14},... | collective-permute-start | bytes 24584 | tf_op jit(solution)/shard_map/ppermute | solution.py:601
  22.1 3.9 %collective-permute-start.9 = (f32[8,256]{1,0:T(8,128)S(1)}, f32[8,256]{1,0:T(8,128)S(1)}, u32[]{:S(2)}, u32[]{:S(2)}) collective-permute-start(f32[8,256]{1,0:T(8,128)S(1)} %get-tuple-element.35), channel_id=1, source_target_pairs={{0,4},{4,0},{8,12},{12,8},{1,5},{5,1},{9,13},{13,9},{2,6},{6,2},{1... | collective-permute-start | bytes 24584 | tf_op jit(solution)/shard_map/ppermute | solution.py:601

commit v5 on v4

--- a/solution.py
+++ b/solution.py
@@ -580,6 +580,7 @@
         in_specs=[vmem] * 3,
         out_specs=vmem,
         compiler_params=limit,
+        cost_estimate=pl.CostEstimate(flops=2_500_000_000, bytes_accessed=0, transcendentals=0),
     )(held, line_taps, column_taps)
     early = lax.ppermute(early, "date", [(i, i ^ reach(dates - 1, dates)) for i in range(dates)])
     out_rows = [chunk_rows + FOLD] * (dates - 1) + [chunk_rows + FOLD - early_rows]

time: 27 us -> 27 us (level)
    ppermute x1, starting transfers between devices: 0.07 us -> 2.44 us  [tiled_body(): lax.ppermute(corner, ('rng', 'az'), [(0, 3), (1, 2), (2, 1), (3, 0)])]
    ppermute x1, starting transfers between devices: 2.56 us -> 0.64 us  [tiled_body(): side = lax.ppermute(side, 'rng', swap)]
    ppermute x1, starting transfers between devices: 0.52 us -> 0.04 us  [tiled_body(): halo_lines = lax.ppermute(halo_lines, 'az', swap)]
where the time goes in v5:
time: 27 us; the launch traced here: 26.9 us
  starting transfers between devices  14.9 us (55%)
  Pallas kernels  6 us (22%)
  waiting for transfers between devices  5.92 us (22%)
    ppermute x6, starting transfers between devices, exchanged(): lax.ppermute(values[step], 'date', [(i, i ^ reach(step, dates)) for i in...  8.87 us
    ppermute x6, waiting for transfers between devices, exchanged(): lax.ppermute(values[step], 'date', [(i, i ^ reach(step, dates)) for i in...  5.91 us
    ppermute x1, starting transfers between devices, tiled_body(): lax.ppermute(early, 'date', [(i, i ^ reach(dates - 1, dates)) for i in ra...  2.91 us
    ppermute x1, starting transfers between devices, tiled_body(): lax.ppermute(corner, ('rng', 'az'), [(0, 3), (1, 2), (2, 1), (3, 0)])  2.44 us
    pallas_call x1, Pallas kernels, tiled_body(): pl.pallas_call(functools.partial(looks_kernel, pairs, dates), out_shape=[...  1.57 us
    pallas_call x1, Pallas kernels, tiled_body(): pl.pallas_call(functools.partial(filter_kernel, pairs), out_shape=[jax.Sh...  1.23 us
    pallas_call x1, Pallas kernels, tiled_body(): pl.pallas_call(prepare_kernel, out_shape=[jax.ShapeDtypeStruct((2, lines,...  1.16 us
    pallas_call x1, Pallas kernels, tiled_body(): pl.pallas_call(resample_kernel, out_shape=[jax.ShapeDtypeStruct((rows, LA...  0.93 us
  transfers between devices with their start and end apart: 10, of which 4 were waited for; matrix products, arithmetic and copies ran while one was open for 0% of the time, Pallas kernels for 9%

profile of v5, /device:TPU:0, one launch (start us, length us, event | category | flops | bytes accessed | tf_op | source)
XLA Modules:
  0.0 26.9 jit_solution(5578807336150377688)
XLA Ops:
  0.0 1.2 %shard_map.46 = (bf16[2,32,128]{2,1,0:T(8,128)(2,1)S(1)}, bf16[2,16,128]{2,1,0:T(8,128)(2,1)S(1)}, bf16[2,16,2560]{2,1,0:T(8,128)(2,1)S(1)}, bf16[2,32,48]{2,1,0...) custom-call(s32[1,2]{1,0:T(1,128)} %offsets_hbm.1, s32[1,2]{1,0:T(1,128)} %index_hbm.1, ...), custom_call_target="tpu_custom_call" | custom-call | tf_op jit(solution)/shard_map/pallas_call | solution.py:552
  1.2 2.4 %collective-permute-start.2 = (bf16[2,16,128]{2,1,0:T(8,128)(2,1)S(1)}, bf16[2,16,128]{2,1,0:T(8,128)(2,1)S(1)}, u32[]{:S(2)}, u32[]{:S(2)}) collective-permute-start(bf16[2,16,128]{2,1,0:T(8,128)(2,1)S(1)} %get-tuple-element.27), channel_id=1, source_target_pairs={{0,3},{1,2},{2,1},{3,0},{4,7},{5,6},{6,5},{7,4},{8,11},{9,10},{10,... | collective-permute-start | bytes 24584 | tf_op jit(solution)/shard_map/ppermute | solution.py:573
  3.6 0.6 %collective-permute-start.1 = (bf16[2,32,128]{2,1,0:T(8,128)(2,1)S(1)}, bf16[2,32,128]{2,1,0:T(8,128)(2,1)S(1)}, u32[]{:S(2)}, u32[]{:S(2)}) collective-permute-start(bf16[2,32,128]{2,1,0:T(8,128)(2,1)S(1)} %get-tuple-element.26), channel_id=1, source_target_pairs={{0,2},{2,0},{1,3},{3,1},{4,6},{6,4},{5,7},{7,5},{8,10},{10,8},{9,1... | collective-permute-start | bytes 49160 | tf_op jit(solution)/shard_map/ppermute | solution.py:572
  4.2 0.0 collective-permute-start.3
  4.3 0.4 %shard_map.47 = bf16[128,128]{1,0:T(8,128)(2,1)S(1)} custom-call(bf16[2,32,2944]{2,1,0:T(8,128)(2,1)S(1)} %get-tuple-element.21.held_ref, bf16[2,32,48]{2,1,0:T(8,128)(2,1)S(1)} %get-tuple-element.22.line_ref, bf16[256,256]{1,0:T(8,128)(2,1)S(1)} %get-tuple-element.23.column_ref), custom_call_target="tpu_custom_call" | custom-call | flops 2500000000 | tf_op jit(solution)/shard_map/pallas_call | solution.py:577
  4.7 2.9 %collective-permute-start = (bf16[128,128]{1,0:T(8,128)(2,1)S(1)}, bf16[128,128]{1,0:T(8,128)(2,1)S(1)}, u32[]{:S(2)}, u32[]{:S(2)}) collective-permute-start(bf16[128,128]{1,0:T(8,128)(2,1)S(1)} %shard_map.47), channel_id=1, source_target_pairs={{0,8},{4,12},{8,0},{12,4},{1,9},{5,13},{9,1},{13,5},{2,10},{6,14},... | collective-permute-start | bytes 98312 | tf_op jit(solution)/shard_map/ppermute | solution.py:585
  7.6 0.0 collective-permute-done.2.corner_ref
  7.6 0.0 collective-permute-done.1.side_ref
  7.6 0.0 collective-permute-done.3.lines_ref
  7.6 0.9 %shard_map.49 = (bf16[336,128]{1,0:T(8,128)(2,1)S(1)}, bf16[336,128]{1,0:T(8,128)(2,1)S(1)}, bf16[336,128]{1,0:T(8,128)(2,1)S(1)}, bf16[208,128]{1,0:T(8,128)(2,1)S(1)}) custom-call(bf16[2,32,128]{2,1,0:T(8,128)(2,1)S(1)} %collective-permute-done.1.side_ref, bf16[2,16,128]{2,1,0:T(8,128)(2,1)S(1)} %collective-permute-done.2.corner_ref, ...), custom_call_target="tpu_custom_call" | custom-call | tf_op jit(solution)/shard_map/pallas_call | solution.py:587
  8.5 3.4 %collective-permute-start.5 = (bf16[336,128]{1,0:T(8,128)(2,1)S(1)}, bf16[336,128]{1,0:T(8,128)(2,1)S(1)}, u32[]{:S(2)}, u32[]{:S(2)}) collective-permute-start(bf16[336,128]{1,0:T(8,128)(2,1)S(1)} %get-tuple-element.30), channel_id=1, source_target_pairs={{0,12},{4,8},{8,4},{12,0},{1,13},{5,9},{9,5},{13,1},{2,14},{6,10},... | collective-permute-start | bytes 258056 | tf_op jit(solution)/shard_map/ppermute | solution.py:602
  12.0 0.0 collective-permute-start.6
  12.0 1.0 %collective-permute-start.4 = (bf16[208,128]{1,0:T(8,128)(2,1)S(1)}, bf16[208,128]{1,0:T(8,128)(2,1)S(1)}, u32[]{:S(2)}, u32[]{:S(2)}) collective-permute-start(bf16[208,128]{1,0:T(8,128)(2,1)S(1)} %get-tuple-element.29), channel_id=1, source_target_pairs={{0,8},{4,12},{8,0},{12,4},{1,9},{5,13},{9,1},{13,5},{2,10},{6,14},... | collective-permute-start | bytes 159752 | tf_op jit(solution)/shard_map/ppermute | solution.py:602
  13.0 0.0 collective-permute-done.early_ref
  13.0 1.2 %shard_map.48 = (bf16[6,256,512]{2,1,0:T(8,128)(2,1)S(1)}, bf16[320,128]{1,0:T(8,128)(2,1)S(1)}) custom-call(f32[4]{0:T(128)} %shift_hbm.1, bf16[128,128]{1,0:T(8,128)(2,1)S(1)} %collective-permute-done.early_ref), custom_call_target="tpu_custom_call" | custom-call | flops 600000000 | tf_op jit(solution)/shard_map/pallas_call | solution.py:609
  14.2 3.4 %collective-permute-done.4.refs_1_ = bf16[208,128]{1,0:T(8,128)(2,1)S(1)} collective-permute-done((bf16[208,128]{1,0:T(8,128)(2,1)S(1)}, bf16[208,128]{1,0:T(8,128)(2,1)S(1)}, u32[]{:S(2)}, u32[]{:S(2)}) %collective-permute-start.4) | collective-permute-done | bytes 53280 | tf_op jit(solution)/shard_map/ppermute | solution.py:602
  17.5 0.0 collective-permute-done.5.refs_2_
  17.6 0.3 %collective-permute-done.6.refs_3_ = bf16[336,128]{1,0:T(8,128)(2,1)S(1)} collective-permute-done((bf16[336,128]{1,0:T(8,128)(2,1)S(1)}, bf16[336,128]{1,0:T(8,128)(2,1)S(1)}, u32[]{:S(2)}, u32[]{:S(2)}) %collective-permute-start.6) | collective-permute-done | bytes 86048 | tf_op jit(solution)/shard_map/ppermute | solution.py:602
  17.8 1.6 %shard_map.50 = (f32[8,256]{1,0:T(8,128)S(1)}, f32[8,256]{1,0:T(8,128)S(1)}, f32[8,256]{1,0:T(8,128)S(1)}, f32[8,256]{1,0:T(8,128)S(1)}) custom-call(bf16[6,256,512]{2,1,0:T(8,128)(2,1)S(1)} %get-tuple-element.24.weight_ref, bf16[320,128]{1,0:T(8,128)(2,1)S(1)} %get-tuple-element.25.refs_0_, bf16[208,128]{1,0:T(8,128)(2,1)S(1)} %collective-permute-done.4.refs_1_, ...), custom_call_target="tpu_custom_call" | custom-call | tf_op jit(solution)/shard_map/pallas_call | solution.py:621
  19.4 2.1 %collective-permute-start.7 = (f32[8,256]{1,0:T(8,128)S(1)}, f32[8,256]{1,0:T(8,128)S(1)}, u32[]{:S(2)}, u32[]{:S(2)}) collective-permute-start(f32[8,256]{1,0:T(8,128)S(1)} %get-tuple-element.33), channel_id=1, source_target_pairs={{0,12},{4,8},{8,4},{12,0},{1,13},{5,9},{9,5},{13,1},{2,14},{6,10},... | collective-permute-start | bytes 24584 | tf_op jit(solution)/shard_map/ppermute | solution.py:602
  21.5 0.6 %collective-permute-start.8 = (f32[8,256]{1,0:T(8,128)S(1)}, f32[8,256]{1,0:T(8,128)S(1)}, u32[]{:S(2)}, u32[]{:S(2)}) collective-permute-start(f32[8,256]{1,0:T(8,128)S(1)} %get-tuple-element.34), channel_id=1, source_target_pairs={{0,8},{4,12},{8,0},{12,4},{1,9},{5,13},{9,1},{13,5},{2,10},{6,14},... | collective-permute-start | bytes 24584 | tf_op jit(solution)/shard_map/ppermute | solution.py:602
  22.1 1.7 %collective-permute-start.9 = (f32[8,256]{1,0:T(8,128)S(1)}, f32[8,256]{1,0:T(8,128)S(1)}, u32[]{:S(2)}, u32[]{:S(2)}) collective-permute-start(f32[8,256]{1,0:T(8,128)S(1)} %get-tuple-element.35), channel_id=1, source_target_pairs={{0,4},{4,0},{8,12},{12,8},{1,5},{5,1},{9,13},{13,9},{2,6},{6,2},{1... | collective-permute-start | bytes 24584 | tf_op jit(solution)/shard_map/ppermute | solution.py:602
  23.9 1.1 %collective-permute-done.7.refs_0_ = f32[8,256]{1,0:T(8,128)S(1)} collective-permute-done((f32[8,256]{1,0:T(8,128)S(1)}, f32[8,256]{1,0:T(8,128)S(1)}, u32[]{:S(2)}, u32[]{:S(2)}) %collective-permute-start.7) | collective-permute-done | bytes 8224 | tf_op jit(solution)/shard_map/ppermute | solution.py:602
  24.9 1.2 %collective-permute-done.8.refs_1_ = f32[8,256]{1,0:T(8,128)S(1)} collective-permute-done((f32[8,256]{1,0:T(8,128)S(1)}, f32[8,256]{1,0:T(8,128)S(1)}, u32[]{:S(2)}, u32[]{:S(2)}) %collective-permute-start.8) | collective-permute-done | bytes 8224 | tf_op jit(solution)/shard_map/ppermute | solution.py:602
  26.1 0.0 collective-permute-done.9.refs_2_
  26.1 0.7 %shard_map.51 = f32[2,8,8,128]{3,2,1,0:T(8,128)} custom-call(f32[8,256]{1,0:T(8,128)S(1)} %collective-permute-done.7.refs_0_, f32[8,256]{1,0:T(8,128)S(1)} %collective-permute-done.8.refs_1_, f32[8,256]{1,0:T(8,128)S(1)} %collective-permute-done.9.refs_2_, f32[8,256]{1,0:T(8,128)S(1)} %get-tuple-element.36.refs_3_), custom_call_target="tpu_custom_call" | custom-call | tf_op jit(solution)/shard_map/pallas_call | solution.py:635
Async XLA Ops:
  1.2 6.4 %collective-permute-start.2 = (bf16[2,16,128]{2,1,0:T(8,128)(2,1)S(1)}, bf16[2,16,128]{2,1,0:T(8,128)(2,1)S(1)}, u32[]{:S(2)}, u32[]{:S(2)}) collective-permute-start(bf16[2,16,128]{2,1,0:T(8,128)(2,1)S(1)} %get-tuple-element.27), channel_id=1, source_target_pairs={{0,3},{1,2},{2,1},{3,0},{4,7},{5,6},{6,5},{7,4},{8,11},{9,10},{10,... | collective-permute-start | bytes 24584 | tf_op jit(solution)/shard_map/ppermute | solution.py:573
  3.6 4.0 %collective-permute-start.1 = (bf16[2,32,128]{2,1,0:T(8,128)(2,1)S(1)}, bf16[2,32,128]{2,1,0:T(8,128)(2,1)S(1)}, u32[]{:S(2)}, u32[]{:S(2)}) collective-permute-start(bf16[2,32,128]{2,1,0:T(8,128)(2,1)S(1)} %get-tuple-element.26), channel_id=1, source_target_pairs={{0,2},{2,0},{1,3},{3,1},{4,6},{6,4},{5,7},{7,5},{8,10},{10,8},{9,1... | collective-permute-start | bytes 49160 | tf_op jit(solution)/shard_map/ppermute | solution.py:572
  4.2 3.3 %collective-permute-start.3 = (bf16[2,16,2560]{2,1,0:T(8,128)(2,1)S(1)}, bf16[2,16,2560]{2,1,0:T(8,128)(2,1)S(1)}, u32[]{:S(2)}, u32[]{:S(2)}) collective-permute-start(bf16[2,16,2560]{2,1,0:T(8,128)(2,1)S(1)} %get-tuple-element.28), channel_id=1, source_target_pairs={{0,1},{1,0},{2,3},{3,2},{4,5},{5,4},{6,7},{7,6},{8,9},{9,8},{10,11... | collective-permute-start | bytes 491528 | tf_op jit(solution)/shard_map/ppermute | solution.py:574
  4.7 8.3 %collective-permute-start = (bf16[128,128]{1,0:T(8,128)(2,1)S(1)}, bf16[128,128]{1,0:T(8,128)(2,1)S(1)}, u32[]{:S(2)}, u32[]{:S(2)}) collective-permute-start(bf16[128,128]{1,0:T(8,128)(2,1)S(1)} %shard_map.47), channel_id=1, source_target_pairs={{0,8},{4,12},{8,0},{12,4},{1,9},{5,13},{9,1},{13,5},{2,10},{6,14},... | collective-permute-start | bytes 98312 | tf_op jit(solution)/shard_map/ppermute | solution.py:585
  8.5 9.0 %collective-permute-start.5 = (bf16[336,128]{1,0:T(8,128)(2,1)S(1)}, bf16[336,128]{1,0:T(8,128)(2,1)S(1)}, u32[]{:S(2)}, u32[]{:S(2)}) collective-permute-start(bf16[336,128]{1,0:T(8,128)(2,1)S(1)} %get-tuple-element.30), channel_id=1, source_target_pairs={{0,12},{4,8},{8,4},{12,0},{1,13},{5,9},{9,5},{13,1},{2,14},{6,10},... | collective-permute-start | bytes 258056 | tf_op jit(solution)/shard_map/ppermute | solution.py:602
  12.0 5.9 %collective-permute-start.6 = (bf16[336,128]{1,0:T(8,128)(2,1)S(1)}, bf16[336,128]{1,0:T(8,128)(2,1)S(1)}, u32[]{:S(2)}, u32[]{:S(2)}) collective-permute-start(bf16[336,128]{1,0:T(8,128)(2,1)S(1)} %get-tuple-element.31), channel_id=1, source_target_pairs={{0,4},{4,0},{8,12},{12,8},{1,5},{5,1},{9,13},{13,9},{2,6},{6,2},{1... | collective-permute-start | bytes 258056 | tf_op jit(solution)/shard_map/ppermute | solution.py:602
  12.0 5.6 %collective-permute-start.4 = (bf16[208,128]{1,0:T(8,128)(2,1)S(1)}, bf16[208,128]{1,0:T(8,128)(2,1)S(1)}, u32[]{:S(2)}, u32[]{:S(2)}) collective-permute-start(bf16[208,128]{1,0:T(8,128)(2,1)S(1)} %get-tuple-element.29), channel_id=1, source_target_pairs={{0,8},{4,12},{8,0},{12,4},{1,9},{5,13},{9,1},{13,5},{2,10},{6,14},... | collective-permute-start | bytes 159752 | tf_op jit(solution)/shard_map/ppermute | solution.py:602
  19.4 5.5 %collective-permute-start.7 = (f32[8,256]{1,0:T(8,128)S(1)}, f32[8,256]{1,0:T(8,128)S(1)}, u32[]{:S(2)}, u32[]{:S(2)}) collective-permute-start(f32[8,256]{1,0:T(8,128)S(1)} %get-tuple-element.33), channel_id=1, source_target_pairs={{0,12},{4,8},{8,4},{12,0},{1,13},{5,9},{9,5},{13,1},{2,14},{6,10},... | collective-permute-start | bytes 24584 | tf_op jit(solution)/shard_map/ppermute | solution.py:602
  21.5 4.6 %collective-permute-start.8 = (f32[8,256]{1,0:T(8,128)S(1)}, f32[8,256]{1,0:T(8,128)S(1)}, u32[]{:S(2)}, u32[]{:S(2)}) collective-permute-start(f32[8,256]{1,0:T(8,128)S(1)} %get-tuple-element.34), channel_id=1, source_target_pairs={{0,8},{4,12},{8,0},{12,4},{1,9},{5,13},{9,1},{13,5},{2,10},{6,14},... | collective-permute-start | bytes 24584 | tf_op jit(solution)/shard_map/ppermute | solution.py:602
  22.1 4.0 %collective-permute-start.9 = (f32[8,256]{1,0:T(8,128)S(1)}, f32[8,256]{1,0:T(8,128)S(1)}, u32[]{:S(2)}, u32[]{:S(2)}) collective-permute-start(f32[8,256]{1,0:T(8,128)S(1)} %get-tuple-element.35), channel_id=1, source_target_pairs={{0,4},{4,0},{8,12},{12,8},{1,5},{5,1},{9,13},{13,9},{2,6},{6,2},{1... | collective-permute-start | bytes 24584 | tf_op jit(solution)/shard_map/ppermute | solution.py:602

commit v6 on v5

--- a/solution.py
+++ b/solution.py
@@ -306,7 +306,7 @@
     return HALO_LINES * ((row // HALO_LINES) ^ az) + LOOK_AZ * (within % quarter) + within // quarter
 
 
-def prepare_kernel(offsets_hbm, index_hbm, slc_ref, side_ref, corner_ref, lines_ref, line_ref, column_ref, held_ref, offsets_ref, index_ref, semaphores):
+def prepare_kernel(offsets_hbm, index_hbm, slc_ref, side_ref, lines_ref, line_ref, column_ref, held_ref, offsets_ref, index_ref, semaphores):
     lines, columns = slc_ref.shape[1:]
     az = lax.axis_index("az")
     row = pl.multiple_of((1 - az) * (lines - HALO_LINES), HALO_LINES)
@@ -316,7 +316,6 @@
         (offsets_hbm, offsets_ref),
         (index_hbm, index_ref),
         (slc_ref.at[:, :, outermost], side_ref),
-        (slc_ref.at[:, nearest, outermost], corner_ref),
         (slc_ref.at[:, nearest, :], lines_ref),
     ]
     for plane in range(2):
@@ -371,16 +370,18 @@
     out_ref[...] = along_range(moved, column_ref, early).astype(jnp.bfloat16)
 
 
-def resample_kernel(side_ref, corner_ref, lines_ref, held_ref, line_ref, column_ref, *outs):
+def resample_kernel(corner_ref, side_ref, lines_ref, held_ref, line_ref, column_ref, *outs):
     outs, tiles_ref, tails_ref = outs[:-2], outs[-2], outs[-1]
     lines, width = held_ref.shape[1:]
     width -= LANES
     block = lax.axis_index("rng")
+    nearest = pl.multiple_of(lax.axis_index("az") * (lines - HALO_LINES), HALO_LINES)
     taps = jnp.concatenate([line_ref[0], line_ref[1]], axis=0)
     moved = [[], []]
     for plane in range(2):
         own = jnp.concatenate([side_ref[plane], held_ref[plane, :, LANES : width - LANES], side_ref[plane]], axis=1)
-        halo = jnp.concatenate([corner_ref[plane], lines_ref[plane], corner_ref[plane]], axis=1)
+        corner = corner_ref[plane, pl.ds(nearest, HALO_LINES), :]
+        halo = jnp.concatenate([corner, lines_ref[plane], corner], axis=1)
         both = dot(taps, jnp.concatenate([own, halo], axis=0))
         for half in range(2):
             at = 2 * half * HALO_LINES
@@ -549,28 +550,27 @@
     tiles = chunk // LANES
     chunk_rows = tiles * 2 * lines
 
-    side, corner, halo_lines, line_taps, column_taps, held = pl.pallas_call(
+    side, halo_lines, line_taps, column_taps, held = pl.pallas_call(
         prepare_kernel,
         out_shape=[
             jax.ShapeDtypeStruct((2, lines, LANES), bf16),
-            jax.ShapeDtypeStruct((2, HALO_LINES, LANES), bf16),
             jax.ShapeDtypeStruct((2, HALO_LINES, columns), bf16),
             jax.ShapeDtypeStruct((2, 2 * HALO_LINES, lines + HALO_LINES), bf16),
             jax.ShapeDtypeStruct((2 * LANES, 2 * LANES), bf16),
             jax.ShapeDtypeStruct((2, lines, columns + 3 * LANES), bf16),
         ],
         in_specs=[hbm] * 3,
-        out_specs=[vmem] * 6,
+        out_specs=[vmem] * 5,
         scratch_shapes=[
             pltpu.SMEM(offsets.shape, jnp.int32),
             pltpu.SMEM(kernel_index.shape, jnp.int32),
-            pltpu.SemaphoreType.DMA((5 + 4 * (lines // HALO_LINES),)),
+            pltpu.SemaphoreType.DMA((4 + 4 * (lines // HALO_LINES),)),
         ],
         compiler_params=limit,
     )(offsets, kernel_index, cells)
     swap = [(0, 1), (1, 0)]
+    corner = lax.ppermute(side, ("rng", "az"), [(0, 3), (1, 2), (2, 1), (3, 0)])
     side = lax.ppermute(side, "rng", swap)
-    corner = lax.ppermute(corner, ("rng", "az"), [(0, 3), (1, 2), (2, 1), (3, 0)])
     halo_lines = lax.ppermute(halo_lines, "az", swap)
 
     early_rows = (tiles - 1) * lines
@@ -594,7 +594,7 @@
             pltpu.VMEM((dates, FOLD, LANES), bf16),
         ],
         compiler_params=limit,
-    )(side, corner, halo_lines, held, line_taps, column_taps)
+    )(corner, side, halo_lines, held, line_taps, column_taps)
 
     def exchanged(values, order):
         arrived = {0: values[0]}

time: 27 us -> 27 us (level)
  starting transfers between devices: 14.9 us -> 15.2 us
    ppermute x1, starting transfers between devices: 2.44 us -> 0.01 us  [tiled_body(): corner = lax.ppermute(side, ('rng', 'az'), [(0, 3), (1, 2), (2, 1), (3, 0)])]
    ppermute x1, starting transfers between devices: 0.64 us -> 3 us  [tiled_body(): side = lax.ppermute(side, 'rng', swap)]
where the time goes in v6:
time: 27 us; the launch traced here: 26.9 us
  starting transfers between devices  15.2 us (56%)
  Pallas kernels  5.98 us (22%)
  waiting for transfers between devices  5.66 us (21%)
    ppermute x6, starting transfers between devices, exchanged(): lax.ppermute(values[step], 'date', [(i, i ^ reach(step, dates)) for i in...  8.87 us
    ppermute x6, waiting for transfers between devices, exchanged(): lax.ppermute(values[step], 'date', [(i, i ^ reach(step, dates)) for i in...  5.65 us
    ppermute x1, starting transfers between devices, tiled_body(): lax.ppermute(early, 'date', [(i, i ^ reach(dates - 1, dates)) for i in ra...  3.11 us
    ppermute x1, starting transfers between devices, tiled_body(): side = lax.ppermute(side, 'rng', swap)  3 us
    pallas_call x1, Pallas kernels, tiled_body(): pl.pallas_call(functools.partial(looks_kernel, pairs, dates), out_shape=[...  1.58 us
    pallas_call x1, Pallas kernels, tiled_body(): pl.pallas_call(functools.partial(filter_kernel, pairs), out_shape=[jax.Sh...  1.23 us
    pallas_call x1, Pallas kernels, tiled_body(): pl.pallas_call(prepare_kernel, out_shape=[jax.ShapeDtypeStruct((2, lines,...  1.13 us
    pallas_call x1, Pallas kernels, tiled_body(): pl.pallas_call(resample_kernel, out_shape=[jax.ShapeDtypeStruct((rows, LA...  0.93 us
  transfers between devices with their start and end apart: 10, of which 4 were waited for; matrix products, arithmetic and copies ran while one was open for 0% of the time, Pallas kernels for 9%

profile of v6, /device:TPU:0, one launch (start us, length us, event | category | flops | bytes accessed | tf_op | source)
XLA Modules:
  0.0 26.9 jit_solution(524848734493255931)
XLA Ops:
  0.0 1.1 %shard_map.46 = (bf16[2,32,128]{2,1,0:T(8,128)(2,1)S(1)}, bf16[2,16,2560]{2,1,0:T(8,128)(2,1)S(1)}, bf16[2,32,48]{2,1,0:T(8,128)(2,1)S(1)}, bf16[256,256]{1,0:T(8,128)(2,1)S(1)}, bf16[2,32,2944]{2,1,0:T(8,128)(2,1)S(1)}) custom-call(s32[1,2]{1,0:T(1,128)} %offsets_hbm.1, s32[1,2]{1,0:T(1,128)} %index_hbm.1, bf16[2,32,2560]{2,1,0:T(8,128)(2,1)} %bitcast.4), custom_call_target="tpu_custom_call" | custom-call | tf_op jit(solution)/shard_map/pallas_call | solution.py:553
  1.1 3.0 %collective-permute-start.2 = (bf16[2,32,128]{2,1,0:T(8,128)(2,1)S(1)}, bf16[2,32,128]{2,1,0:T(8,128)(2,1)S(1)}, u32[]{:S(2)}, u32[]{:S(2)}) collective-permute-start(bf16[2,32,128]{2,1,0:T(8,128)(2,1)S(1)} %get-tuple-element.25), channel_id=1, source_target_pairs={{0,2},{2,0},{1,3},{3,1},{4,6},{6,4},{5,7},{7,5},{8,10},{10,8},{9,1... | collective-permute-start | bytes 49160 | tf_op jit(solution)/shard_map/ppermute | solution.py:573
  4.1 0.0 collective-permute-start.1
  4.2 0.2 collective-permute-start.3
  4.3 0.4 %shard_map.47 = bf16[128,128]{1,0:T(8,128)(2,1)S(1)} custom-call(bf16[2,32,2944]{2,1,0:T(8,128)(2,1)S(1)} %get-tuple-element.20.held_ref, bf16[2,32,48]{2,1,0:T(8,128)(2,1)S(1)} %get-tuple-element.21.line_ref, bf16[256,256]{1,0:T(8,128)(2,1)S(1)} %get-tuple-element.22.column_ref), custom_call_target="tpu_custom_call" | custom-call | flops 2500000000 | tf_op jit(solution)/shard_map/pallas_call | solution.py:577
  4.7 3.1 %collective-permute-start = (bf16[128,128]{1,0:T(8,128)(2,1)S(1)}, bf16[128,128]{1,0:T(8,128)(2,1)S(1)}, u32[]{:S(2)}, u32[]{:S(2)}) collective-permute-start(bf16[128,128]{1,0:T(8,128)(2,1)S(1)} %shard_map.47), channel_id=1, source_target_pairs={{0,8},{4,12},{8,0},{12,4},{1,9},{5,13},{9,1},{13,5},{2,10},{6,14},... | collective-permute-start | bytes 98312 | tf_op jit(solution)/shard_map/ppermute | solution.py:585
  7.8 0.0 collective-permute-done.2.side_ref
  7.8 0.0 collective-permute-done.1.corner_ref
  7.8 0.0 collective-permute-done.3.lines_ref
  7.9 0.9 %shard_map.49 = (bf16[336,128]{1,0:T(8,128)(2,1)S(1)}, bf16[336,128]{1,0:T(8,128)(2,1)S(1)}, bf16[336,128]{1,0:T(8,128)(2,1)S(1)}, bf16[208,128]{1,0:T(8,128)(2,1)S(1)}) custom-call(bf16[2,32,128]{2,1,0:T(8,128)(2,1)S(1)} %collective-permute-done.1.corner_ref, bf16[2,32,128]{2,1,0:T(8,128)(2,1)S(1)} %collective-permute-done.2.side_ref, ...), custom_call_target="tpu_custom_call" | custom-call | tf_op jit(solution)/shard_map/pallas_call | solution.py:587
  8.8 3.1 %collective-permute-start.5 = (bf16[336,128]{1,0:T(8,128)(2,1)S(1)}, bf16[336,128]{1,0:T(8,128)(2,1)S(1)}, u32[]{:S(2)}, u32[]{:S(2)}) collective-permute-start(bf16[336,128]{1,0:T(8,128)(2,1)S(1)} %get-tuple-element.28), channel_id=1, source_target_pairs={{0,12},{4,8},{8,4},{12,0},{1,13},{5,9},{9,5},{13,1},{2,14},{6,10},... | collective-permute-start | bytes 258056 | tf_op jit(solution)/shard_map/ppermute | solution.py:602
  11.9 0.0 collective-permute-start.6
  11.9 1.3 %collective-permute-start.4 = (bf16[208,128]{1,0:T(8,128)(2,1)S(1)}, bf16[208,128]{1,0:T(8,128)(2,1)S(1)}, u32[]{:S(2)}, u32[]{:S(2)}) collective-permute-start(bf16[208,128]{1,0:T(8,128)(2,1)S(1)} %get-tuple-element.27), channel_id=1, source_target_pairs={{0,8},{4,12},{8,0},{12,4},{1,9},{5,13},{9,1},{13,5},{2,10},{6,14},... | collective-permute-start | bytes 159752 | tf_op jit(solution)/shard_map/ppermute | solution.py:602
  13.2 0.0 collective-permute-done.early_ref
  13.2 1.2 %shard_map.48 = (bf16[6,256,512]{2,1,0:T(8,128)(2,1)S(1)}, bf16[320,128]{1,0:T(8,128)(2,1)S(1)}) custom-call(f32[4]{0:T(128)} %shift_hbm.1, bf16[128,128]{1,0:T(8,128)(2,1)S(1)} %collective-permute-done.early_ref), custom_call_target="tpu_custom_call" | custom-call | flops 600000000 | tf_op jit(solution)/shard_map/pallas_call | solution.py:609
  14.4 3.2 %collective-permute-done.4.refs_1_ = bf16[208,128]{1,0:T(8,128)(2,1)S(1)} collective-permute-done((bf16[208,128]{1,0:T(8,128)(2,1)S(1)}, bf16[208,128]{1,0:T(8,128)(2,1)S(1)}, u32[]{:S(2)}, u32[]{:S(2)}) %collective-permute-start.4) | collective-permute-done | bytes 53280 | tf_op jit(solution)/shard_map/ppermute | solution.py:602
  17.6 0.0 collective-permute-done.5.refs_2_
  17.6 0.3 collective-permute-done.6.refs_3_
  17.9 1.6 %shard_map.50 = (f32[8,256]{1,0:T(8,128)S(1)}, f32[8,256]{1,0:T(8,128)S(1)}, f32[8,256]{1,0:T(8,128)S(1)}, f32[8,256]{1,0:T(8,128)S(1)}) custom-call(bf16[6,256,512]{2,1,0:T(8,128)(2,1)S(1)} %get-tuple-element.23.weight_ref, bf16[320,128]{1,0:T(8,128)(2,1)S(1)} %get-tuple-element.24.refs_0_, bf16[208,128]{1,0:T(8,128)(2,1)S(1)} %collective-permute-done.4.refs_1_, ...), custom_call_target="tpu_custom_call" | custom-call | tf_op jit(solution)/shard_map/pallas_call | solution.py:621
  19.5 2.1 %collective-permute-start.7 = (f32[8,256]{1,0:T(8,128)S(1)}, f32[8,256]{1,0:T(8,128)S(1)}, u32[]{:S(2)}, u32[]{:S(2)}) collective-permute-start(f32[8,256]{1,0:T(8,128)S(1)} %get-tuple-element.31), channel_id=1, source_target_pairs={{0,12},{4,8},{8,4},{12,0},{1,13},{5,9},{9,5},{13,1},{2,14},{6,10},... | collective-permute-start | bytes 24584 | tf_op jit(solution)/shard_map/ppermute | solution.py:602
  21.5 0.6 %collective-permute-start.8 = (f32[8,256]{1,0:T(8,128)S(1)}, f32[8,256]{1,0:T(8,128)S(1)}, u32[]{:S(2)}, u32[]{:S(2)}) collective-permute-start(f32[8,256]{1,0:T(8,128)S(1)} %get-tuple-element.32), channel_id=1, source_target_pairs={{0,8},{4,12},{8,0},{12,4},{1,9},{5,13},{9,1},{13,5},{2,10},{6,14},... | collective-permute-start | bytes 24584 | tf_op jit(solution)/shard_map/ppermute | solution.py:602
  22.1 1.8 %collective-permute-start.9 = (f32[8,256]{1,0:T(8,128)S(1)}, f32[8,256]{1,0:T(8,128)S(1)}, u32[]{:S(2)}, u32[]{:S(2)}) collective-permute-start(f32[8,256]{1,0:T(8,128)S(1)} %get-tuple-element.33), channel_id=1, source_target_pairs={{0,4},{4,0},{8,12},{12,8},{1,5},{5,1},{9,13},{13,9},{2,6},{6,2},{1... | collective-permute-start | bytes 24584 | tf_op jit(solution)/shard_map/ppermute | solution.py:602
  23.9 1.1 %collective-permute-done.7.refs_0_ = f32[8,256]{1,0:T(8,128)S(1)} collective-permute-done((f32[8,256]{1,0:T(8,128)S(1)}, f32[8,256]{1,0:T(8,128)S(1)}, u32[]{:S(2)}, u32[]{:S(2)}) %collective-permute-start.7) | collective-permute-done | bytes 8224 | tf_op jit(solution)/shard_map/ppermute | solution.py:602
  25.0 1.2 %collective-permute-done.8.refs_1_ = f32[8,256]{1,0:T(8,128)S(1)} collective-permute-done((f32[8,256]{1,0:T(8,128)S(1)}, f32[8,256]{1,0:T(8,128)S(1)}, u32[]{:S(2)}, u32[]{:S(2)}) %collective-permute-start.8) | collective-permute-done | bytes 8224 | tf_op jit(solution)/shard_map/ppermute | solution.py:602
  26.1 0.0 collective-permute-done.9.refs_2_
  26.1 0.7 %shard_map.51 = f32[2,8,8,128]{3,2,1,0:T(8,128)} custom-call(f32[8,256]{1,0:T(8,128)S(1)} %collective-permute-done.7.refs_0_, f32[8,256]{1,0:T(8,128)S(1)} %collective-permute-done.8.refs_1_, f32[8,256]{1,0:T(8,128)S(1)} %collective-permute-done.9.refs_2_, f32[8,256]{1,0:T(8,128)S(1)} %get-tuple-element.34.refs_3_), custom_call_target="tpu_custom_call" | custom-call | tf_op jit(solution)/shard_map/pallas_call | solution.py:635
Async XLA Ops:
  1.1 6.7 %collective-permute-start.2 = (bf16[2,32,128]{2,1,0:T(8,128)(2,1)S(1)}, bf16[2,32,128]{2,1,0:T(8,128)(2,1)S(1)}, u32[]{:S(2)}, u32[]{:S(2)}) collective-permute-start(bf16[2,32,128]{2,1,0:T(8,128)(2,1)S(1)} %get-tuple-element.25), channel_id=1, source_target_pairs={{0,2},{2,0},{1,3},{3,1},{4,6},{6,4},{5,7},{7,5},{8,10},{10,8},{9,1... | collective-permute-start | bytes 49160 | tf_op jit(solution)/shard_map/ppermute | solution.py:573
  4.1 3.7 %collective-permute-start.1 = (bf16[2,32,128]{2,1,0:T(8,128)(2,1)S(1)}, bf16[2,32,128]{2,1,0:T(8,128)(2,1)S(1)}, u32[]{:S(2)}, u32[]{:S(2)}) collective-permute-start(bf16[2,32,128]{2,1,0:T(8,128)(2,1)S(1)} %get-tuple-element.25), channel_id=1, source_target_pairs={{0,3},{1,2},{2,1},{3,0},{4,7},{5,6},{6,5},{7,4},{8,11},{9,10},{10,... | collective-permute-start | bytes 49160 | tf_op jit(solution)/shard_map/ppermute | solution.py:572
  4.2 3.7 %collective-permute-start.3 = (bf16[2,16,2560]{2,1,0:T(8,128)(2,1)S(1)}, bf16[2,16,2560]{2,1,0:T(8,128)(2,1)S(1)}, u32[]{:S(2)}, u32[]{:S(2)}) collective-permute-start(bf16[2,16,2560]{2,1,0:T(8,128)(2,1)S(1)} %get-tuple-element.26), channel_id=1, source_target_pairs={{0,1},{1,0},{2,3},{3,2},{4,5},{5,4},{6,7},{7,6},{8,9},{9,8},{10,11... | collective-permute-start | bytes 491528 | tf_op jit(solution)/shard_map/ppermute | solution.py:574
  4.7 8.5 %collective-permute-start = (bf16[128,128]{1,0:T(8,128)(2,1)S(1)}, bf16[128,128]{1,0:T(8,128)(2,1)S(1)}, u32[]{:S(2)}, u32[]{:S(2)}) collective-permute-start(bf16[128,128]{1,0:T(8,128)(2,1)S(1)} %shard_map.47), channel_id=1, source_target_pairs={{0,8},{4,12},{8,0},{12,4},{1,9},{5,13},{9,1},{13,5},{2,10},{6,14},... | collective-permute-start | bytes 98312 | tf_op jit(solution)/shard_map/ppermute | solution.py:585
  8.8 8.8 %collective-permute-start.5 = (bf16[336,128]{1,0:T(8,128)(2,1)S(1)}, bf16[336,128]{1,0:T(8,128)(2,1)S(1)}, u32[]{:S(2)}, u32[]{:S(2)}) collective-permute-start(bf16[336,128]{1,0:T(8,128)(2,1)S(1)} %get-tuple-element.28), channel_id=1, source_target_pairs={{0,12},{4,8},{8,4},{12,0},{1,13},{5,9},{9,5},{13,1},{2,14},{6,10},... | collective-permute-start | bytes 258056 | tf_op jit(solution)/shard_map/ppermute | solution.py:602
  11.9 6.0 %collective-permute-start.6 = (bf16[336,128]{1,0:T(8,128)(2,1)S(1)}, bf16[336,128]{1,0:T(8,128)(2,1)S(1)}, u32[]{:S(2)}, u32[]{:S(2)}) collective-permute-start(bf16[336,128]{1,0:T(8,128)(2,1)S(1)} %get-tuple-element.29), channel_id=1, source_target_pairs={{0,4},{4,0},{8,12},{12,8},{1,5},{5,1},{9,13},{13,9},{2,6},{6,2},{1... | collective-permute-start | bytes 258056 | tf_op jit(solution)/shard_map/ppermute | solution.py:602
  11.9 5.7 %collective-permute-start.4 = (bf16[208,128]{1,0:T(8,128)(2,1)S(1)}, bf16[208,128]{1,0:T(8,128)(2,1)S(1)}, u32[]{:S(2)}, u32[]{:S(2)}) collective-permute-start(bf16[208,128]{1,0:T(8,128)(2,1)S(1)} %get-tuple-element.27), channel_id=1, source_target_pairs={{0,8},{4,12},{8,0},{12,4},{1,9},{5,13},{9,1},{13,5},{2,10},{6,14},... | collective-permute-start | bytes 159752 | tf_op jit(solution)/shard_map/ppermute | solution.py:602
  19.5 5.5 %collective-permute-start.7 = (f32[8,256]{1,0:T(8,128)S(1)}, f32[8,256]{1,0:T(8,128)S(1)}, u32[]{:S(2)}, u32[]{:S(2)}) collective-permute-start(f32[8,256]{1,0:T(8,128)S(1)} %get-tuple-element.31), channel_id=1, source_target_pairs={{0,12},{4,8},{8,4},{12,0},{1,13},{5,9},{9,5},{13,1},{2,14},{6,10},... | collective-permute-start | bytes 24584 | tf_op jit(solution)/shard_map/ppermute | solution.py:602
  21.5 4.6 %collective-permute-start.8 = (f32[8,256]{1,0:T(8,128)S(1)}, f32[8,256]{1,0:T(8,128)S(1)}, u32[]{:S(2)}, u32[]{:S(2)}) collective-permute-start(f32[8,256]{1,0:T(8,128)S(1)} %get-tuple-element.32), channel_id=1, source_target_pairs={{0,8},{4,12},{8,0},{12,4},{1,9},{5,13},{9,1},{13,5},{2,10},{6,14},... | collective-permute-start | bytes 24584 | tf_op jit(solution)/shard_map/ppermute | solution.py:602
  22.1 4.0 %collective-permute-start.9 = (f32[8,256]{1,0:T(8,128)S(1)}, f32[8,256]{1,0:T(8,128)S(1)}, u32[]{:S(2)}, u32[]{:S(2)}) collective-permute-start(f32[8,256]{1,0:T(8,128)S(1)} %get-tuple-element.33), channel_id=1, source_target_pairs={{0,4},{4,0},{8,12},{12,8},{1,5},{5,1},{9,13},{13,9},{2,6},{6,2},{1... | collective-permute-start | bytes 24584 | tf_op jit(solution)/shard_map/ppermute | solution.py:602

commit v7 on v6

--- a/solution.py
+++ b/solution.py
@@ -516,20 +516,23 @@
 
 
 def place_kernel(used_lags, looks, *refs):
-    out_ref = refs[-1]
+    received, out_ref = refs[:-1][::-1], refs[-1]
     groups, columns = out_ref.shape[2:]
     date = lax.axis_index("date")
-    lane = lax.broadcasted_iota(jnp.int32, (groups, LANES), 1) // looks
-    out_ref[...] = jnp.zeros_like(out_ref)
-    each = LANES // looks
-    for step, recv_ref in enumerate(refs[:-1][::-1]):
-        chunk = date ^ step
+    lane = lax.broadcasted_iota(jnp.int32, (groups, columns), 1) // looks
+    here = [lane == (date ^ step) for step in range(len(received))]
+    each = columns // looks
+    for part in range(2):
         for lag in range(used_lags):
-            for part in range(2):
-                tile, group = divmod(lag * 2 + part, each)
-                block = recv_ref[:, tile * LANES : (tile + 1) * LANES]
-                block = pltpu.roll(block, lax.bitwise_and(looks * (chunk - group), LANES - 1), 1)
-                out_ref[part, lag] = jnp.where(lane == chunk, block, out_ref[part, lag])
+            tile, group = divmod(lag * 2 + part, each)
+            value = jnp.zeros((groups, columns), jnp.float32)
+            for step, recv_ref in enumerate(received):
+                shift = lax.bitwise_and(looks * ((date ^ step) - group), columns - 1)
+                block = pltpu.roll(recv_ref[:, tile * columns : (tile + 1) * columns], shift, 1)
+                value = jnp.where(here[step], block, value)
+            out_ref[part, lag] = value
+        for lag in range(used_lags, out_ref.shape[1]):
+            out_ref[part, lag] = jnp.zeros((groups, columns), jnp.float32)
 
 
 def tiled_body(slc, offsets, kernel_index, range_shift):

time: 27 us -> 27 us (level)
  no operation moved by 1% of the time
where the time goes in v7:
time: 27 us; the launch traced here: 26.9 us
  starting transfers between devices  15.2 us (56%)
  Pallas kernels  5.98 us (22%)
  waiting for transfers between devices  5.66 us (21%)
    ppermute x6, starting transfers between devices, exchanged(): lax.ppermute(values[step], 'date', [(i, i ^ reach(step, dates)) for i in...  8.87 us
    ppermute x6, waiting for transfers between devices, exchanged(): lax.ppermute(values[step], 'date', [(i, i ^ reach(step, dates)) for i in...  5.65 us
    ppermute x1, starting transfers between devices, tiled_body(): lax.ppermute(early, 'date', [(i, i ^ reach(dates - 1, dates)) for i in ra...  3.11 us
    ppermute x1, starting transfers between devices, tiled_body(): side = lax.ppermute(side, 'rng', swap)  3 us
    pallas_call x1, Pallas kernels, tiled_body(): pl.pallas_call(functools.partial(looks_kernel, pairs, dates), out_shape=[...  1.58 us
    pallas_call x1, Pallas kernels, tiled_body(): pl.pallas_call(functools.partial(filter_kernel, pairs), out_shape=[jax.Sh...  1.23 us
    pallas_call x1, Pallas kernels, tiled_body(): pl.pallas_call(prepare_kernel, out_shape=[jax.ShapeDtypeStruct((2, lines,...  1.13 us
    pallas_call x1, Pallas kernels, tiled_body(): pl.pallas_call(resample_kernel, out_shape=[jax.ShapeDtypeStruct((rows, LA...  0.93 us
  transfers between devices with their start and end apart: 10, of which 4 were waited for; matrix products, arithmetic and copies ran while one was open for 0% of the time, Pallas kernels for 9%

profile of v7, /device:TPU:0, one launch (start us, length us, event | category | flops | bytes accessed | tf_op | source)
XLA Modules:
  0.0 26.9 jit_solution(5254064844119061142)
XLA Ops:
  0.0 1.1 %shard_map.46 = (bf16[2,32,128]{2,1,0:T(8,128)(2,1)S(1)}, bf16[2,16,2560]{2,1,0:T(8,128)(2,1)S(1)}, bf16[2,32,48]{2,1,0:T(8,128)(2,1)S(1)}, bf16[256,256]{1,0:T(8,128)(2,1)S(1)}, bf16[2,32,2944]{2,1,0:T(8,128)(2,1)S(1)}) custom-call(s32[1,2]{1,0:T(1,128)} %offsets_hbm.1, s32[1,2]{1,0:T(1,128)} %index_hbm.1, bf16[2,32,2560]{2,1,0:T(8,128)(2,1)} %bitcast.4), custom_call_target="tpu_custom_call" | custom-call | tf_op jit(solution)/shard_map/pallas_call | solution.py:556
  1.1 3.0 %collective-permute-start.2 = (bf16[2,32,128]{2,1,0:T(8,128)(2,1)S(1)}, bf16[2,32,128]{2,1,0:T(8,128)(2,1)S(1)}, u32[]{:S(2)}, u32[]{:S(2)}) collective-permute-start(bf16[2,32,128]{2,1,0:T(8,128)(2,1)S(1)} %get-tuple-element.25), channel_id=1, source_target_pairs={{0,2},{2,0},{1,3},{3,1},{4,6},{6,4},{5,7},{7,5},{8,10},{10,8},{9,1... | collective-permute-start | bytes 49160 | tf_op jit(solution)/shard_map/ppermute | solution.py:576
  4.1 0.0 collective-permute-start.1
  4.2 0.2 collective-permute-start.3
  4.3 0.4 %shard_map.47 = bf16[128,128]{1,0:T(8,128)(2,1)S(1)} custom-call(bf16[2,32,2944]{2,1,0:T(8,128)(2,1)S(1)} %get-tuple-element.20.held_ref, bf16[2,32,48]{2,1,0:T(8,128)(2,1)S(1)} %get-tuple-element.21.line_ref, bf16[256,256]{1,0:T(8,128)(2,1)S(1)} %get-tuple-element.22.column_ref), custom_call_target="tpu_custom_call" | custom-call | flops 2500000000 | tf_op jit(solution)/shard_map/pallas_call | solution.py:580
  4.7 3.1 %collective-permute-start = (bf16[128,128]{1,0:T(8,128)(2,1)S(1)}, bf16[128,128]{1,0:T(8,128)(2,1)S(1)}, u32[]{:S(2)}, u32[]{:S(2)}) collective-permute-start(bf16[128,128]{1,0:T(8,128)(2,1)S(1)} %shard_map.47), channel_id=1, source_target_pairs={{0,8},{4,12},{8,0},{12,4},{1,9},{5,13},{9,1},{13,5},{2,10},{6,14},... | collective-permute-start | bytes 98312 | tf_op jit(solution)/shard_map/ppermute | solution.py:588
  7.8 0.0 collective-permute-done.2.side_ref
  7.8 0.0 collective-permute-done.1.corner_ref
  7.8 0.0 collective-permute-done.3.lines_ref
  7.9 0.9 %shard_map.49 = (bf16[336,128]{1,0:T(8,128)(2,1)S(1)}, bf16[336,128]{1,0:T(8,128)(2,1)S(1)}, bf16[336,128]{1,0:T(8,128)(2,1)S(1)}, bf16[208,128]{1,0:T(8,128)(2,1)S(1)}) custom-call(bf16[2,32,128]{2,1,0:T(8,128)(2,1)S(1)} %collective-permute-done.1.corner_ref, bf16[2,32,128]{2,1,0:T(8,128)(2,1)S(1)} %collective-permute-done.2.side_ref, ...), custom_call_target="tpu_custom_call" | custom-call | tf_op jit(solution)/shard_map/pallas_call | solution.py:590
  8.8 3.1 %collective-permute-start.5 = (bf16[336,128]{1,0:T(8,128)(2,1)S(1)}, bf16[336,128]{1,0:T(8,128)(2,1)S(1)}, u32[]{:S(2)}, u32[]{:S(2)}) collective-permute-start(bf16[336,128]{1,0:T(8,128)(2,1)S(1)} %get-tuple-element.28), channel_id=1, source_target_pairs={{0,12},{4,8},{8,4},{12,0},{1,13},{5,9},{9,5},{13,1},{2,14},{6,10},... | collective-permute-start | bytes 258056 | tf_op jit(solution)/shard_map/ppermute | solution.py:605
  11.9 0.0 collective-permute-start.6
  11.9 1.3 %collective-permute-start.4 = (bf16[208,128]{1,0:T(8,128)(2,1)S(1)}, bf16[208,128]{1,0:T(8,128)(2,1)S(1)}, u32[]{:S(2)}, u32[]{:S(2)}) collective-permute-start(bf16[208,128]{1,0:T(8,128)(2,1)S(1)} %get-tuple-element.27), channel_id=1, source_target_pairs={{0,8},{4,12},{8,0},{12,4},{1,9},{5,13},{9,1},{13,5},{2,10},{6,14},... | collective-permute-start | bytes 159752 | tf_op jit(solution)/shard_map/ppermute | solution.py:605
  13.2 0.0 collective-permute-done.early_ref
  13.2 1.2 %shard_map.48 = (bf16[6,256,512]{2,1,0:T(8,128)(2,1)S(1)}, bf16[320,128]{1,0:T(8,128)(2,1)S(1)}) custom-call(f32[4]{0:T(128)} %shift_hbm.1, bf16[128,128]{1,0:T(8,128)(2,1)S(1)} %collective-permute-done.early_ref), custom_call_target="tpu_custom_call" | custom-call | flops 600000000 | tf_op jit(solution)/shard_map/pallas_call | solution.py:612
  14.4 3.2 %collective-permute-done.4.refs_1_ = bf16[208,128]{1,0:T(8,128)(2,1)S(1)} collective-permute-done((bf16[208,128]{1,0:T(8,128)(2,1)S(1)}, bf16[208,128]{1,0:T(8,128)(2,1)S(1)}, u32[]{:S(2)}, u32[]{:S(2)}) %collective-permute-start.4) | collective-permute-done | bytes 53280 | tf_op jit(solution)/shard_map/ppermute | solution.py:605
  17.6 0.0 collective-permute-done.5.refs_2_
  17.6 0.3 collective-permute-done.6.refs_3_
  17.9 1.6 %shard_map.50 = (f32[8,256]{1,0:T(8,128)S(1)}, f32[8,256]{1,0:T(8,128)S(1)}, f32[8,256]{1,0:T(8,128)S(1)}, f32[8,256]{1,0:T(8,128)S(1)}) custom-call(bf16[6,256,512]{2,1,0:T(8,128)(2,1)S(1)} %get-tuple-element.23.weight_ref, bf16[320,128]{1,0:T(8,128)(2,1)S(1)} %get-tuple-element.24.refs_0_, bf16[208,128]{1,0:T(8,128)(2,1)S(1)} %collective-permute-done.4.refs_1_, ...), custom_call_target="tpu_custom_call" | custom-call | tf_op jit(solution)/shard_map/pallas_call | solution.py:624
  19.5 2.1 %collective-permute-start.7 = (f32[8,256]{1,0:T(8,128)S(1)}, f32[8,256]{1,0:T(8,128)S(1)}, u32[]{:S(2)}, u32[]{:S(2)}) collective-permute-start(f32[8,256]{1,0:T(8,128)S(1)} %get-tuple-element.31), channel_id=1, source_target_pairs={{0,12},{4,8},{8,4},{12,0},{1,13},{5,9},{9,5},{13,1},{2,14},{6,10},... | collective-permute-start | bytes 24584 | tf_op jit(solution)/shard_map/ppermute | solution.py:605
  21.5 0.6 %collective-permute-start.8 = (f32[8,256]{1,0:T(8,128)S(1)}, f32[8,256]{1,0:T(8,128)S(1)}, u32[]{:S(2)}, u32[]{:S(2)}) collective-permute-start(f32[8,256]{1,0:T(8,128)S(1)} %get-tuple-element.32), channel_id=1, source_target_pairs={{0,8},{4,12},{8,0},{12,4},{1,9},{5,13},{9,1},{13,5},{2,10},{6,14},... | collective-permute-start | bytes 24584 | tf_op jit(solution)/shard_map/ppermute | solution.py:605
  22.1 1.8 %collective-permute-start.9 = (f32[8,256]{1,0:T(8,128)S(1)}, f32[8,256]{1,0:T(8,128)S(1)}, u32[]{:S(2)}, u32[]{:S(2)}) collective-permute-start(f32[8,256]{1,0:T(8,128)S(1)} %get-tuple-element.33), channel_id=1, source_target_pairs={{0,4},{4,0},{8,12},{12,8},{1,5},{5,1},{9,13},{13,9},{2,6},{6,2},{1... | collective-permute-start | bytes 24584 | tf_op jit(solution)/shard_map/ppermute | solution.py:605
  23.9 1.1 %collective-permute-done.7.refs_0_ = f32[8,256]{1,0:T(8,128)S(1)} collective-permute-done((f32[8,256]{1,0:T(8,128)S(1)}, f32[8,256]{1,0:T(8,128)S(1)}, u32[]{:S(2)}, u32[]{:S(2)}) %collective-permute-start.7) | collective-permute-done | bytes 8224 | tf_op jit(solution)/shard_map/ppermute | solution.py:605
  25.0 1.2 %collective-permute-done.8.refs_1_ = f32[8,256]{1,0:T(8,128)S(1)} collective-permute-done((f32[8,256]{1,0:T(8,128)S(1)}, f32[8,256]{1,0:T(8,128)S(1)}, u32[]{:S(2)}, u32[]{:S(2)}) %collective-permute-start.8) | collective-permute-done | bytes 8224 | tf_op jit(solution)/shard_map/ppermute | solution.py:605
  26.1 0.0 collective-permute-done.9.refs_2_
  26.1 0.7 %shard_map.51 = f32[2,8,8,128]{3,2,1,0:T(8,128)} custom-call(f32[8,256]{1,0:T(8,128)S(1)} %collective-permute-done.7.refs_0_, f32[8,256]{1,0:T(8,128)S(1)} %collective-permute-done.8.refs_1_, f32[8,256]{1,0:T(8,128)S(1)} %collective-permute-done.9.refs_2_, f32[8,256]{1,0:T(8,128)S(1)} %get-tuple-element.34.refs_3_), custom_call_target="tpu_custom_call" | custom-call | tf_op jit(solution)/shard_map/pallas_call | solution.py:638
Async XLA Ops:
  1.1 6.7 %collective-permute-start.2 = (bf16[2,32,128]{2,1,0:T(8,128)(2,1)S(1)}, bf16[2,32,128]{2,1,0:T(8,128)(2,1)S(1)}, u32[]{:S(2)}, u32[]{:S(2)}) collective-permute-start(bf16[2,32,128]{2,1,0:T(8,128)(2,1)S(1)} %get-tuple-element.25), channel_id=1, source_target_pairs={{0,2},{2,0},{1,3},{3,1},{4,6},{6,4},{5,7},{7,5},{8,10},{10,8},{9,1... | collective-permute-start | bytes 49160 | tf_op jit(solution)/shard_map/ppermute | solution.py:576
  4.1 3.7 %collective-permute-start.1 = (bf16[2,32,128]{2,1,0:T(8,128)(2,1)S(1)}, bf16[2,32,128]{2,1,0:T(8,128)(2,1)S(1)}, u32[]{:S(2)}, u32[]{:S(2)}) collective-permute-start(bf16[2,32,128]{2,1,0:T(8,128)(2,1)S(1)} %get-tuple-element.25), channel_id=1, source_target_pairs={{0,3},{1,2},{2,1},{3,0},{4,7},{5,6},{6,5},{7,4},{8,11},{9,10},{10,... | collective-permute-start | bytes 49160 | tf_op jit(solution)/shard_map/ppermute | solution.py:575
  4.2 3.7 %collective-permute-start.3 = (bf16[2,16,2560]{2,1,0:T(8,128)(2,1)S(1)}, bf16[2,16,2560]{2,1,0:T(8,128)(2,1)S(1)}, u32[]{:S(2)}, u32[]{:S(2)}) collective-permute-start(bf16[2,16,2560]{2,1,0:T(8,128)(2,1)S(1)} %get-tuple-element.26), channel_id=1, source_target_pairs={{0,1},{1,0},{2,3},{3,2},{4,5},{5,4},{6,7},{7,6},{8,9},{9,8},{10,11... | collective-permute-start | bytes 491528 | tf_op jit(solution)/shard_map/ppermute | solution.py:577
  4.7 8.5 %collective-permute-start = (bf16[128,128]{1,0:T(8,128)(2,1)S(1)}, bf16[128,128]{1,0:T(8,128)(2,1)S(1)}, u32[]{:S(2)}, u32[]{:S(2)}) collective-permute-start(bf16[128,128]{1,0:T(8,128)(2,1)S(1)} %shard_map.47), channel_id=1, source_target_pairs={{0,8},{4,12},{8,0},{12,4},{1,9},{5,13},{9,1},{13,5},{2,10},{6,14},... | collective-permute-start | bytes 98312 | tf_op jit(solution)/shard_map/ppermute | solution.py:588
  8.8 8.8 %collective-permute-start.5 = (bf16[336,128]{1,0:T(8,128)(2,1)S(1)}, bf16[336,128]{1,0:T(8,128)(2,1)S(1)}, u32[]{:S(2)}, u32[]{:S(2)}) collective-permute-start(bf16[336,128]{1,0:T(8,128)(2,1)S(1)} %get-tuple-element.28), channel_id=1, source_target_pairs={{0,12},{4,8},{8,4},{12,0},{1,13},{5,9},{9,5},{13,1},{2,14},{6,10},... | collective-permute-start | bytes 258056 | tf_op jit(solution)/shard_map/ppermute | solution.py:605
  11.9 6.0 %collective-permute-start.6 = (bf16[336,128]{1,0:T(8,128)(2,1)S(1)}, bf16[336,128]{1,0:T(8,128)(2,1)S(1)}, u32[]{:S(2)}, u32[]{:S(2)}) collective-permute-start(bf16[336,128]{1,0:T(8,128)(2,1)S(1)} %get-tuple-element.29), channel_id=1, source_target_pairs={{0,4},{4,0},{8,12},{12,8},{1,5},{5,1},{9,13},{13,9},{2,6},{6,2},{1... | collective-permute-start | bytes 258056 | tf_op jit(solution)/shard_map/ppermute | solution.py:605
  11.9 5.7 %collective-permute-start.4 = (bf16[208,128]{1,0:T(8,128)(2,1)S(1)}, bf16[208,128]{1,0:T(8,128)(2,1)S(1)}, u32[]{:S(2)}, u32[]{:S(2)}) collective-permute-start(bf16[208,128]{1,0:T(8,128)(2,1)S(1)} %get-tuple-element.27), channel_id=1, source_target_pairs={{0,8},{4,12},{8,0},{12,4},{1,9},{5,13},{9,1},{13,5},{2,10},{6,14},... | collective-permute-start | bytes 159752 | tf_op jit(solution)/shard_map/ppermute | solution.py:605
  19.5 5.5 %collective-permute-start.7 = (f32[8,256]{1,0:T(8,128)S(1)}, f32[8,256]{1,0:T(8,128)S(1)}, u32[]{:S(2)}, u32[]{:S(2)}) collective-permute-start(f32[8,256]{1,0:T(8,128)S(1)} %get-tuple-element.31), channel_id=1, source_target_pairs={{0,12},{4,8},{8,4},{12,0},{1,13},{5,9},{9,5},{13,1},{2,14},{6,10},... | collective-permute-start | bytes 24584 | tf_op jit(solution)/shard_map/ppermute | solution.py:605
  21.5 4.6 %collective-permute-start.8 = (f32[8,256]{1,0:T(8,128)S(1)}, f32[8,256]{1,0:T(8,128)S(1)}, u32[]{:S(2)}, u32[]{:S(2)}) collective-permute-start(f32[8,256]{1,0:T(8,128)S(1)} %get-tuple-element.32), channel_id=1, source_target_pairs={{0,8},{4,12},{8,0},{12,4},{1,9},{5,13},{9,1},{13,5},{2,10},{6,14},... | collective-permute-start | bytes 24584 | tf_op jit(solution)/shard_map/ppermute | solution.py:605
  22.1 4.0 %collective-permute-start.9 = (f32[8,256]{1,0:T(8,128)S(1)}, f32[8,256]{1,0:T(8,128)S(1)}, u32[]{:S(2)}, u32[]{:S(2)}) collective-permute-start(f32[8,256]{1,0:T(8,128)S(1)} %get-tuple-element.33), channel_id=1, source_target_pairs={{0,4},{4,0},{8,12},{12,8},{1,5},{5,1},{9,13},{13,9},{2,6},{6,2},{1... | collective-permute-start | bytes 24584 | tf_op jit(solution)/shard_map/ppermute | solution.py:605

commit v8 on v7

--- a/solution.py
+++ b/solution.py
@@ -597,6 +597,7 @@
             pltpu.VMEM((dates, FOLD, LANES), bf16),
         ],
         compiler_params=limit,
+        cost_estimate=pl.CostEstimate(flops=800_000_000, bytes_accessed=0, transcendentals=0),
     )(corner, side, halo_lines, held, line_taps, column_taps)
 
     def exchanged(values, order):
@@ -619,7 +620,7 @@
         out_specs=[vmem] * 2,
         scratch_shapes=[pltpu.SMEM(range_shift.shape, jnp.float32), pltpu.SemaphoreType.DMA],
         compiler_params=limit,
-        cost_estimate=pl.CostEstimate(flops=600_000_000, bytes_accessed=0, transcendentals=0),
+        cost_estimate=pl.CostEstimate(flops=1_100_000_000, bytes_accessed=0, transcendentals=0),
     )(range_shift, early)
     looked = pl.pallas_call(
         functools.partial(looks_kernel, pairs, dates),

time: 27 us -> 27.6 us (1.022)
  waiting for transfers between devices: 5.66 us -> 6.71 us
  starting transfers between devices: 15.2 us -> 14.7 us
    ppermute x6, waiting for transfers between devices: 5.65 us -> 6.7 us  [exchanged(): lax.ppermute(values[step], 'date', [(i, i ^ reach(step, dates)) for i in...]
    ppermute x6, starting transfers between devices: 8.87 us -> 8.43 us  [exchanged(): lax.ppermute(values[step], 'date', [(i, i ^ reach(step, dates)) for i in...]
  transfers between devices with their start and end apart: 10 -> 10, of which waited for: 4 -> 5; matrix products, arithmetic and copies ran while one was open for 0% -> 0% of each run, Pallas kernels for 9% -> 9%
where the time goes in v8:
time: 27.6 us; the launch traced here: 27.5 us
  starting transfers between devices  14.7 us (53%)
  waiting for transfers between devices  6.71 us (24%)
  Pallas kernels  5.97 us (22%)
    ppermute x6, starting transfers between devices, exchanged(): lax.ppermute(values[step], 'date', [(i, i ^ reach(step, dates)) for i in...  8.43 us
    ppermute x6, waiting for transfers between devices, exchanged(): lax.ppermute(values[step], 'date', [(i, i ^ reach(step, dates)) for i in...  6.7 us
    ppermute x1, starting transfers between devices, tiled_body(): lax.ppermute(early, 'date', [(i, i ^ reach(dates - 1, dates)) for i in ra...  3.11 us
    ppermute x1, starting transfers between devices, tiled_body(): side = lax.ppermute(side, 'rng', swap)  3 us
    pallas_call x1, Pallas kernels, tiled_body(): pl.pallas_call(functools.partial(looks_kernel, pairs, dates), out_shape=[...  1.57 us
    pallas_call x1, Pallas kernels, tiled_body(): pl.pallas_call(functools.partial(filter_kernel, pairs), out_shape=[jax.Sh...  1.23 us
    pallas_call x1, Pallas kernels, tiled_body(): pl.pallas_call(prepare_kernel, out_shape=[jax.ShapeDtypeStruct((2, lines,...  1.13 us
    pallas_call x1, Pallas kernels, tiled_body(): pl.pallas_call(resample_kernel, out_shape=[jax.ShapeDtypeStruct((rows, LA...  0.93 us
  transfers between devices with their start and end apart: 10, of which 5 were waited for; matrix products, arithmetic and copies ran while one was open for 0% of the time, Pallas kernels for 9%

profile of v8, /device:TPU:0, one launch (start us, length us, event | category | flops | bytes accessed | tf_op | source)
XLA Modules:
  0.0 27.5 jit_solution(2200302217425821929)
XLA Ops:
  0.0 1.1 %shard_map.46 = (bf16[2,32,128]{2,1,0:T(8,128)(2,1)S(1)}, bf16[2,16,2560]{2,1,0:T(8,128)(2,1)S(1)}, bf16[2,32,48]{2,1,0:T(8,128)(2,1)S(1)}, bf16[256,256]{1,0:T(8,128)(2,1)S(1)}, bf16[2,32,2944]{2,1,0:T(8,128)(2,1)S(1)}) custom-call(s32[1,2]{1,0:T(1,128)} %offsets_hbm.1, s32[1,2]{1,0:T(1,128)} %index_hbm.1, bf16[2,32,2560]{2,1,0:T(8,128)(2,1)} %bitcast.4), custom_call_target="tpu_custom_call" | custom-call | tf_op jit(solution)/shard_map/pallas_call | solution.py:556
  1.1 3.0 %collective-permute-start.2 = (bf16[2,32,128]{2,1,0:T(8,128)(2,1)S(1)}, bf16[2,32,128]{2,1,0:T(8,128)(2,1)S(1)}, u32[]{:S(2)}, u32[]{:S(2)}) collective-permute-start(bf16[2,32,128]{2,1,0:T(8,128)(2,1)S(1)} %get-tuple-element.25), channel_id=1, source_target_pairs={{0,2},{2,0},{1,3},{3,1},{4,6},{6,4},{5,7},{7,5},{8,10},{10,8},{9,1... | collective-permute-start | bytes 49160 | tf_op jit(solution)/shard_map/ppermute | solution.py:576
  4.1 0.0 collective-permute-start.1
  4.2 0.2 collective-permute-start.3
  4.3 0.4 %shard_map.47 = bf16[128,128]{1,0:T(8,128)(2,1)S(1)} custom-call(bf16[2,32,2944]{2,1,0:T(8,128)(2,1)S(1)} %get-tuple-element.20.held_ref, bf16[2,32,48]{2,1,0:T(8,128)(2,1)S(1)} %get-tuple-element.21.line_ref, bf16[256,256]{1,0:T(8,128)(2,1)S(1)} %get-tuple-element.22.column_ref), custom_call_target="tpu_custom_call" | custom-call | flops 2500000000 | tf_op jit(solution)/shard_map/pallas_call | solution.py:580
  4.7 3.1 %collective-permute-start = (bf16[128,128]{1,0:T(8,128)(2,1)S(1)}, bf16[128,128]{1,0:T(8,128)(2,1)S(1)}, u32[]{:S(2)}, u32[]{:S(2)}) collective-permute-start(bf16[128,128]{1,0:T(8,128)(2,1)S(1)} %shard_map.47), channel_id=1, source_target_pairs={{0,8},{4,12},{8,0},{12,4},{1,9},{5,13},{9,1},{13,5},{2,10},{6,14},... | collective-permute-start | bytes 98312 | tf_op jit(solution)/shard_map/ppermute | solution.py:588
  7.8 0.0 collective-permute-done.2.side_ref
  7.8 0.0 collective-permute-done.1.corner_ref
  7.8 0.0 collective-permute-done.3.lines_ref
  7.9 0.9 %shard_map.49 = (bf16[336,128]{1,0:T(8,128)(2,1)S(1)}, bf16[336,128]{1,0:T(8,128)(2,1)S(1)}, bf16[336,128]{1,0:T(8,128)(2,1)S(1)}, bf16[208,128]{1,0:T(8,128)(2,1)S(1)}) custom-call(bf16[2,32,128]{2,1,0:T(8,128)(2,1)S(1)} %collective-permute-done.1.corner_ref, bf16[2,32,128]{2,1,0:T(8,128)(2,1)S(1)} %collective-permute-done.2.side_ref, ...), custom_call_target="tpu_custom_call" | custom-call | flops 800000000 | tf_op jit(solution)/shard_map/pallas_call | solution.py:590
  8.8 2.1 %collective-permute-start.4 = (bf16[208,128]{1,0:T(8,128)(2,1)S(1)}, bf16[208,128]{1,0:T(8,128)(2,1)S(1)}, u32[]{:S(2)}, u32[]{:S(2)}) collective-permute-start(bf16[208,128]{1,0:T(8,128)(2,1)S(1)} %get-tuple-element.27), channel_id=1, source_target_pairs={{0,8},{4,12},{8,0},{12,4},{1,9},{5,13},{9,1},{13,5},{2,10},{6,14},... | collective-permute-start | bytes 159752 | tf_op jit(solution)/shard_map/ppermute | solution.py:606
  10.9 1.9 %collective-permute-start.5 = (bf16[336,128]{1,0:T(8,128)(2,1)S(1)}, bf16[336,128]{1,0:T(8,128)(2,1)S(1)}, u32[]{:S(2)}, u32[]{:S(2)}) collective-permute-start(bf16[336,128]{1,0:T(8,128)(2,1)S(1)} %get-tuple-element.28), channel_id=1, source_target_pairs={{0,12},{4,8},{8,4},{12,0},{1,13},{5,9},{9,5},{13,1},{2,14},{6,10},... | collective-permute-start | bytes 258056 | tf_op jit(solution)/shard_map/ppermute | solution.py:606
  12.8 0.0 collective-permute-start.6
  12.8 0.0 collective-permute-done.early_ref
  12.8 1.2 %shard_map.48 = (bf16[6,256,512]{2,1,0:T(8,128)(2,1)S(1)}, bf16[320,128]{1,0:T(8,128)(2,1)S(1)}) custom-call(f32[4]{0:T(128)} %shift_hbm.1, bf16[128,128]{1,0:T(8,128)(2,1)S(1)} %collective-permute-done.early_ref), custom_call_target="tpu_custom_call" | custom-call | flops 1100000000 | tf_op jit(solution)/shard_map/pallas_call | solution.py:613
  14.0 2.1 %collective-permute-done.4.refs_1_ = bf16[208,128]{1,0:T(8,128)(2,1)S(1)} collective-permute-done((bf16[208,128]{1,0:T(8,128)(2,1)S(1)}, bf16[208,128]{1,0:T(8,128)(2,1)S(1)}, u32[]{:S(2)}, u32[]{:S(2)}) %collective-permute-start.4) | collective-permute-done | bytes 53280 | tf_op jit(solution)/shard_map/ppermute | solution.py:606
  16.1 1.6 %collective-permute-done.5.refs_2_ = bf16[336,128]{1,0:T(8,128)(2,1)S(1)} collective-permute-done((bf16[336,128]{1,0:T(8,128)(2,1)S(1)}, bf16[336,128]{1,0:T(8,128)(2,1)S(1)}, u32[]{:S(2)}, u32[]{:S(2)}) %collective-permute-start.5) | collective-permute-done | bytes 86048 | tf_op jit(solution)/shard_map/ppermute | solution.py:606
  17.7 0.6 %collective-permute-done.6.refs_3_ = bf16[336,128]{1,0:T(8,128)(2,1)S(1)} collective-permute-done((bf16[336,128]{1,0:T(8,128)(2,1)S(1)}, bf16[336,128]{1,0:T(8,128)(2,1)S(1)}, u32[]{:S(2)}, u32[]{:S(2)}) %collective-permute-start.6) | collective-permute-done | bytes 86048 | tf_op jit(solution)/shard_map/ppermute | solution.py:606
  18.3 1.6 %shard_map.50 = (f32[8,256]{1,0:T(8,128)S(1)}, f32[8,256]{1,0:T(8,128)S(1)}, f32[8,256]{1,0:T(8,128)S(1)}, f32[8,256]{1,0:T(8,128)S(1)}) custom-call(bf16[6,256,512]{2,1,0:T(8,128)(2,1)S(1)} %get-tuple-element.23.weight_ref, bf16[320,128]{1,0:T(8,128)(2,1)S(1)} %get-tuple-element.24.refs_0_, bf16[208,128]{1,0:T(8,128)(2,1)S(1)} %collective-permute-done.4.refs_1_, ...), custom_call_target="tpu_custom_call" | custom-call | tf_op jit(solution)/shard_map/pallas_call | solution.py:625
  19.9 2.3 %collective-permute-start.7 = (f32[8,256]{1,0:T(8,128)S(1)}, f32[8,256]{1,0:T(8,128)S(1)}, u32[]{:S(2)}, u32[]{:S(2)}) collective-permute-start(f32[8,256]{1,0:T(8,128)S(1)} %get-tuple-element.31), channel_id=1, source_target_pairs={{0,12},{4,8},{8,4},{12,0},{1,13},{5,9},{9,5},{13,1},{2,14},{6,10},... | collective-permute-start | bytes 24584 | tf_op jit(solution)/shard_map/ppermute | solution.py:606
  22.2 0.0 collective-permute-start.8
  22.2 2.2 %collective-permute-start.9 = (f32[8,256]{1,0:T(8,128)S(1)}, f32[8,256]{1,0:T(8,128)S(1)}, u32[]{:S(2)}, u32[]{:S(2)}) collective-permute-start(f32[8,256]{1,0:T(8,128)S(1)} %get-tuple-element.33), channel_id=1, source_target_pairs={{0,4},{4,0},{8,12},{12,8},{1,5},{5,1},{9,13},{13,9},{2,6},{6,2},{1... | collective-permute-start | bytes 24584 | tf_op jit(solution)/shard_map/ppermute | solution.py:606
  24.3 1.1 %collective-permute-done.7.refs_0_ = f32[8,256]{1,0:T(8,128)S(1)} collective-permute-done((f32[8,256]{1,0:T(8,128)S(1)}, f32[8,256]{1,0:T(8,128)S(1)}, u32[]{:S(2)}, u32[]{:S(2)}) %collective-permute-start.7) | collective-permute-done | bytes 8224 | tf_op jit(solution)/shard_map/ppermute | solution.py:606
  25.4 1.3 %collective-permute-done.8.refs_1_ = f32[8,256]{1,0:T(8,128)S(1)} collective-permute-done((f32[8,256]{1,0:T(8,128)S(1)}, f32[8,256]{1,0:T(8,128)S(1)}, u32[]{:S(2)}, u32[]{:S(2)}) %collective-permute-start.8) | collective-permute-done | bytes 8224 | tf_op jit(solution)/shard_map/ppermute | solution.py:606
  26.7 0.0 collective-permute-done.9.refs_2_
  26.7 0.7 %shard_map.51 = f32[2,8,8,128]{3,2,1,0:T(8,128)} custom-call(f32[8,256]{1,0:T(8,128)S(1)} %collective-permute-done.7.refs_0_, f32[8,256]{1,0:T(8,128)S(1)} %collective-permute-done.8.refs_1_, f32[8,256]{1,0:T(8,128)S(1)} %collective-permute-done.9.refs_2_, f32[8,256]{1,0:T(8,128)S(1)} %get-tuple-element.34.refs_3_), custom_call_target="tpu_custom_call" | custom-call | tf_op jit(solution)/shard_map/pallas_call | solution.py:639
Async XLA Ops:
  1.1 6.7 %collective-permute-start.2 = (bf16[2,32,128]{2,1,0:T(8,128)(2,1)S(1)}, bf16[2,32,128]{2,1,0:T(8,128)(2,1)S(1)}, u32[]{:S(2)}, u32[]{:S(2)}) collective-permute-start(bf16[2,32,128]{2,1,0:T(8,128)(2,1)S(1)} %get-tuple-element.25), channel_id=1, source_target_pairs={{0,2},{2,0},{1,3},{3,1},{4,6},{6,4},{5,7},{7,5},{8,10},{10,8},{9,1... | collective-permute-start | bytes 49160 | tf_op jit(solution)/shard_map/ppermute | solution.py:576
  4.1 3.7 %collective-permute-start.1 = (bf16[2,32,128]{2,1,0:T(8,128)(2,1)S(1)}, bf16[2,32,128]{2,1,0:T(8,128)(2,1)S(1)}, u32[]{:S(2)}, u32[]{:S(2)}) collective-permute-start(bf16[2,32,128]{2,1,0:T(8,128)(2,1)S(1)} %get-tuple-element.25), channel_id=1, source_target_pairs={{0,3},{1,2},{2,1},{3,0},{4,7},{5,6},{6,5},{7,4},{8,11},{9,10},{10,... | collective-permute-start | bytes 49160 | tf_op jit(solution)/shard_map/ppermute | solution.py:575
  4.2 3.7 %collective-permute-start.3 = (bf16[2,16,2560]{2,1,0:T(8,128)(2,1)S(1)}, bf16[2,16,2560]{2,1,0:T(8,128)(2,1)S(1)}, u32[]{:S(2)}, u32[]{:S(2)}) collective-permute-start(bf16[2,16,2560]{2,1,0:T(8,128)(2,1)S(1)} %get-tuple-element.26), channel_id=1, source_target_pairs={{0,1},{1,0},{2,3},{3,2},{4,5},{5,4},{6,7},{7,6},{8,9},{9,8},{10,11... | collective-permute-start | bytes 491528 | tf_op jit(solution)/shard_map/ppermute | solution.py:577
  4.7 8.0 %collective-permute-start = (bf16[128,128]{1,0:T(8,128)(2,1)S(1)}, bf16[128,128]{1,0:T(8,128)(2,1)S(1)}, u32[]{:S(2)}, u32[]{:S(2)}) collective-permute-start(bf16[128,128]{1,0:T(8,128)(2,1)S(1)} %shard_map.47), channel_id=1, source_target_pairs={{0,8},{4,12},{8,0},{12,4},{1,9},{5,13},{9,1},{13,5},{2,10},{6,14},... | collective-permute-start | bytes 98312 | tf_op jit(solution)/shard_map/ppermute | solution.py:588
  8.8 7.3 %collective-permute-start.4 = (bf16[208,128]{1,0:T(8,128)(2,1)S(1)}, bf16[208,128]{1,0:T(8,128)(2,1)S(1)}, u32[]{:S(2)}, u32[]{:S(2)}) collective-permute-start(bf16[208,128]{1,0:T(8,128)(2,1)S(1)} %get-tuple-element.27), channel_id=1, source_target_pairs={{0,8},{4,12},{8,0},{12,4},{1,9},{5,13},{9,1},{13,5},{2,10},{6,14},... | collective-permute-start | bytes 159752 | tf_op jit(solution)/shard_map/ppermute | solution.py:606
  10.9 6.9 %collective-permute-start.5 = (bf16[336,128]{1,0:T(8,128)(2,1)S(1)}, bf16[336,128]{1,0:T(8,128)(2,1)S(1)}, u32[]{:S(2)}, u32[]{:S(2)}) collective-permute-start(bf16[336,128]{1,0:T(8,128)(2,1)S(1)} %get-tuple-element.28), channel_id=1, source_target_pairs={{0,12},{4,8},{8,4},{12,0},{1,13},{5,9},{9,5},{13,1},{2,14},{6,10},... | collective-permute-start | bytes 258056 | tf_op jit(solution)/shard_map/ppermute | solution.py:606
  12.8 5.5 %collective-permute-start.6 = (bf16[336,128]{1,0:T(8,128)(2,1)S(1)}, bf16[336,128]{1,0:T(8,128)(2,1)S(1)}, u32[]{:S(2)}, u32[]{:S(2)}) collective-permute-start(bf16[336,128]{1,0:T(8,128)(2,1)S(1)} %get-tuple-element.29), channel_id=1, source_target_pairs={{0,4},{4,0},{8,12},{12,8},{1,5},{5,1},{9,13},{13,9},{2,6},{6,2},{1... | collective-permute-start | bytes 258056 | tf_op jit(solution)/shard_map/ppermute | solution.py:606
  19.9 5.5 %collective-permute-start.7 = (f32[8,256]{1,0:T(8,128)S(1)}, f32[8,256]{1,0:T(8,128)S(1)}, u32[]{:S(2)}, u32[]{:S(2)}) collective-permute-start(f32[8,256]{1,0:T(8,128)S(1)} %get-tuple-element.31), channel_id=1, source_target_pairs={{0,12},{4,8},{8,4},{12,0},{1,13},{5,9},{9,5},{13,1},{2,14},{6,10},... | collective-permute-start | bytes 24584 | tf_op jit(solution)/shard_map/ppermute | solution.py:606
  22.2 4.5 %collective-permute-start.8 = (f32[8,256]{1,0:T(8,128)S(1)}, f32[8,256]{1,0:T(8,128)S(1)}, u32[]{:S(2)}, u32[]{:S(2)}) collective-permute-start(f32[8,256]{1,0:T(8,128)S(1)} %get-tuple-element.32), channel_id=1, source_target_pairs={{0,8},{4,12},{8,0},{12,4},{1,9},{5,13},{9,1},{13,5},{2,10},{6,14},... | collective-permute-start | bytes 24584 | tf_op jit(solution)/shard_map/ppermute | solution.py:606
  22.2 4.5 %collective-permute-start.9 = (f32[8,256]{1,0:T(8,128)S(1)}, f32[8,256]{1,0:T(8,128)S(1)}, u32[]{:S(2)}, u32[]{:S(2)}) collective-permute-start(f32[8,256]{1,0:T(8,128)S(1)} %get-tuple-element.33), channel_id=1, source_target_pairs={{0,4},{4,0},{8,12},{12,8},{1,5},{5,1},{9,13},{13,9},{2,6},{6,2},{1... | collective-permute-start | bytes 24584 | tf_op jit(solution)/shard_map/ppermute | solution.py:606

commit v9 on v7

--- a/solution.py
+++ b/solution.py
@@ -583,7 +583,7 @@
         in_specs=[vmem] * 3,
         out_specs=vmem,
         compiler_params=limit,
-        cost_estimate=pl.CostEstimate(flops=2_500_000_000, bytes_accessed=0, transcendentals=0),
+        cost_estimate=pl.CostEstimate(flops=1_000_000_000, bytes_accessed=0, transcendentals=0),
     )(held, line_taps, column_taps)
     early = lax.ppermute(early, "date", [(i, i ^ reach(dates - 1, dates)) for i in range(dates)])
     out_rows = [chunk_rows + FOLD] * (dates - 1) + [chunk_rows + FOLD - early_rows]

time: 27 us -> 26.9 us (level)
  starting transfers between devices: 15.2 us -> 14.9 us
    ppermute x1, starting transfers between devices: 3 us -> 2.56 us  [tiled_body(): side = lax.ppermute(side, 'rng', swap)]
    ppermute x1, starting transfers between devices: 0.19 us -> 0.52 us  [tiled_body(): halo_lines = lax.ppermute(halo_lines, 'az', swap)]
where the time goes in v9:
time: 26.9 us; the launch traced here: 26.8 us
  starting transfers between devices  14.9 us (55%)
  Pallas kernels  5.98 us (22%)
  waiting for transfers between devices  5.84 us (22%)
    ppermute x6, starting transfers between devices, exchanged(): lax.ppermute(values[step], 'date', [(i, i ^ reach(step, dates)) for i in...  8.87 us
    ppermute x6, waiting for transfers between devices, exchanged(): lax.ppermute(values[step], 'date', [(i, i ^ reach(step, dates)) for i in...  5.83 us
    ppermute x1, starting transfers between devices, tiled_body(): lax.ppermute(early, 'date', [(i, i ^ reach(dates - 1, dates)) for i in ra...  2.89 us
    ppermute x1, starting transfers between devices, tiled_body(): side = lax.ppermute(side, 'rng', swap)  2.56 us
    pallas_call x1, Pallas kernels, tiled_body(): pl.pallas_call(functools.partial(looks_kernel, pairs, dates), out_shape=[...  1.58 us
    pallas_call x1, Pallas kernels, tiled_body(): pl.pallas_call(functools.partial(filter_kernel, pairs), out_shape=[jax.Sh...  1.23 us
    pallas_call x1, Pallas kernels, tiled_body(): pl.pallas_call(prepare_kernel, out_shape=[jax.ShapeDtypeStruct((2, lines,...  1.13 us
    pallas_call x1, Pallas kernels, tiled_body(): pl.pallas_call(resample_kernel, out_shape=[jax.ShapeDtypeStruct((rows, LA...  0.93 us
  transfers between devices with their start and end apart: 10, of which 4 were waited for; matrix products, arithmetic and copies ran while one was open for 0% of the time, Pallas kernels for 9%

profile of v9, /device:TPU:0, one launch (start us, length us, event | category | flops | bytes accessed | tf_op | source)
XLA Modules:
  0.0 26.8 jit_solution(10182101188217610490)
XLA Ops:
  0.0 1.1 %shard_map.46 = (bf16[2,32,128]{2,1,0:T(8,128)(2,1)S(1)}, bf16[2,16,2560]{2,1,0:T(8,128)(2,1)S(1)}, bf16[2,32,48]{2,1,0:T(8,128)(2,1)S(1)}, bf16[256,256]{1,0:T(8,128)(2,1)S(1)}, bf16[2,32,2944]{2,1,0:T(8,128)(2,1)S(1)}) custom-call(s32[1,2]{1,0:T(1,128)} %offsets_hbm.1, s32[1,2]{1,0:T(1,128)} %index_hbm.1, bf16[2,32,2560]{2,1,0:T(8,128)(2,1)} %bitcast.4), custom_call_target="tpu_custom_call" | custom-call | tf_op jit(solution)/shard_map/pallas_call | solution.py:556
  1.1 0.5 %collective-permute-start.3 = (bf16[2,16,2560]{2,1,0:T(8,128)(2,1)S(1)}, bf16[2,16,2560]{2,1,0:T(8,128)(2,1)S(1)}, u32[]{:S(2)}, u32[]{:S(2)}) collective-permute-start(bf16[2,16,2560]{2,1,0:T(8,128)(2,1)S(1)} %get-tuple-element.26), channel_id=1, source_target_pairs={{0,1},{1,0},{2,3},{3,2},{4,5},{5,4},{6,7},{7,6},{8,9},{9,8},{10,11... | collective-permute-start | bytes 491528 | tf_op jit(solution)/shard_map/ppermute | solution.py:577
  1.7 2.6 %collective-permute-start.2 = (bf16[2,32,128]{2,1,0:T(8,128)(2,1)S(1)}, bf16[2,32,128]{2,1,0:T(8,128)(2,1)S(1)}, u32[]{:S(2)}, u32[]{:S(2)}) collective-permute-start(bf16[2,32,128]{2,1,0:T(8,128)(2,1)S(1)} %get-tuple-element.25), channel_id=1, source_target_pairs={{0,2},{2,0},{1,3},{3,1},{4,6},{6,4},{5,7},{7,5},{8,10},{10,8},{9,1... | collective-permute-start | bytes 49160 | tf_op jit(solution)/shard_map/ppermute | solution.py:576
  4.2 0.1 collective-permute-start.1
  4.3 0.4 %shard_map.47 = bf16[128,128]{1,0:T(8,128)(2,1)S(1)} custom-call(bf16[2,32,2944]{2,1,0:T(8,128)(2,1)S(1)} %get-tuple-element.20.held_ref, bf16[2,32,48]{2,1,0:T(8,128)(2,1)S(1)} %get-tuple-element.21.line_ref, bf16[256,256]{1,0:T(8,128)(2,1)S(1)} %get-tuple-element.22.column_ref), custom_call_target="tpu_custom_call" | custom-call | flops 1000000000 | tf_op jit(solution)/shard_map/pallas_call | solution.py:580
  4.7 2.9 %collective-permute-start = (bf16[128,128]{1,0:T(8,128)(2,1)S(1)}, bf16[128,128]{1,0:T(8,128)(2,1)S(1)}, u32[]{:S(2)}, u32[]{:S(2)}) collective-permute-start(bf16[128,128]{1,0:T(8,128)(2,1)S(1)} %shard_map.47), channel_id=1, source_target_pairs={{0,8},{4,12},{8,0},{12,4},{1,9},{5,13},{9,1},{13,5},{2,10},{6,14},... | collective-permute-start | bytes 98312 | tf_op jit(solution)/shard_map/ppermute | solution.py:588
  7.6 0.0 collective-permute-done.2.side_ref
  7.6 0.0 collective-permute-done.1.corner_ref
  7.6 0.0 collective-permute-done.3.lines_ref
  7.6 0.9 %shard_map.49 = (bf16[336,128]{1,0:T(8,128)(2,1)S(1)}, bf16[336,128]{1,0:T(8,128)(2,1)S(1)}, bf16[336,128]{1,0:T(8,128)(2,1)S(1)}, bf16[208,128]{1,0:T(8,128)(2,1)S(1)}) custom-call(bf16[2,32,128]{2,1,0:T(8,128)(2,1)S(1)} %collective-permute-done.1.corner_ref, bf16[2,32,128]{2,1,0:T(8,128)(2,1)S(1)} %collective-permute-done.2.side_ref, ...), custom_call_target="tpu_custom_call" | custom-call | tf_op jit(solution)/shard_map/pallas_call | solution.py:590
  8.5 3.5 %collective-permute-start.5 = (bf16[336,128]{1,0:T(8,128)(2,1)S(1)}, bf16[336,128]{1,0:T(8,128)(2,1)S(1)}, u32[]{:S(2)}, u32[]{:S(2)}) collective-permute-start(bf16[336,128]{1,0:T(8,128)(2,1)S(1)} %get-tuple-element.28), channel_id=1, source_target_pairs={{0,12},{4,8},{8,4},{12,0},{1,13},{5,9},{9,5},{13,1},{2,14},{6,10},... | collective-permute-start | bytes 258056 | tf_op jit(solution)/shard_map/ppermute | solution.py:605
  12.0 0.0 collective-permute-start.6
  12.0 0.9 %collective-permute-start.4 = (bf16[208,128]{1,0:T(8,128)(2,1)S(1)}, bf16[208,128]{1,0:T(8,128)(2,1)S(1)}, u32[]{:S(2)}, u32[]{:S(2)}) collective-permute-start(bf16[208,128]{1,0:T(8,128)(2,1)S(1)} %get-tuple-element.27), channel_id=1, source_target_pairs={{0,8},{4,12},{8,0},{12,4},{1,9},{5,13},{9,1},{13,5},{2,10},{6,14},... | collective-permute-start | bytes 159752 | tf_op jit(solution)/shard_map/ppermute | solution.py:605
  12.9 0.0 collective-permute-done.early_ref
  12.9 1.2 %shard_map.48 = (bf16[6,256,512]{2,1,0:T(8,128)(2,1)S(1)}, bf16[320,128]{1,0:T(8,128)(2,1)S(1)}) custom-call(f32[4]{0:T(128)} %shift_hbm.1, bf16[128,128]{1,0:T(8,128)(2,1)S(1)} %collective-permute-done.early_ref), custom_call_target="tpu_custom_call" | custom-call | flops 600000000 | tf_op jit(solution)/shard_map/pallas_call | solution.py:612
  14.2 3.5 %collective-permute-done.4.refs_1_ = bf16[208,128]{1,0:T(8,128)(2,1)S(1)} collective-permute-done((bf16[208,128]{1,0:T(8,128)(2,1)S(1)}, bf16[208,128]{1,0:T(8,128)(2,1)S(1)}, u32[]{:S(2)}, u32[]{:S(2)}) %collective-permute-start.4) | collective-permute-done | bytes 53280 | tf_op jit(solution)/shard_map/ppermute | solution.py:605
  17.7 0.0 collective-permute-done.5.refs_2_
  17.7 0.4 %collective-permute-done.6.refs_3_ = bf16[336,128]{1,0:T(8,128)(2,1)S(1)} collective-permute-done((bf16[336,128]{1,0:T(8,128)(2,1)S(1)}, bf16[336,128]{1,0:T(8,128)(2,1)S(1)}, u32[]{:S(2)}, u32[]{:S(2)}) %collective-permute-start.6) | collective-permute-done | bytes 86048 | tf_op jit(solution)/shard_map/ppermute | solution.py:605
  18.1 1.6 %shard_map.50 = (f32[8,256]{1,0:T(8,128)S(1)}, f32[8,256]{1,0:T(8,128)S(1)}, f32[8,256]{1,0:T(8,128)S(1)}, f32[8,256]{1,0:T(8,128)S(1)}) custom-call(bf16[6,256,512]{2,1,0:T(8,128)(2,1)S(1)} %get-tuple-element.23.weight_ref, bf16[320,128]{1,0:T(8,128)(2,1)S(1)} %get-tuple-element.24.refs_0_, bf16[208,128]{1,0:T(8,128)(2,1)S(1)} %collective-permute-done.4.refs_1_, ...), custom_call_target="tpu_custom_call" | custom-call | tf_op jit(solution)/shard_map/pallas_call | solution.py:624
  19.7 1.8 %collective-permute-start.7 = (f32[8,256]{1,0:T(8,128)S(1)}, f32[8,256]{1,0:T(8,128)S(1)}, u32[]{:S(2)}, u32[]{:S(2)}) collective-permute-start(f32[8,256]{1,0:T(8,128)S(1)} %get-tuple-element.31), channel_id=1, source_target_pairs={{0,12},{4,8},{8,4},{12,0},{1,13},{5,9},{9,5},{13,1},{2,14},{6,10},... | collective-permute-start | bytes 24584 | tf_op jit(solution)/shard_map/ppermute | solution.py:605
  21.5 0.7 %collective-permute-start.8 = (f32[8,256]{1,0:T(8,128)S(1)}, f32[8,256]{1,0:T(8,128)S(1)}, u32[]{:S(2)}, u32[]{:S(2)}) collective-permute-start(f32[8,256]{1,0:T(8,128)S(1)} %get-tuple-element.32), channel_id=1, source_target_pairs={{0,8},{4,12},{8,0},{12,4},{1,9},{5,13},{9,1},{13,5},{2,10},{6,14},... | collective-permute-start | bytes 24584 | tf_op jit(solution)/shard_map/ppermute | solution.py:605
  22.2 1.9 %collective-permute-start.9 = (f32[8,256]{1,0:T(8,128)S(1)}, f32[8,256]{1,0:T(8,128)S(1)}, u32[]{:S(2)}, u32[]{:S(2)}) collective-permute-start(f32[8,256]{1,0:T(8,128)S(1)} %get-tuple-element.33), channel_id=1, source_target_pairs={{0,4},{4,0},{8,12},{12,8},{1,5},{5,1},{9,13},{13,9},{2,6},{6,2},{1... | collective-permute-start | bytes 24584 | tf_op jit(solution)/shard_map/ppermute | solution.py:605
  24.1 1.1 %collective-permute-done.7.refs_0_ = f32[8,256]{1,0:T(8,128)S(1)} collective-permute-done((f32[8,256]{1,0:T(8,128)S(1)}, f32[8,256]{1,0:T(8,128)S(1)}, u32[]{:S(2)}, u32[]{:S(2)}) %collective-permute-start.7) | collective-permute-done | bytes 8224 | tf_op jit(solution)/shard_map/ppermute | solution.py:605
  25.2 0.8 %collective-permute-done.8.refs_1_ = f32[8,256]{1,0:T(8,128)S(1)} collective-permute-done((f32[8,256]{1,0:T(8,128)S(1)}, f32[8,256]{1,0:T(8,128)S(1)}, u32[]{:S(2)}, u32[]{:S(2)}) %collective-permute-start.8) | collective-permute-done | bytes 8224 | tf_op jit(solution)/shard_map/ppermute | solution.py:605
  26.1 0.0 collective-permute-done.9.refs_2_
  26.1 0.7 %shard_map.51 = f32[2,8,8,128]{3,2,1,0:T(8,128)} custom-call(f32[8,256]{1,0:T(8,128)S(1)} %collective-permute-done.7.refs_0_, f32[8,256]{1,0:T(8,128)S(1)} %collective-permute-done.8.refs_1_, f32[8,256]{1,0:T(8,128)S(1)} %collective-permute-done.9.refs_2_, f32[8,256]{1,0:T(8,128)S(1)} %get-tuple-element.34.refs_3_), custom_call_target="tpu_custom_call" | custom-call | tf_op jit(solution)/shard_map/pallas_call | solution.py:638
Async XLA Ops:
  1.1 6.4 %collective-permute-start.3 = (bf16[2,16,2560]{2,1,0:T(8,128)(2,1)S(1)}, bf16[2,16,2560]{2,1,0:T(8,128)(2,1)S(1)}, u32[]{:S(2)}, u32[]{:S(2)}) collective-permute-start(bf16[2,16,2560]{2,1,0:T(8,128)(2,1)S(1)} %get-tuple-element.26), channel_id=1, source_target_pairs={{0,1},{1,0},{2,3},{3,2},{4,5},{5,4},{6,7},{7,6},{8,9},{9,8},{10,11... | collective-permute-start | bytes 491528 | tf_op jit(solution)/shard_map/ppermute | solution.py:577
  1.7 5.9 %collective-permute-start.2 = (bf16[2,32,128]{2,1,0:T(8,128)(2,1)S(1)}, bf16[2,32,128]{2,1,0:T(8,128)(2,1)S(1)}, u32[]{:S(2)}, u32[]{:S(2)}) collective-permute-start(bf16[2,32,128]{2,1,0:T(8,128)(2,1)S(1)} %get-tuple-element.25), channel_id=1, source_target_pairs={{0,2},{2,0},{1,3},{3,1},{4,6},{6,4},{5,7},{7,5},{8,10},{10,8},{9,1... | collective-permute-start | bytes 49160 | tf_op jit(solution)/shard_map/ppermute | solution.py:576
  4.2 3.4 %collective-permute-start.1 = (bf16[2,32,128]{2,1,0:T(8,128)(2,1)S(1)}, bf16[2,32,128]{2,1,0:T(8,128)(2,1)S(1)}, u32[]{:S(2)}, u32[]{:S(2)}) collective-permute-start(bf16[2,32,128]{2,1,0:T(8,128)(2,1)S(1)} %get-tuple-element.25), channel_id=1, source_target_pairs={{0,3},{1,2},{2,1},{3,0},{4,7},{5,6},{6,5},{7,4},{8,11},{9,10},{10,... | collective-permute-start | bytes 49160 | tf_op jit(solution)/shard_map/ppermute | solution.py:575
  4.7 8.3 %collective-permute-start = (bf16[128,128]{1,0:T(8,128)(2,1)S(1)}, bf16[128,128]{1,0:T(8,128)(2,1)S(1)}, u32[]{:S(2)}, u32[]{:S(2)}) collective-permute-start(bf16[128,128]{1,0:T(8,128)(2,1)S(1)} %shard_map.47), channel_id=1, source_target_pairs={{0,8},{4,12},{8,0},{12,4},{1,9},{5,13},{9,1},{13,5},{2,10},{6,14},... | collective-permute-start | bytes 98312 | tf_op jit(solution)/shard_map/ppermute | solution.py:588
  8.5 9.2 %collective-permute-start.5 = (bf16[336,128]{1,0:T(8,128)(2,1)S(1)}, bf16[336,128]{1,0:T(8,128)(2,1)S(1)}, u32[]{:S(2)}, u32[]{:S(2)}) collective-permute-start(bf16[336,128]{1,0:T(8,128)(2,1)S(1)} %get-tuple-element.28), channel_id=1, source_target_pairs={{0,12},{4,8},{8,4},{12,0},{1,13},{5,9},{9,5},{13,1},{2,14},{6,10},... | collective-permute-start | bytes 258056 | tf_op jit(solution)/shard_map/ppermute | solution.py:605
  12.0 6.1 %collective-permute-start.6 = (bf16[336,128]{1,0:T(8,128)(2,1)S(1)}, bf16[336,128]{1,0:T(8,128)(2,1)S(1)}, u32[]{:S(2)}, u32[]{:S(2)}) collective-permute-start(bf16[336,128]{1,0:T(8,128)(2,1)S(1)} %get-tuple-element.29), channel_id=1, source_target_pairs={{0,4},{4,0},{8,12},{12,8},{1,5},{5,1},{9,13},{13,9},{2,6},{6,2},{1... | collective-permute-start | bytes 258056 | tf_op jit(solution)/shard_map/ppermute | solution.py:605
  12.0 5.7 %collective-permute-start.4 = (bf16[208,128]{1,0:T(8,128)(2,1)S(1)}, bf16[208,128]{1,0:T(8,128)(2,1)S(1)}, u32[]{:S(2)}, u32[]{:S(2)}) collective-permute-start(bf16[208,128]{1,0:T(8,128)(2,1)S(1)} %get-tuple-element.27), channel_id=1, source_target_pairs={{0,8},{4,12},{8,0},{12,4},{1,9},{5,13},{9,1},{13,5},{2,10},{6,14},... | collective-permute-start | bytes 159752 | tf_op jit(solution)/shard_map/ppermute | solution.py:605
  19.7 5.5 %collective-permute-start.7 = (f32[8,256]{1,0:T(8,128)S(1)}, f32[8,256]{1,0:T(8,128)S(1)}, u32[]{:S(2)}, u32[]{:S(2)}) collective-permute-start(f32[8,256]{1,0:T(8,128)S(1)} %get-tuple-element.31), channel_id=1, source_target_pairs={{0,12},{4,8},{8,4},{12,0},{1,13},{5,9},{9,5},{13,1},{2,14},{6,10},... | collective-permute-start | bytes 24584 | tf_op jit(solution)/shard_map/ppermute | solution.py:605
  21.5 4.5 %collective-permute-start.8 = (f32[8,256]{1,0:T(8,128)S(1)}, f32[8,256]{1,0:T(8,128)S(1)}, u32[]{:S(2)}, u32[]{:S(2)}) collective-permute-start(f32[8,256]{1,0:T(8,128)S(1)} %get-tuple-element.32), channel_id=1, source_target_pairs={{0,8},{4,12},{8,0},{12,4},{1,9},{5,13},{9,1},{13,5},{2,10},{6,14},... | collective-permute-start | bytes 24584 | tf_op jit(solution)/shard_map/ppermute | solution.py:605
  22.2 3.8 %collective-permute-start.9 = (f32[8,256]{1,0:T(8,128)S(1)}, f32[8,256]{1,0:T(8,128)S(1)}, u32[]{:S(2)}, u32[]{:S(2)}) collective-permute-start(f32[8,256]{1,0:T(8,128)S(1)} %get-tuple-element.33), channel_id=1, source_target_pairs={{0,4},{4,0},{8,12},{12,8},{1,5},{5,1},{9,13},{13,9},{2,6},{6,2},{1... | collective-permute-start | bytes 24584 | tf_op jit(solution)/shard_map/ppermute | solution.py:605
